TPU v7x, 32 devices: a whole 2x2x4 slice. The times are simulated.
32 devices in a mesh: narrow: 2 (over core), wide: 16 (over z, y, x).
Axes of the slice: x: 2, y: 2, z: 4, core: 2. Of those that a mesh axis runs over, the one named last changes fastest.
Arguments:
- char_ids: int32 [32, 512, 50], P(('narrow', 'wide')), may hold values from 0 to 261
- word_lengths: int32 [32, 512], P(('narrow', 'wide')), may hold values from 1 to 50, as said below
- type_ids: int32 [32, 512], P(('narrow', 'wide')), may hold values from 0 to 1
- cotangent: bfloat16 [32, 512, 768], P(('narrow', 'wide')), may hold values from -6 to 6
- character_embedding_table: bfloat16 [262, 16], replicated, may hold values from -4 to 4
- conv_weight: bfloat16 [112, 2048], P(None, 'wide'), may hold values from -0.75 to 0.75
- conv_bias: bfloat16 [2048], P('wide'), may hold values from -1.75 to 1.75
- high_weight: bfloat16 [2, 2048, 4096], P(None, None, 'wide'), may hold values from -0.125 to 0.125
- high_bias: bfloat16 [2, 4096], P(None, 'wide'), may hold values from -1.75 to 1.75
- proj_weight: bfloat16 [2048, 768], P('wide'), may hold values from -0.25 to 0.25
- proj_bias: bfloat16 [768], P('wide'), may hold values from -1.75 to 1.75
- pos_table: bfloat16 [512, 768], P(None, 'wide'), may hold values from -3 to 3
- type_table: bfloat16 [2, 768], P(None, 'wide'), may hold values from -3 to 3
- embed_gain: bfloat16 [768], P('wide'), may hold values from 0.5 to 1.5
- embed_shift: bfloat16 [768], P('wide'), may hold values from -1.75 to 1.75
- qkv_weight: bfloat16 [768, 2304], P(None, 'wide'), may hold values from -0.21875 to 0.21875
- attn_bias: bfloat16 [1536], P('wide'), may hold values from -1.75 to 1.75
- out_weight: bfloat16 [768, 768], P('wide'), may hold values from -1.25 to 1.25
- out_bias: bfloat16 [768], P('wide'), may hold values from -1.75 to 1.75
- attn_gain: bfloat16 [768], P('wide'), may hold values from 0.5 to 1.5
- attn_shift: bfloat16 [768], P('wide'), may hold values from -1.75 to 1.75
- up_weight: bfloat16 [768, 3072], P(None, 'wide'), may hold values from -0.21875 to 0.21875
- up_bias: bfloat16 [3072], P('wide'), may hold values from -1.75 to 1.75
- down_weight: bfloat16 [3072, 768], P('wide'), may hold values from -0.109375 to 0.109375
- down_bias: bfloat16 [768], P('wide'), may hold values from -1.75 to 1.75
- ffn_gain: bfloat16 [768], P('wide'), may hold values from 0.5 to 1.5
- ffn_shift: bfloat16 [768], P('wide'), may hold values from -1.75 to 1.75
Outputs:
- hidden_out: bfloat16 [32, 512, 768], P(('narrow', 'wide'))
- grad_char_table: float32 [262, 16], replicated
- grad_conv_weight: float32 [112, 2048], P(None, ('narrow', 'wide'))
- grad_conv_bias: float32 [2048], P(('narrow', 'wide'))
- grad_high_weight: float32 [2, 2048, 4096], P(None, None, ('narrow', 'wide'))
- grad_high_bias: float32 [2, 4096], P(None, ('narrow', 'wide'))
- grad_proj_weight: float32 [2048, 768], P(('narrow', 'wide'))
- grad_proj_bias: float32 [768], P(('narrow', 'wide'))
- grad_pos_table: float32 [512, 768], P(None, ('narrow', 'wide'))
- grad_type_table: float32 [2, 768], P(None, ('narrow', 'wide'))
- grad_embed_gain: float32 [768], P(('narrow', 'wide'))
- grad_embed_shift: float32 [768], P(('narrow', 'wide'))
- grad_qkv_weight: float32 [768, 2304], P(None, ('narrow', 'wide'))
- grad_attn_bias: float32 [1536], P(('narrow', 'wide'))
- grad_out_weight: float32 [768, 768], P(('narrow', 'wide'))
- grad_out_bias: float32 [768], P(('narrow', 'wide'))
- grad_attn_gain: float32 [768], P(('narrow', 'wide'))
- grad_attn_shift: float32 [768], P(('narrow', 'wide'))
- grad_up_weight: float32 [768, 3072], P(None, ('narrow', 'wide'))
- grad_up_bias: float32 [3072], P(('narrow', 'wide'))
- grad_down_weight: float32 [3072, 768], P(('narrow', 'wide'))
- grad_down_bias: float32 [768], P(('narrow', 'wide'))
- grad_ffn_gain: float32 [768], P(('narrow', 'wide'))
- grad_ffn_shift: float32 [768], P(('narrow', 'wide'))
Inputs may be any that keep to these rules, and one draw needn't show every extreme that they name: `word_lengths`: every sequence holds at least one word of 50 characters.
All inputs are finite; a program needn't handle non-finite values.
Results may differ from a plain program's by a relative error of at most 0.017.
Values may be sent and summed in bfloat16 or wider, within the bound.
No kernel may reach another device: no remote copies, remote signals or barrier semaphores. Data moves between devices by JAX's collectives and lax.ppermute only.
A program may use at most 384 MiB of HBM per device.

v0:
```python
from functools import partial
import math

import jax
import jax.numpy as jnp
from jax import lax
from jax.sharding import PartitionSpec as P

HEADS = 12
HEAD_DIM = 64
CHAR_DIM = 16
TAPS = 7


EPSILON = 1e-12


def outer_sum(left_rows, right_rows):
    return lax.dot_general(
        left_rows, right_rows, (((0,), (0,)), ((), ())), preferred_element_type=jnp.float32
    )


def back_dot(grad_rows, weight):
    return lax.dot_general(
        grad_rows, weight, (((1,), (1,)), ((), ())), preferred_element_type=jnp.float32
    )


def column_sum(values):
    return jnp.sum(values.astype(jnp.float32), axis=0)


def norm_rows(value, norm_gain, norm_shift):
    center = jnp.mean(value, axis=-1, keepdims=True)
    offsets = value - center
    spread = jnp.mean(offsets * offsets, axis=-1, keepdims=True)
    return offsets * lax.rsqrt(spread + EPSILON) * norm_gain + norm_shift


def norm_back(value, norm_gain, norm_shift, grad_rows):
    _, pullback = jax.vjp(norm_rows, value, norm_gain, norm_shift)
    return pullback(grad_rows)


def filter_widths(filter_count):
    column = jnp.arange(filter_count)
    widths = jnp.ones((filter_count,), jnp.int32)
    for exponent in range(6):
        widths = widths + (column >= filter_count * 2**exponent // 64).astype(jnp.int32)
    return widths


def conv_matrix(weight):
    row_count, filter_count = weight.shape
    usable = jnp.arange(row_count)[:, None] // CHAR_DIM < filter_widths(filter_count)[None, :]
    masked = jnp.where(usable, weight, jnp.zeros_like(weight))
    return (
        jnp.concatenate([masked, jnp.zeros((CHAR_DIM, filter_count), weight.dtype)], axis=0),
        usable,
    )


def char_vectors(identifier_block, block_size_entry, table):
    char_count = identifier_block.shape[1]
    live_mask = (jnp.arange(char_count)[None, :] < block_size_entry[:, None]).astype(jnp.float32)
    one_hot = (identifier_block[:, :, None] == jnp.arange(table.shape[0])[None, None, :]).astype(
        jnp.bfloat16
    )
    vectors = jnp.einsum("wcv,ve->wce", one_hot, table, preferred_element_type=jnp.float32)
    return (vectors * live_mask[:, :, None], live_mask, one_hot)


def char_windows(vectors):
    char_count = vectors.shape[1]
    padded = jnp.pad(vectors, ((0, 0), (0, TAPS), (0, 0)))
    pieces = [padded[:, offset : offset + char_count, :] for offset in range(TAPS + 1)]
    return jnp.concatenate(pieces, axis=2).astype(jnp.bfloat16)


def pool_block(identifier_block, block_size_entry, table, matrix, conv_offset):
    vectors, live_mask, one_hot = char_vectors(identifier_block, block_size_entry, table)
    windows = char_windows(vectors)
    word_count, char_count, taps_width = windows.shape
    prior_value = (
        jnp.dot(
            windows.reshape(word_count * char_count, taps_width),
            matrix,
            preferred_element_type=jnp.float32,
        )
        + conv_offset
    )
    prior_value = prior_value.reshape(word_count, char_count, -1)
    pooled = jnp.sum(jax.nn.silu(prior_value) * live_mask[:, :, None], axis=1) / block_size_entry[
        :, None
    ].astype(jnp.float32)
    return (pooled, prior_value)


def convolution_pullback(
    identifier_block, block_size_entry, table, matrix, prior_value, pooling_gradient
):
    vectors, live_mask, one_hot = char_vectors(identifier_block, block_size_entry, table)
    windows = char_windows(vectors)
    word_count, char_count, taps_width = windows.shape
    grad_act = (pooling_gradient / block_size_entry[:, None].astype(jnp.float32))[
        :, None, :
    ] * live_mask[:, :, None]
    sigmoid_pre = jax.nn.sigmoid(prior_value)
    grad_before = (
        grad_act * (sigmoid_pre + prior_value * sigmoid_pre * (1.0 - sigmoid_pre))
    ).astype(jnp.bfloat16)
    flat_grad = grad_before.reshape(word_count * char_count, -1)
    flat_windows = windows.reshape(word_count * char_count, taps_width)
    grad_matrix = outer_sum(flat_windows, flat_grad)
    grad_bias = column_sum(flat_grad)
    grad_windows = back_dot(flat_grad, matrix).reshape(word_count, char_count, taps_width)
    grad_vectors = jnp.zeros((word_count, char_count + TAPS, CHAR_DIM), jnp.float32)
    for offset in range(TAPS + 1):
        section = grad_windows[:, :, offset * CHAR_DIM : (offset + 1) * CHAR_DIM]
        grad_vectors = grad_vectors + jnp.pad(section, ((0, 0), (offset, TAPS - offset), (0, 0)))
    grad_chars = grad_vectors[:, :char_count].astype(jnp.bfloat16) * live_mask[:, :, None].astype(
        jnp.bfloat16
    )
    grad_table = jnp.einsum("wcv,wce->ve", one_hot, grad_chars, preferred_element_type=jnp.float32)
    return (grad_matrix, grad_bias, grad_table)


def attend(qkv_seq):
    length = qkv_seq.shape[0]
    sections = qkv_seq.reshape(length, 3, HEADS, HEAD_DIM)
    scaling = HEAD_DIM ** (-0.5)
    scores = (
        jnp.einsum(
            "qhd,khd->hqk", sections[:, 0], sections[:, 1], preferred_element_type=jnp.float32
        )
        * scaling
    )
    highest = jnp.max(scores, axis=-1, keepdims=True)
    exponent = jnp.exp(scores - highest)
    summed_exp = jnp.sum(exponent, axis=-1, keepdims=True)
    attention = (exponent / summed_exp).astype(jnp.bfloat16)
    context = jnp.einsum(
        "hqk,khd->qhd", attention, sections[:, 2], preferred_element_type=jnp.float32
    )
    return (
        context.reshape(length, HEADS * HEAD_DIM).astype(jnp.bfloat16),
        (highest + jnp.log(summed_exp))[:, :, 0],
    )


def attend_back(qkv_seq, log_total, grad_context):
    length = qkv_seq.shape[0]
    sections = qkv_seq.reshape(length, 3, HEADS, HEAD_DIM)
    scaling = HEAD_DIM ** (-0.5)
    query, keys_part, values_part = (sections[:, 0], sections[:, 1], sections[:, 2])
    scores = (
        jnp.einsum("qhd,khd->hqk", query, keys_part, preferred_element_type=jnp.float32) * scaling
    )
    attention = jnp.exp(scores - log_total[:, :, None])
    grad_heads = grad_context.reshape(length, HEADS, HEAD_DIM)
    grad_attention = jnp.einsum(
        "qhd,khd->hqk", grad_heads, values_part, preferred_element_type=jnp.float32
    )
    grad_values = jnp.einsum(
        "hqk,qhd->khd",
        attention.astype(jnp.bfloat16),
        grad_heads,
        preferred_element_type=jnp.float32,
    )
    inner_sum = jnp.sum(grad_attention * attention, axis=-1, keepdims=True)
    grad_scores = (attention * (grad_attention - inner_sum)).astype(jnp.bfloat16)
    grad_query = (
        jnp.einsum("hqk,khd->qhd", grad_scores, keys_part, preferred_element_type=jnp.float32)
        * scaling
    )
    grad_keys = (
        jnp.einsum("hqk,qhd->khd", grad_scores, query, preferred_element_type=jnp.float32) * scaling
    )
    return jnp.stack([grad_query, grad_keys, grad_values], axis=1).reshape(
        length, 3 * HEADS * HEAD_DIM
    )


def body(
    char_ids,
    word_lengths,
    type_ids,
    cotangent,
    character_embedding_table,
    conv_weight,
    conv_bias,
    high_weight,
    high_bias,
    proj_weight,
    proj_bias,
    pos_table,
    type_table,
    embed_gain,
    embed_shift,
    qkv_weight,
    attn_bias,
    out_weight,
    out_bias,
    attn_gain,
    attn_shift,
    up_weight,
    up_bias,
    down_weight,
    down_bias,
    ffn_gain,
    ffn_shift,
):
    seq_count, seq_len, char_count = char_ids.shape
    word_count = seq_count * seq_len
    block_words = math.gcd(word_count, 128)
    block_count = word_count // block_words
    id_blocks = char_ids.reshape(block_count, block_words, char_count)
    size_blocks = word_lengths.reshape(block_count, block_words)
    embed_full = (
        lax.all_gather(conv_weight, "wide", axis=1, tiled=True),
        lax.all_gather(conv_bias, "wide", axis=0, tiled=True),
        lax.all_gather(high_weight, "wide", axis=2, tiled=True),
        lax.all_gather(high_bias, "wide", axis=1, tiled=True),
        lax.all_gather(proj_weight, "wide", axis=0, tiled=True),
        lax.all_gather(proj_bias, "wide", axis=0, tiled=True),
        lax.all_gather(pos_table, "wide", axis=1, tiled=True),
        lax.all_gather(type_table, "wide", axis=1, tiled=True),
        lax.all_gather(embed_gain, "wide", axis=0, tiled=True),
        lax.all_gather(embed_shift, "wide", axis=0, tiled=True),
    )
    encoder_full = (
        lax.all_gather(qkv_weight, "wide", axis=1, tiled=True),
        lax.all_gather(attn_bias, "wide", axis=0, tiled=True),
        lax.all_gather(out_weight, "wide", axis=0, tiled=True),
        lax.all_gather(out_bias, "wide", axis=0, tiled=True),
        lax.all_gather(attn_gain, "wide", axis=0, tiled=True),
        lax.all_gather(attn_shift, "wide", axis=0, tiled=True),
        lax.all_gather(up_weight, "wide", axis=1, tiled=True),
        lax.all_gather(up_bias, "wide", axis=0, tiled=True),
        lax.all_gather(down_weight, "wide", axis=0, tiled=True),
        lax.all_gather(down_bias, "wide", axis=0, tiled=True),
        lax.all_gather(ffn_gain, "wide", axis=0, tiled=True),
        lax.all_gather(ffn_shift, "wide", axis=0, tiled=True),
    )
    (
        conv_all,
        conv_bias_all,
        high_all,
        high_bias_all,
        proj_all,
        proj_bias_all,
        pos_all,
        type_all,
        gain_zero,
        shift_zero,
    ) = embed_full
    (
        qkv_all,
        attn_bias_all,
        out_all,
        out_bias_all,
        gain_one,
        shift_one,
        up_all,
        up_bias_all,
        down_all,
        down_bias_all,
        gain_two,
        shift_two,
    ) = encoder_full
    gain_zero = gain_zero.astype(jnp.float32)
    shift_zero = shift_zero.astype(jnp.float32)
    gain_one = gain_one.astype(jnp.float32)
    shift_one = shift_one.astype(jnp.float32)
    gain_two = gain_two.astype(jnp.float32)
    shift_two = shift_two.astype(jnp.float32)
    matrix, usable = conv_matrix(conv_all)
    conv_offset = conv_bias_all.astype(jnp.float32)

    def pool_only(inputs):
        return pool_block(inputs[0], inputs[1], character_embedding_table, matrix, conv_offset)[0]

    pooled = lax.map(pool_only, (id_blocks, size_blocks))
    pooled = pooled.reshape(word_count, -1)
    filter_count = pooled.shape[1]
    layer_count = high_all.shape[0]
    layer_inputs = []
    layer_transforms = []
    layer_gatings = []
    layer_activated = []
    highway = pooled
    for layer in range(layer_count):
        highway_in = jnp.dot(
            highway.astype(jnp.bfloat16), high_all[layer], preferred_element_type=jnp.float32
        ) + high_bias_all[layer].astype(jnp.float32)
        transform = highway_in[:, :filter_count]
        gating = jax.nn.sigmoid(highway_in[:, filter_count:])
        activated = jax.nn.silu(transform)
        layer_inputs.append(highway)
        layer_transforms.append(transform)
        layer_gatings.append(gating)
        layer_activated.append(activated)
        highway = gating * highway + (1.0 - gating) * activated
    word_vec = jnp.dot(
        highway.astype(jnp.bfloat16), proj_all, preferred_element_type=jnp.float32
    ) + proj_bias_all.astype(jnp.float32)
    type_hot = (type_ids.reshape(word_count) == 1).astype(jnp.float32)[:, None]
    type_rows = type_all.astype(jnp.float32)
    type_vec = type_hot * type_rows[1][None, :] + (1.0 - type_hot) * type_rows[0][None, :]
    summed = (word_vec.reshape(seq_count, seq_len, -1) + pos_all.astype(jnp.float32)[None]).reshape(
        word_count, -1
    ) + type_vec
    embedded = norm_rows(summed, gain_zero, shift_zero)
    model_width = embedded.shape[1]
    bias_three = jnp.concatenate(
        [
            attn_bias_all[:model_width],
            jnp.zeros((model_width,), attn_bias_all.dtype),
            attn_bias_all[model_width:],
        ]
    ).astype(jnp.float32)
    qkv_rows = (
        jnp.dot(embedded.astype(jnp.bfloat16), qkv_all, preferred_element_type=jnp.float32)
        + bias_three
    ).astype(jnp.bfloat16)
    qkv_seqs = qkv_rows.reshape(seq_count, seq_len, -1)
    context, log_total = lax.map(attend, qkv_seqs)
    context = context.reshape(word_count, -1)
    first_in = embedded + (
        jnp.dot(context, out_all, preferred_element_type=jnp.float32)
        + out_bias_all.astype(jnp.float32)
    )
    first = norm_rows(first_in, gain_one, shift_one)
    inner = jnp.dot(
        first.astype(jnp.bfloat16), up_all, preferred_element_type=jnp.float32
    ) + up_bias_all.astype(jnp.float32)
    activation = jax.nn.gelu(inner, approximate=False).astype(jnp.bfloat16)
    second_in = first + (
        jnp.dot(activation, down_all, preferred_element_type=jnp.float32)
        + down_bias_all.astype(jnp.float32)
    )
    hidden_out = norm_rows(second_in, gain_two, shift_two)
    qkv_again, out_again, up_again, down_again = (
        lax.all_gather(qkv_weight, "wide", axis=1, tiled=True),
        lax.all_gather(out_weight, "wide", axis=0, tiled=True),
        lax.all_gather(up_weight, "wide", axis=1, tiled=True),
        lax.all_gather(down_weight, "wide", axis=0, tiled=True),
    )
    conv_again, high_again, proj_again = (
        lax.all_gather(conv_weight, "wide", axis=1, tiled=True),
        lax.all_gather(high_weight, "wide", axis=2, tiled=True),
        lax.all_gather(proj_weight, "wide", axis=0, tiled=True),
    )
    grad_second, grad_ffn_gain, grad_ffn_shift = norm_back(
        second_in, gain_two, shift_two, cotangent.reshape(word_count, -1).astype(jnp.float32)
    )
    grad_ffn = grad_second.astype(jnp.bfloat16)
    grad_down_weight = outer_sum(activation, grad_ffn)
    grad_down_bias = column_sum(grad_ffn)
    grad_act = back_dot(grad_ffn, down_again)
    _, gelu_pull = jax.vjp(partial(jax.nn.gelu, approximate=False), inner)
    grad_inner = gelu_pull(grad_act)[0].astype(jnp.bfloat16)
    grad_up_weight = outer_sum(first.astype(jnp.bfloat16), grad_inner)
    grad_up_bias = column_sum(grad_inner)
    grad_first = grad_second + back_dot(grad_inner, up_again)
    grad_resid, grad_attn_gain, grad_attn_shift = norm_back(
        first_in, gain_one, shift_one, grad_first
    )
    grad_branch = grad_resid.astype(jnp.bfloat16)
    grad_out_weight = outer_sum(context, grad_branch)
    grad_out_bias = column_sum(grad_branch)
    grad_context = back_dot(grad_branch, out_again).astype(jnp.bfloat16)

    def attend_step(inputs):
        return attend_back(inputs[0], inputs[1], inputs[2])

    grad_qkv = lax.map(
        attend_step, (qkv_seqs, log_total, grad_context.reshape(seq_count, seq_len, -1))
    )
    grad_qkv = grad_qkv.reshape(word_count, -1).astype(jnp.bfloat16)
    grad_qkv_weight = outer_sum(embedded.astype(jnp.bfloat16), grad_qkv)
    qkv_sums = column_sum(grad_qkv)
    grad_attn_bias = jnp.concatenate([qkv_sums[:model_width], qkv_sums[2 * model_width :]])
    grad_embedded = grad_resid + back_dot(grad_qkv, qkv_again)
    encoder_sums = (
        lax.psum_scatter(grad_qkv_weight, ("narrow", "wide"), scatter_dimension=1, tiled=True),
        lax.psum_scatter(grad_attn_bias, ("narrow", "wide"), scatter_dimension=0, tiled=True),
        lax.psum_scatter(grad_out_weight, ("narrow", "wide"), scatter_dimension=0, tiled=True),
        lax.psum_scatter(grad_out_bias, ("narrow", "wide"), scatter_dimension=0, tiled=True),
        lax.psum_scatter(grad_attn_gain, ("narrow", "wide"), scatter_dimension=0, tiled=True),
        lax.psum_scatter(grad_attn_shift, ("narrow", "wide"), scatter_dimension=0, tiled=True),
        lax.psum_scatter(grad_up_weight, ("narrow", "wide"), scatter_dimension=1, tiled=True),
        lax.psum_scatter(grad_up_bias, ("narrow", "wide"), scatter_dimension=0, tiled=True),
        lax.psum_scatter(grad_down_weight, ("narrow", "wide"), scatter_dimension=0, tiled=True),
        lax.psum_scatter(grad_down_bias, ("narrow", "wide"), scatter_dimension=0, tiled=True),
        lax.psum_scatter(grad_ffn_gain, ("narrow", "wide"), scatter_dimension=0, tiled=True),
        lax.psum_scatter(grad_ffn_shift, ("narrow", "wide"), scatter_dimension=0, tiled=True),
    )
    grad_summed, grad_embed_gain, grad_embed_shift = norm_back(
        summed, gain_zero, shift_zero, grad_embedded
    )
    grad_pos_table = jnp.sum(grad_summed.reshape(seq_count, seq_len, -1), axis=0)
    grad_type_table = jnp.stack(
        [jnp.sum((1.0 - type_hot) * grad_summed, axis=0), jnp.sum(type_hot * grad_summed, axis=0)]
    )
    grad_word = grad_summed.astype(jnp.bfloat16)
    grad_proj_weight = outer_sum(highway.astype(jnp.bfloat16), grad_word)
    grad_proj_bias = column_sum(grad_word)
    grad_running = back_dot(grad_word, proj_again)
    weight_grads = [None] * layer_count
    bias_grads = [None] * layer_count
    for layer in reversed(range(layer_count)):
        transform = layer_transforms[layer]
        gating = layer_gatings[layer]
        layer_input = layer_inputs[layer]
        sigmoid_transform = jax.nn.sigmoid(transform)
        grad_transform = (
            grad_running
            * (1.0 - gating)
            * (sigmoid_transform + transform * sigmoid_transform * (1.0 - sigmoid_transform))
        )
        grad_gating = (
            grad_running * (layer_input - layer_activated[layer]) * gating * (1.0 - gating)
        )
        grad_mixed = jnp.concatenate([grad_transform, grad_gating], axis=1).astype(jnp.bfloat16)
        weight_grads[layer] = outer_sum(layer_input.astype(jnp.bfloat16), grad_mixed)
        bias_grads[layer] = column_sum(grad_mixed)
        grad_running = grad_running * gating + back_dot(grad_mixed, high_again[layer])
    grad_high_weight = jnp.stack(weight_grads)
    grad_high_bias = jnp.stack(bias_grads)
    matrix_pullback = conv_matrix(conv_again)[0]
    grad_pool_blocks = grad_running.reshape(block_count, block_words, -1)
    starting = (
        jnp.zeros(matrix_pullback.shape, jnp.float32),
        jnp.zeros((filter_count,), jnp.float32),
        jnp.zeros(character_embedding_table.shape, jnp.float32),
    )

    def back_step(running_total, inputs):
        identifier_block, block_size_entry, pooling_gradient = inputs
        prior_value = pool_block(
            identifier_block,
            block_size_entry,
            character_embedding_table,
            matrix_pullback,
            conv_offset,
        )[1]
        summand_terms = convolution_pullback(
            identifier_block,
            block_size_entry,
            character_embedding_table,
            matrix_pullback,
            prior_value,
            pooling_gradient,
        )
        return (
            tuple(
                (
                    incomplete_sum + summand_term
                    for incomplete_sum, summand_term in zip(running_total, summand_terms)
                )
            ),
            None,
        )

    (grad_matrix, grad_conv_bias, grad_table), _ = lax.scan(
        back_step, starting, (id_blocks, size_blocks, grad_pool_blocks)
    )
    grad_conv_weight = jnp.where(usable, grad_matrix[: usable.shape[0]], 0.0)
    embed_sums = (
        lax.psum_scatter(grad_conv_weight, ("narrow", "wide"), scatter_dimension=1, tiled=True),
        lax.psum_scatter(grad_conv_bias, ("narrow", "wide"), scatter_dimension=0, tiled=True),
        lax.psum_scatter(grad_high_weight, ("narrow", "wide"), scatter_dimension=2, tiled=True),
        lax.psum_scatter(grad_high_bias, ("narrow", "wide"), scatter_dimension=1, tiled=True),
        lax.psum_scatter(grad_proj_weight, ("narrow", "wide"), scatter_dimension=0, tiled=True),
        lax.psum_scatter(grad_proj_bias, ("narrow", "wide"), scatter_dimension=0, tiled=True),
        lax.psum_scatter(grad_pos_table, ("narrow", "wide"), scatter_dimension=1, tiled=True),
        lax.psum_scatter(grad_type_table, ("narrow", "wide"), scatter_dimension=1, tiled=True),
        lax.psum_scatter(grad_embed_gain, ("narrow", "wide"), scatter_dimension=0, tiled=True),
        lax.psum_scatter(grad_embed_shift, ("narrow", "wide"), scatter_dimension=0, tiled=True),
    )
    table_total = lax.psum(grad_table, ("narrow", "wide"))
    return (
        (hidden_out.reshape(seq_count, seq_len, -1).astype(jnp.bfloat16), table_total)
        + tuple(embed_sums)
        + tuple(encoder_sums)
    )


def solution(mesh):
    placed = (
        P(("narrow", "wide"), None, None),
        P(("narrow", "wide"), None),
        P(("narrow", "wide"), None),
        P(("narrow", "wide"), None, None),
        P(),
        P(None, "wide"),
        P("wide"),
        P(None, None, "wide"),
        P(None, "wide"),
        P("wide", None),
        P("wide"),
        P(None, "wide"),
        P(None, "wide"),
        P("wide"),
        P("wide"),
        P(None, "wide"),
        P("wide"),
        P("wide", None),
        P("wide"),
        P("wide"),
        P("wide"),
        P(None, "wide"),
        P("wide"),
        P("wide", None),
        P("wide"),
        P("wide"),
        P("wide"),
    )
    return jax.shard_map(
        body,
        mesh=mesh,
        in_specs=placed,
        out_specs=(
            P(("narrow", "wide"), None, None),
            P(),
            P(None, ("narrow", "wide")),
            P(("narrow", "wide")),
            P(None, None, ("narrow", "wide")),
            P(None, ("narrow", "wide")),
            P(("narrow", "wide"), None),
            P(("narrow", "wide")),
            P(None, ("narrow", "wide")),
            P(None, ("narrow", "wide")),
            P(("narrow", "wide")),
            P(("narrow", "wide")),
            P(None, ("narrow", "wide")),
            P(("narrow", "wide")),
            P(("narrow", "wide"), None),
            P(("narrow", "wide")),
            P(("narrow", "wide")),
            P(("narrow", "wide")),
            P(None, ("narrow", "wide")),
            P(("narrow", "wide")),
            P(("narrow", "wide"), None),
            P(("narrow", "wide")),
            P(("narrow", "wide")),
            P(("narrow", "wide")),
        ),
        check_vma=False,
    )
```

profile of v0, /device:TPU:0, one launch (start us, length us, event | category | flops | bytes accessed | tf_op | source)
XLA Modules:
  0.0 5253.2 jit_solution(14756759983866011657)
XLA Ops:
  26.9 125.1 %all-reduce.36 = (bf16[1536]{0:T(1024)(128)(2,1)S(1)}, bf16[768]{0:T(1024)(128)(2,1)S(1)}, bf16[768]{0:T(1024)(128)(2,1)S(1)}, bf16[768]{0:T(1024)(128)(2,1)S(1)...) all-reduce(bf16[1536]{0:T(1024)(128)(2,1)S(1)} %dynamic-update-slic, ...), channel_id=1, replica_groups=mesh['narrow'=2,'wide'=16] {'wide'}, use_global_device_ids=true, to_apply=%add.14 | all-reduce | flops 11520 | bytes 46080
  157.9 66.8 %all-gather = bf16[16,1,128]{2,1,0:T(2,128)(2,1)S(1)} all-gather(bf16[1,1,128]{2,1,0:T(2,128)(2,1)} %bitcast.277), channel_id=1, replica_groups=mesh['narrow'=2,'wide'=16] {'wide'}, dimensions={0}, use_global_device_ids=true | all-gather | bytes 4352 | tf_op jit(solution)/shard_map/all_gather | solution.py:222
  224.8 62.4 %all-gather.1 = bf16[16,48,2]{1,2,0:T(2,128)(2,1)S(1)} all-gather(bf16[1,48,2]{1,2,0:T(2,128)(2,1)S(1)} %bitcast.278), channel_id=1, replica_groups=mesh['narrow'=2,'wide'=16] {'wide'}, dimensions={0}, use_global_device_ids=true | all-gather | bytes 3264 | tf_op jit(solution)/shard_map/all_gather | solution.py:228
  288.5 71.8 %all_gather.76 = bf16[2,4096]{1,0:T(2,128)(2,1)S(1)} all-gather(bf16[2,256]{1,0:T(2,128)(2,1)S(1)} %copy-done.94), channel_id=1, replica_groups=mesh['narrow'=2,'wide'=16] {'wide'}, dimensions={1}, use_global_device_ids=true | all-gather | bytes 17408 | tf_op jit(solution)/shard_map/all_gather | solution.py:224
  361.1 72.6 %all_gather.73 = bf16[112,2048]{0,1:T(8,128)(2,1)S(1)} all-gather(bf16[112,128]{0,1:T(8,128)(2,1)S(1)} %copy.164), channel_id=1, replica_groups=mesh['narrow'=2,'wide'=16] {'wide'}, dimensions={1}, use_global_device_ids=true | all-gather | bytes 487424 | tf_op jit(solution)/shard_map/all_gather | solution.py:221
  434.3 91.5 %all_gather.79 = bf16[512,768]{0,1:T(8,128)(2,1)S(1)} all-gather(bf16[512,48]{0,1:T(8,128)(2,1)S(1)} %copy-done.53), channel_id=1, replica_groups=mesh['narrow'=2,'wide'=16] {'wide'}, dimensions={1}, use_global_device_ids=true | all-gather | bytes 835584 | tf_op jit(solution)/shard_map/all_gather | solution.py:227
  527.8 461.5 %while.38 = (s32[]{:T(128)}, f32[4,128,2048]{2,1,0:T(8,128)}, s32[4,128,50]{1,2,0:T(8,128)S(1)}, bf16[262,16]{0,1:T(8,128)(2,1)S(1)}, s32[4,128]{1,0:T(4,128)}, ...) while((s32[]{:T(128)}, f32[4,128,2048]{2,1,0:T(8,128)}, s32[4,128,50]{1,2,0:T(8,128)S(1)}, ...), condition=%wide.region_2.3_spmd, body=%wide.region_0.2_spmd.sunk | while | flops 3502745600 | bytes 229407600 | solution.py:284
  560.2 47.5 reshape.751
  675.2 47.4 reshape.751
  905.7 47.4 reshape.751
  1218.8 1473.0 %while.39 = (s32[]{:T(128)}, f32[128,2048]{1,0:T(8,128)}, f32[2048]{0:T(1024)}, f32[262,16]{0,1:T(8,128)}, s32[4,128,50]{1,2,0:T(8,128)}, /*index=5*/bf16[262,16...) while((s32[]{:T(128)}, f32[128,2048]{1,0:T(8,128)}, ...), condition=%wide.region_20.21_spmd.clone, body=%wide.region_18.20_spmd.clone.sunk | while | flops 10480435200 | bytes 648956928 | solution.py:467
  1259.8 47.7 mul.874
  1307.5 48.8 convert_reduce_fusion.10
  1511.7 70.5 %fusion.207 = f32[128,50,128]{0,2,1:T(8,128)S(1)} fusion(bf16[128,50,2048]{2,1,0:T(8,128)(2,1)} %dot_general.165, bf16[128,2048]{1,0:T(8,128)(2,1)} %get-tuple-element.865), kind=kOutput, calls=%fused_computation.27.clone.1 | convolution fusion | flops 3355443200 | bytes 30015488 | tf_op jit(solution)/shard_map/while/body/eval_jaxpr/dot_general | solution.py:25
  1625.7 47.7 mul.874
  1673.5 48.8 convert_reduce_fusion.10
  1877.8 70.5 %fusion.207 = f32[128,50,128]{0,2,1:T(8,128)S(1)} fusion(bf16[128,50,2048]{2,1,0:T(8,128)(2,1)} %dot_general.165, bf16[128,2048]{1,0:T(8,128)(2,1)} %get-tuple-element.865), kind=kOutput, calls=%fused_computation.27.clone.1 | convolution fusion | flops 3355443200 | bytes 30015488 | tf_op jit(solution)/shard_map/while/body/eval_jaxpr/dot_general | solution.py:25
  1991.8 47.7 mul.874
  2039.5 48.8 convert_reduce_fusion.10
  2243.9 70.5 %fusion.207 = f32[128,50,128]{0,2,1:T(8,128)S(1)} fusion(bf16[128,50,2048]{2,1,0:T(8,128)(2,1)} %dot_general.165, bf16[128,2048]{1,0:T(8,128)(2,1)} %get-tuple-element.865), kind=kOutput, calls=%fused_computation.27.clone.1 | convolution fusion | flops 3355443200 | bytes 30015488 | tf_op jit(solution)/shard_map/while/body/eval_jaxpr/dot_general | solution.py:25
  2357.9 47.7 mul.874
  2405.6 48.8 convert_reduce_fusion.10
  2609.9 70.5 %fusion.207 = f32[128,50,128]{0,2,1:T(8,128)S(1)} fusion(bf16[128,50,2048]{2,1,0:T(8,128)(2,1)} %dot_general.165, bf16[128,2048]{1,0:T(8,128)(2,1)} %get-tuple-element.865), kind=kOutput, calls=%fused_computation.27.clone.1 | convolution fusion | flops 3355443200 | bytes 30015488 | tf_op jit(solution)/shard_map/while/body/eval_jaxpr/dot_general | solution.py:25
  2841.1 129.2 %reduce-scatter.29.cloned.1.call-done = f32[128,2]{1,0:T(8,128)} async-done(((f32[4096,2]{1,0:T(8,128)}), f32[128,2]{1,0:T(8,128)}) %reduce-scatter.29.cloned.1.call-update) | async-done | bytes 1040
  2971.8 137.3 %reduce-scatter.15.cloned.1.call-done = f32[112,64]{0,1:T(8,128)} async-done(((f32[112,2048]{0,1:T(8,128)}), f32[112,64]{0,1:T(8,128)}) %reduce-scatter.15.cloned.1.call-update) | async-done | bytes 28688 | tf_op jit(solution)/shard_map/reduce_scatter | solution.py:472
  3109.2 99.3 %reduce-scatter.31.cloned.1.call-done = f32[24,512]{1,0:T(8,128)} async-done(((f32[768,512]{1,0:T(8,128)}), f32[24,512]{1,0:T(8,128)}) %reduce-scatter.31.cloned.1.call-update) | async-done | bytes 49168
  3208.5 103.9 %reduce-scatter.23.cloned.1.call-done = f32[24,768]{1,0:T(8,128)} async-done(((f32[768,768]{1,0:T(8,128)}), f32[24,768]{1,0:T(8,128)}) %reduce-scatter.23.cloned.1.call-update) | async-done | bytes 73744 | tf_op jit(solution)/shard_map/reduce_scatter | solution.py:389
  3312.4 120.4 %reduce-scatter.19.cloned.1.call-done = f32[64,768]{1,0:T(8,128)} async-done(((f32[2048,768]{1,0:T(8,128)}), f32[64,768]{1,0:T(8,128)}) %reduce-scatter.19.cloned.1.call-update) | async-done | bytes 196624 | tf_op jit(solution)/shard_map/reduce_scatter | solution.py:476
  3432.8 124.6 %reduce-scatter.21.cloned.1.call-done = f32[768,72]{0,1:T(8,128)} async-done(((f32[768,2304]{0,1:T(8,128)}), f32[768,72]{0,1:T(8,128)}) %reduce-scatter.21.cloned.1.call-update) | async-done | bytes 221200 | tf_op jit(solution)/shard_map/reduce_scatter | solution.py:387
  3557.5 142.2 %reduce-scatter.25.cloned.1.call-done = f32[768,96]{0,1:T(8,128)} async-done(((f32[768,3072]{0,1:T(8,128)}), f32[768,96]{0,1:T(8,128)}) %reduce-scatter.25.cloned.1.call-update) | async-done | bytes 294928 | tf_op jit(solution)/shard_map/reduce_scatter | solution.py:393
  3699.7 140.9 %reduce-scatter.27.cloned.1.call-done = f32[96,768]{1,0:T(8,128)} async-done(((f32[3072,768]{1,0:T(8,128)}), f32[96,768]{1,0:T(8,128)}) %reduce-scatter.27.cloned.1.call-update) | async-done | bytes 294928 | tf_op jit(solution)/shard_map/reduce_scatter | solution.py:395
  3840.6 1404.6 %reduce-scatter.17.cloned.1.call-done = f32[2,2048,128]{2,1,0:T(8,128)} async-done(((f32[2,2048,4096]{2,1,0:T(8,128)}), f32[2,2048,128]{2,1,0:T(8,128)}) %reduce-scatter.17.cloned.1.call-update) | async-done | bytes 2097168 | tf_op jit(solution)/shard_map/reduce_scatter | solution.py:474
  (841 shorter events, 1520.4 us)
Async XLA Ops:
  7.2 217.6 %copy-start.95 = (bf16[2,48]{1,0:T(2,128)(2,1)S(1)}, bf16[2,48]{1,0:T(2,128)(2,1)}, u32[]{:S(2)}) copy-start(bf16[2,48]{1,0:T(2,128)(2,1)} %param.43) | copy-start | bytes 580
  7.2 281.3 %copy-start.94 = (bf16[2,256]{1,0:T(2,128)(2,1)S(1)}, bf16[2,256]{1,0:T(2,128)(2,1)}, u32[]{:S(2)}) copy-start(bf16[2,256]{1,0:T(2,128)(2,1)} %param.39) | copy-start | bytes 3076
  7.2 353.7 %copy-start.55 = (bf16[112,128]{1,0:T(8,128)(2,1)S(1)}, bf16[112,128]{1,0:T(8,128)(2,1)}, u32[]{:S(2)}) copy-start(bf16[112,128]{1,0:T(8,128)(2,1)} %param.36) | copy-start | bytes 86020
  7.2 353.8 %copy-start.48 = (s32[1,512,50]{1,0,2:T(1,128)S(1)}, s32[1,512,50]{1,0,2:T(1,128)}, u32[]{:S(2)}) copy-start(s32[1,512,50]{1,0,2:T(1,128)} %param.31) | copy-start | bytes 307204
  7.2 427.0 %copy-start.53 = (bf16[512,48]{0,1:T(8,128)(2,1)S(1)}, bf16[512,48]{0,1:T(8,128)(2,1)}, u32[]{:S(2)}) copy-start(bf16[512,48]{0,1:T(8,128)(2,1)} %param.42) | copy-start | bytes 147460
  7.2 988.2 %all-gather.9.cloned.1.call-start = ((), (), s32[]{:S(2)}) async-start(), calls=%async_computation.9 | async-start | bytes 35651584 | tf_op jit(solution)/shard_map/all_gather | solution.py:223
  8.0 1021.7 %all-gather.11.cloned.1.call-start = ((), (), s32[]{:S(2)}) async-start(), calls=%async_computation.10 | async-start | bytes 3342336 | tf_op jit(solution)/shard_map/all_gather | solution.py:225
  8.7 519.0 %copy-start.101 = (bf16[262,16]{0,1:T(8,128)(2,1)S(1)}, bf16[262,16]{0,1:T(8,128)(2,1)}, u32[]{:S(2)}) copy-start(bf16[262,16]{0,1:T(8,128)(2,1)} %param.35) | copy-start | bytes 25156
  8.7 1027.0 %all-gather.13.cloned.1.call-start = ((), (), s32[]{:S(2)}) async-start(), calls=%async_computation.11 | async-start | bytes 3760128 | tf_op jit(solution)/shard_map/all_gather | solution.py:233
  9.5 1044.7 %all-gather.15.cloned.1.call-start = ((), (), s32[]{:S(2)}) async-start(), calls=%async_computation.12 | async-start | bytes 1253376 | tf_op jit(solution)/shard_map/all_gather | solution.py:235
  10.1 1048.8 %all-gather.17.cloned.1.call-start = ((), (), s32[]{:S(2)}) async-start(), calls=%async_computation.13 | async-start | bytes 5013504 | tf_op jit(solution)/shard_map/all_gather | solution.py:239
  10.6 1083.3 %all-gather.19.cloned.1.call-start = ((), (), s32[]{:S(2)}) async-start(), calls=%async_computation.14 | async-start | bytes 5013504 | tf_op jit(solution)/shard_map/all_gather | solution.py:241
  11.2 2813.4 %all-reduce.39.cloned.1.call-start = ((), (), s32[]{:S(2)}) async-start(), calls=%async_computation.24 | async-start | bytes 192512 | tf_op jit(solution)/shard_map/psum | solution.py:483
  11.3 422.8 %copy-start.92 = (s32[112]{0:T(128)}, s32[112]{0:T(128)S(1)}, u32[]{:S(2)}) copy-start(s32[112]{0:T(128)S(1)} %and_select_fusion) | copy-start | bytes 1348
  11.3 422.8 %copy-start.49 = (s32[2048]{0:T(1024)}, s32[2048]{0:T(1024)S(1)}, u32[]{:S(2)}) copy-start(s32[2048]{0:T(1024)S(1)} %convert_add_fusion) | copy-start | bytes 24580
  1034.3 126.3 %copy-start.58 = (f32[512]{0:T(512)}, f32[512]{0:T(512)S(1)}, u32[]{:S(2)}) copy-start(f32[512]{0:T(512)S(1)} %broadcast_multiply_fusion.2) | copy-start | bytes 6148
  1035.7 124.8 %copy-start.76 = (f32[512]{0:T(512)}, f32[512]{0:T(512)S(1)}, u32[]{:S(2)}) copy-start(f32[512]{0:T(512)S(1)} %fusion.89) | copy-start | bytes 6148
  1218.7 1473.1 %copy-start.65 = (f32[768]{0:T(1024)S(1)}, f32[768]{0:T(1024)}, u32[]{:S(2)}) copy-start(f32[768]{0:T(1024)} %slice.244) | copy-start | bytes 9220
  1218.7 1473.1 %copy-start.66 = (f32[768]{0:T(1024)S(1)}, f32[768]{0:T(1024)}, u32[]{:S(2)}) copy-start(f32[768]{0:T(1024)} %slice.246) | copy-start | bytes 9220
  1218.7 1473.7 %copy-start.74 = (f32[1,768]{1,0:T(1,128)S(1)}, f32[1,768]{1,0:T(1,128)}, u32[]{:S(2)}) copy-start(f32[1,768]{1,0:T(1,128)} %stack.53) | copy-start | bytes 9220
  1218.7 1473.7 %copy-start.75 = (f32[1,768]{1,0:T(1,128)S(1)}, f32[1,768]{1,0:T(1,128)}, u32[]{:S(2)}) copy-start(f32[1,768]{1,0:T(1,128)} %stack.54) | copy-start | bytes 9220
  1218.7 1474.4 %copy-start.51 = (f32[4096]{0:T(1024)S(1)}, f32[4096]{0:T(1024)}, u32[]{:S(2)}) copy-start(f32[4096]{0:T(1024)} %convert_reduce_fusion.1) | copy-start | bytes 49156
  1218.8 1474.4 %copy-start.52 = (f32[4096]{0:T(1024)S(1)}, f32[4096]{0:T(1024)}, u32[]{:S(2)}) copy-start(f32[4096]{0:T(1024)} %convert_reduce_fusion.2) | copy-start | bytes 49156
  2693.1 277.2 %reduce-scatter.29.cloned.1.call-start = ((), (), s32[]{:S(2)}) async-start(), calls=%async_computation.22 | async-start | bytes 2162688
  2696.8 412.3 %reduce-scatter.15.cloned.1.call-start = ((), (), s32[]{:S(2)}) async-start(), calls=%async_computation.15 | async-start | bytes 1081344 | tf_op jit(solution)/shard_map/reduce_scatter | solution.py:472
  2698.3 510.2 %reduce-scatter.31.cloned.1.call-start = ((), (), s32[]{:S(2)}) async-start(), calls=%async_computation.23 | async-start | bytes 1622016
  2700.0 612.5 %reduce-scatter.23.cloned.1.call-start = ((), (), s32[]{:S(2)}) async-start(), calls=%async_computation.19 | async-start | bytes 2433024 | tf_op jit(solution)/shard_map/reduce_scatter | solution.py:389
  2702.2 730.6 %reduce-scatter.19.cloned.1.call-start = ((), (), s32[]{:S(2)}) async-start(), calls=%async_computation.17 | async-start | bytes 6488064 | tf_op jit(solution)/shard_map/reduce_scatter | solution.py:476
  2708.4 849.1 %reduce-scatter.21.cloned.1.call-start = ((), (), s32[]{:S(2)}) async-start(), calls=%async_computation.18 | async-start | bytes 7299072 | tf_op jit(solution)/shard_map/reduce_scatter | solution.py:387
  2716.6 983.1 %reduce-scatter.25.cloned.1.call-start = ((), (), s32[]{:S(2)}) async-start(), calls=%async_computation.20 | async-start | bytes 9732096 | tf_op jit(solution)/shard_map/reduce_scatter | solution.py:393
  2726.4 1114.2 %reduce-scatter.27.cloned.1.call-start = ((), (), s32[]{:S(2)}) async-start(), calls=%async_computation.21 | async-start | bytes 9732096 | tf_op jit(solution)/shard_map/reduce_scatter | solution.py:395
  2735.6 2509.5 %reduce-scatter.17.cloned.1.call-start = ((), (), s32[]{:S(2)}) async-start(), calls=%async_computation.16 | async-start | bytes 69206016 | tf_op jit(solution)/shard_map/reduce_scatter | solution.py:474
  (147 other events, 2015.8 us)
Sparse Core Ops, SparseCore 0:
  9.5 717.7 all-gather.8
  730.1 70.1 all-gather.10
  803.0 69.7 all-gather.12
  875.4 54.6 all-gather.14
  932.8 79.3 all-gather.16
  1014.8 79.0 all-gather.18
  2693.2 131.3 all-reduce.38
  2826.9 143.3 reduce-scatter.28
  2973.3 135.8 reduce-scatter.14
  3114.8 93.6 reduce-scatter.30
  3214.3 98.0 reduce-scatter.22
  3319.4 113.3 reduce-scatter.18
  3439.1 118.3 reduce-scatter.20
  3564.8 134.8 reduce-scatter.24
  3706.0 134.5 reduce-scatter.26
  3843.5 1401.5 reduce-scatter.16
where the time goes:
time: 5270 us; the launch traced here: 5250 us
  waiting for transfers between devices  2430 us (46%)
  matrix products  983 us (19%)
  local copies, waits for them, and re-layouts  953 us (18%)
  blocking collectives  490 us (9%)
  other arithmetic  368 us (7%)
    reduce_scatter x1, waiting for transfers between devices, body(): lax.psum_scatter(grad_high_weight, ('narrow', 'wide'), scatter_dimension=...  1400 us
    reshape x8, local copies, waits for them, and re-layouts, pool_block(): prior_value = prior_value.reshape(word_count, char_count, -1)  379 us
    dot_general x11, matrix products, back_dot(): lax.dot_general(grad_rows, weight, (((1,), (1,)), ((), ())), preferred_el...  350 us
    dot_general x8, matrix products, pool_block(): jnp.dot(windows.reshape(word_count * char_count, taps_width), matrix, pre...  281 us
    mul x8, local copies, waits for them, and re-layouts, convolution_pullback(): (pooling_gradient / block_size_entry[:, None].astype(jnp.float32))[:, Non...  268 us
    dot_general x11, matrix products, outer_sum(): lax.dot_general(left_rows, right_rows, (((0,), (0,)), ((), ())), preferre...  243 us
    unnamed x18, waiting for transfers between devices  232 us
    reduce_scatter x1, waiting for transfers between devices, body(): lax.psum_scatter(grad_up_weight, ('narrow', 'wide'), scatter_dimension=1,...  142 us
  transfers between devices with their start and end apart: 16, of which 11 were waited for; matrix products, arithmetic and copies ran while one was open for 13% of the time, Pallas kernels for 0%

commit v1 on v0

v1 whole, which is shorter than its diff:
```python
from functools import partial

import jax
import jax.numpy as jnp
from jax import lax
from jax.experimental import pallas as pl
from jax.experimental.pallas import tpu as pltpu
from jax.sharding import PartitionSpec as P

HEADS = 12
HEAD_DIM = 64
CHAR_DIM = 16
TAPS = 7
EPSILON = 1e-12

LANES = 128
GROUP = LANES // CHAR_DIM
BLOCK_WORDS = 32
CHUNK_BLOCKS = 16
CHUNK = BLOCK_WORDS * CHUNK_BLOCKS
TABLE_PAD = 384
ROW_TILE = 128
BIAS_LANE = TAPS * CHAR_DIM

F32 = jnp.float32
BF16 = jnp.bfloat16
VMEM = pl.BlockSpec(memory_space=pltpu.VMEM)
SMEM = pl.BlockSpec(memory_space=pltpu.SMEM)
MIB = 1024 * 1024


def dot(left, right):
    return lax.dot_general(left, right, (((1,), (0,)), ((), ())), preferred_element_type=F32)


def dot_nt(left, right):
    return lax.dot_general(left, right, (((1,), (1,)), ((), ())), preferred_element_type=F32)


def dot_tn(left, right):
    return lax.dot_general(left, right, (((0,), (0,)), ((), ())), preferred_element_type=F32)


def column_sum(values):
    return jnp.sum(values.astype(F32), axis=0)


def filter_widths(filter_count):
    column = jnp.arange(filter_count)
    widths = jnp.ones((filter_count,), jnp.int32)
    for exponent in range(6):
        widths = widths + (column >= filter_count * 2**exponent // 64).astype(jnp.int32)
    return widths


def sort_words(char_ids, lengths, groups):
    words, chars = char_ids.shape
    index = jnp.arange(words)
    longer = lengths[None, :] > lengths[:, None]
    tie = (lengths[None, :] == lengths[:, None]) & (index[None, :] < index[:, None])
    rank = jnp.sum((longer | tie).astype(jnp.int32), axis=1)
    perm = (rank[None, :] == index[:, None]).astype(BF16)
    live = jnp.arange(chars)[None, :] < lengths[:, None]
    shifted = jnp.where(live, char_ids + 1, 0)
    packed = jnp.concatenate(
        [shifted >> 4, shifted & 15, lengths[:, None]], axis=1
    ).astype(BF16)
    sorted_packed = dot(perm, packed).astype(jnp.int32)
    ids = (sorted_packed[:, :chars] << 4) + sorted_packed[:, chars : 2 * chars] - 1
    ids = jnp.pad(ids, ((0, 0), (0, GROUP * groups - chars)), constant_values=-1)
    sorted_lengths = sorted_packed[:, 2 * chars]
    tile_count = words // BLOCK_WORDS
    tile_max = jnp.max(sorted_lengths.reshape(tile_count, BLOCK_WORDS), axis=1)
    cum = jnp.cumsum(tile_max)
    total = cum[-1]
    block = jnp.arange(tile_count * chars + CHUNK_BLOCKS)
    tile = jnp.sum((block[:, None] >= cum[None, :]).astype(jnp.int32), axis=1)
    start = jnp.sum(
        jnp.where(tile[:, None] == jnp.arange(tile_count)[None, :], (cum - tile_max)[None, :], 0),
        axis=1,
    )
    valid = block < total
    position = jnp.where(valid, block - start, chars).astype(jnp.int32)
    tile = jnp.where(valid, tile, 0).astype(jnp.int32)
    chunks = (total + CHUNK_BLOCKS - 1) // CHUNK_BLOCKS
    reach = jnp.sum(
        (sorted_lengths[None, :] > GROUP * jnp.arange(groups - 1)[:, None]).astype(jnp.int32), axis=1
    )
    scalars = jnp.concatenate([chunks[None], (reach + ROW_TILE - 1) // ROW_TILE]).astype(jnp.int32)
    return perm, ids, sorted_lengths, scalars, tile, position


def build_windows(chunk, tile_ref, pos_ref, g_ref, len_ref, x_ref):
    lane = lax.broadcasted_iota(jnp.int32, (BLOCK_WORDS, LANES), 1)
    for b in range(CHUNK_BLOCKS):
        block = chunk * CHUNK_BLOCKS + b
        row = pl.multiple_of(tile_ref[block] * BLOCK_WORDS, BLOCK_WORDS)
        position = pos_ref[block]
        group = position >> 3
        offset = (position & 7) * CHAR_DIM
        shift = lax.rem(LANES - offset, LANES)
        here = pltpu.roll(g_ref[group, pl.ds(row, BLOCK_WORDS), :].astype(F32), shift, 1)
        after = pltpu.roll(g_ref[group + 1, pl.ds(row, BLOCK_WORDS), :].astype(F32), shift, 1)
        live = (len_ref[pl.ds(row, BLOCK_WORDS), :] > position).astype(F32)
        value = jnp.where(lane < LANES - offset, here, after)
        value = jnp.where(lane < BIAS_LANE, value, jnp.where(lane == BIAS_LANE, live, 0.0))
        x_ref[b * BLOCK_WORDS : (b + 1) * BLOCK_WORDS, :] = value.astype(BF16)


def conv_forward_kernel(
    scalar_ref, tile_ref, pos_ref, ids_ref, table_ref, w_ref, len_ref, pooled_ref, g_ref, x_ref, pre_ref
):
    groups = g_ref.shape[0]
    filters = w_ref.shape[1]
    part = pre_ref.shape[1]
    g_ref[...] = jnp.zeros_like(g_ref)
    pooled_ref[...] = jnp.zeros_like(pooled_ref)
    identity = lax.broadcasted_iota(jnp.int32, (ROW_TILE, TABLE_PAD), 1)
    for group in range(groups - 1):

        def embed(step, carry, group=group):
            row = pl.multiple_of(step * ROW_TILE, ROW_TILE)
            total = jnp.zeros((ROW_TILE, LANES), F32)
            for k in range(GROUP):
                column = group * GROUP + k
                hot = (ids_ref[pl.ds(row, ROW_TILE), column : column + 1] == identity).astype(F32)
                total = total + dot(hot.astype(BF16), table_ref[k])
            g_ref[group, pl.ds(row, ROW_TILE), :] = total.astype(BF16)
            return carry

        lax.fori_loop(0, scalar_ref[1 + group], embed, 0)

    def step(chunk, carry):
        build_windows(chunk, tile_ref, pos_ref, g_ref, len_ref, x_ref)
        for first in range(0, filters, part):
            half = dot(x_ref[...], w_ref[:, first : first + part])
            pre_ref[...] = half + half * jnp.tanh(half)
            for b in range(CHUNK_BLOCKS):
                row = pl.multiple_of(
                    tile_ref[chunk * CHUNK_BLOCKS + b] * BLOCK_WORDS, BLOCK_WORDS
                )
                pooled_ref[pl.ds(row, BLOCK_WORDS), first : first + part] += pre_ref[
                    b * BLOCK_WORDS : (b + 1) * BLOCK_WORDS, :
                ]
        return carry

    lax.fori_loop(0, scalar_ref[0], step, 0)
    pooled_ref[...] = pooled_ref[...] / len_ref[...].astype(F32)


def conv_forward(prep, table_blocks, half_matrix):
    _, ids, lengths, scalars, tile, position = prep
    words = ids.shape[0]
    groups = ids.shape[1] // GROUP
    filters = half_matrix.shape[1]
    return pl.pallas_call(
        conv_forward_kernel,
        out_shape=(
            jax.ShapeDtypeStruct((words, filters), F32),
            jax.ShapeDtypeStruct((groups, words, LANES), BF16),
        ),
        in_specs=[SMEM, SMEM, SMEM, VMEM, VMEM, VMEM, VMEM],
        out_specs=(VMEM, VMEM),
        scratch_shapes=[pltpu.VMEM((CHUNK, LANES), BF16), pltpu.VMEM((CHUNK, 512), F32)],
        compiler_params=pltpu.CompilerParams(vmem_limit_bytes=32 * MIB),
        name="conv_forward",
    )(scalars, tile, position, ids, table_blocks, half_matrix, lengths[:, None])


def conv_backward_kernel(
    scalar_ref, tile_ref, pos_ref, g_ref, w_ref, len_ref, gp_ref, gg_in_ref, dw_ref, gg_ref, x_ref, d_ref
):
    lane = lax.broadcasted_iota(jnp.int32, (BLOCK_WORDS, LANES), 1)
    dw_ref[...] = jnp.zeros_like(dw_ref)
    gg_ref[...] = gg_in_ref[...]

    def step(chunk, carry):
        build_windows(chunk, tile_ref, pos_ref, g_ref, len_ref, x_ref)
        half = dot(x_ref[...], w_ref[...])
        tanh = jnp.tanh(half)
        slope = (1.0 + tanh) * (1.0 + (half - half * tanh))
        for b in range(CHUNK_BLOCKS):
            rows = slice(b * BLOCK_WORDS, (b + 1) * BLOCK_WORDS)
            row = pl.multiple_of(tile_ref[chunk * CHUNK_BLOCKS + b] * BLOCK_WORDS, BLOCK_WORDS)
            d_ref[rows, :] = (gp_ref[pl.ds(row, BLOCK_WORDS), :] * slope[rows]).astype(BF16)
        dw_ref[...] += dot_tn(x_ref[...], d_ref[...])
        gx = dot_nt(d_ref[...], w_ref[...])
        for b in range(CHUNK_BLOCKS):
            block = chunk * CHUNK_BLOCKS + b
            row = pl.multiple_of(tile_ref[block] * BLOCK_WORDS, BLOCK_WORDS)
            position = pos_ref[block]
            group = position >> 3
            offset = (position & 7) * CHAR_DIM
            value = gx[b * BLOCK_WORDS : (b + 1) * BLOCK_WORDS, :]
            value = pltpu.roll(jnp.where(lane < BIAS_LANE, value, 0.0), offset, 1)
            gg_ref[group, pl.ds(row, BLOCK_WORDS), :] += jnp.where(lane >= offset, value, 0.0)
            gg_ref[group + 1, pl.ds(row, BLOCK_WORDS), :] += jnp.where(lane < offset, value, 0.0)
        return carry

    lax.fori_loop(0, scalar_ref[0], step, 0)


def conv_backward(prep, char_groups, half_matrix, grad_scaled, grad_groups, first, part):
    _, ids, lengths, scalars, tile, position = prep
    filters = half_matrix.shape[1]
    return pl.pallas_call(
        conv_backward_kernel,
        grid=(1,),
        out_shape=(
            jax.ShapeDtypeStruct((LANES, part), F32),
            jax.ShapeDtypeStruct(grad_groups.shape, F32),
        ),
        in_specs=[
            SMEM,
            SMEM,
            SMEM,
            VMEM,
            pl.BlockSpec((LANES, part), lambda i: (0, first // part)),
            VMEM,
            pl.BlockSpec((grad_scaled.shape[0], part), lambda i: (0, first // part)),
            VMEM,
        ],
        out_specs=(VMEM, VMEM),
        scratch_shapes=[pltpu.VMEM((CHUNK, LANES), BF16), pltpu.VMEM((CHUNK, part), BF16)],
        compiler_params=pltpu.CompilerParams(vmem_limit_bytes=32 * MIB),
        name="conv_backward",
    )(scalars, tile, position, char_groups, half_matrix, lengths[:, None], grad_scaled, grad_groups)


def table_kernel(scalar_ref, ids_ref, gg_ref, out_ref):
    groups = gg_ref.shape[0]
    out_ref[...] = jnp.zeros_like(out_ref)
    identity = lax.broadcasted_iota(jnp.int32, (TABLE_PAD, ROW_TILE), 0)
    for group in range(groups - 1):

        def step(index, carry, group=group):
            row = pl.multiple_of(index * ROW_TILE, ROW_TILE)
            grad = (2.0 * gg_ref[group, pl.ds(row, ROW_TILE), :]).astype(BF16)
            for k in range(GROUP):
                column = group * GROUP + k
                hot = (ids_ref[column : column + 1, pl.ds(row, ROW_TILE)] == identity).astype(F32)
                out_ref[k] += dot(hot.astype(BF16), grad)
            return carry

        lax.fori_loop(0, scalar_ref[1 + group], step, 0)


def table_gradient(prep, grad_groups, vocabulary):
    ids, scalars = prep[1], prep[3]
    total = pl.pallas_call(
        table_kernel,
        out_shape=jax.ShapeDtypeStruct((GROUP, TABLE_PAD, LANES), F32),
        in_specs=[SMEM, VMEM, VMEM],
        out_specs=VMEM,
        compiler_params=pltpu.CompilerParams(vmem_limit_bytes=32 * MIB),
        name="table_gradient",
    )(scalars, ids.T, grad_groups)
    parts = [total[k, :vocabulary, k * CHAR_DIM : (k + 1) * CHAR_DIM] for k in range(GROUP)]
    return sum(parts[1:], parts[0])


def table_lanes(table):
    padded = jnp.pad(table, ((0, TABLE_PAD - table.shape[0]), (0, 0)))
    return jnp.stack(
        [
            jnp.pad(padded, ((0, 0), (k * CHAR_DIM, LANES - (k + 1) * CHAR_DIM)))
            for k in range(GROUP)
        ]
    )


def piece_specs(pieces, steps_per_array=2):
    specs = []
    for half in pieces:
        for chunk in half:
            for number, array in enumerate(chunk):

                def index(j, *_, number=number):
                    return (0, jnp.clip(j - number * steps_per_array, 0, steps_per_array - 1), 0, 0)

                specs.append(pl.BlockSpec((2, 1) + array.shape[2:], index))
    return specs


def flat_pieces(pieces):
    return [array for half in pieces for chunk in half for array in chunk]


def highway_forward_kernel(layout, place_ref, select_ref, core_ref, h_ref, bias_ref, *refs):
    halves, chunks, arrays, rows = layout
    pieces = refs[: halves * chunks * arrays]
    next_ref, transform_ref, gating_ref, low_ref = refs[halves * chunks * arrays :]
    step = pl.program_id(0)
    width = next_ref.shape[1]

    @pl.when(step == 0)
    def _():
        low_ref[...] = h_ref[...].astype(BF16)

    block = place_ref[step]
    blocks = bias_ref.shape[0] // 2
    first = select_ref[step]
    own = core_ref[0]
    for array in range(arrays):

        @pl.when(step // 2 == array)
        def _(array=array):
            transform = jnp.broadcast_to(bias_ref[block], transform_ref.shape)
            gate = jnp.broadcast_to(bias_ref[block + blocks], transform_ref.shape)
            for half in range(halves):
                for chunk in range(chunks):
                    ref = pieces[(half * chunks + chunk) * arrays + array]
                    start = (own if half == 0 else 1 - own) * (chunks * rows) + chunk * rows
                    left = low_ref[:, pl.ds(pl.multiple_of(start, rows), rows)]
                    transform = transform + dot(left, ref[first, 0])
                    gate = gate + dot(left, ref[1 - first, 0])
            gating = 1.0 / (1.0 + jnp.exp(-gate))
            activated = transform / (1.0 + jnp.exp(-transform))
            h = h_ref[:, pl.ds(pl.multiple_of(block * width, width), width)]
            transform_ref[...] = transform
            gating_ref[...] = gating
            next_ref[...] = gating * h + (1.0 - gating) * activated


def highway_forward(h, pieces, bias_blocks, place, select, core):
    words, features = h.shape
    width = bias_blocks.shape[2]
    flat = flat_pieces(pieces)
    layout = (len(pieces), len(pieces[0]), len(pieces[0][0]), flat[0].shape[2])
    column = pl.BlockSpec((words, width), lambda j, place, *_: (0, place[j]))
    whole = lambda shape: pl.BlockSpec(shape, lambda j, *_: (0,) * len(shape))
    return pl.pallas_call(
        partial(highway_forward_kernel, layout),
        grid_spec=pltpu.PrefetchScalarGridSpec(
            num_scalar_prefetch=3,
            grid=(features // width,),
            in_specs=[whole(h.shape), whole(bias_blocks.shape)] + piece_specs(pieces),
            out_specs=[column, column, column, whole(h.shape)],
        ),
        out_shape=(
            jax.ShapeDtypeStruct(h.shape, F32),
            jax.ShapeDtypeStruct(h.shape, F32),
            jax.ShapeDtypeStruct(h.shape, F32),
            jax.ShapeDtypeStruct(h.shape, BF16),
        ),
        compiler_params=pltpu.CompilerParams(vmem_limit_bytes=56 * MIB),
        name="highway_forward",
    )(place, select, core, h, bias_blocks, *flat)


def highway_backward_kernel(layout, place_ref, select_ref, core_ref, grad_ref, h_ref, t_ref, g_ref, *refs):
    halves, chunks, arrays, rows = layout
    pieces = refs[: halves * chunks * arrays]
    mixed_ref, sums_ref, out_ref = refs[halves * chunks * arrays :]
    step = pl.program_id(0)
    width = grad_ref.shape[1]

    @pl.when(step == 0)
    def _():
        out_ref[...] = jnp.zeros_like(out_ref)

    own = core_ref[0]
    block = place_ref[step]
    first = select_ref[step]
    grad = grad_ref[...]
    transform = t_ref[...]
    gating = g_ref[...]
    sigmoid = 1.0 / (1.0 + jnp.exp(-transform))
    activated = transform * sigmoid
    low_t = (grad * (1.0 - gating) * (sigmoid + activated * (1.0 - sigmoid))).astype(BF16)
    low_g = (grad * (h_ref[...] - activated) * gating * (1.0 - gating)).astype(BF16)
    mixed_ref[0] = low_t
    mixed_ref[1] = low_g
    sums_ref[0] = jnp.sum(low_t.astype(F32), axis=0, keepdims=True)
    sums_ref[1] = jnp.sum(low_g.astype(F32), axis=0, keepdims=True)
    for array in range(arrays):

        @pl.when(step // 2 == array)
        def _(array=array):
            for half in range(halves):
                for chunk in range(chunks):
                    ref = pieces[(half * chunks + chunk) * arrays + array]
                    start = (own if half == 0 else 1 - own) * (chunks * rows) + chunk * rows
                    columns = pl.ds(pl.multiple_of(start, rows), rows)
                    out_ref[:, columns] += dot_nt(low_t, ref[first, 0]) + dot_nt(
                        low_g, ref[1 - first, 0]
                    )

    out_ref[:, pl.ds(pl.multiple_of(block * width, width), width)] += grad * gating


def highway_backward(grad, h, transform, gating, pieces, place, select, core):
    words, features = h.shape
    flat = flat_pieces(pieces)
    width = flat[0].shape[3]
    layout = (len(pieces), len(pieces[0]), len(pieces[0][0]), flat[0].shape[2])
    column = pl.BlockSpec((words, width), lambda j, place, *_: (0, place[j]))
    return pl.pallas_call(
        partial(highway_backward_kernel, layout),
        grid_spec=pltpu.PrefetchScalarGridSpec(
            num_scalar_prefetch=3,
            grid=(features // width,),
            in_specs=[column] * 4 + piece_specs(pieces),
            out_specs=[
                pl.BlockSpec((2, words, width), lambda j, place, *_: (0, 0, place[j])),
                pl.BlockSpec((2, 1, width), lambda j, place, *_: (0, 0, place[j])),
                pl.BlockSpec(h.shape, lambda j, *_: (0, 0)),
            ],
        ),
        out_shape=(
            jax.ShapeDtypeStruct((2, words, features), BF16),
            jax.ShapeDtypeStruct((2, 1, features), F32),
            jax.ShapeDtypeStruct(h.shape, F32),
        ),
        compiler_params=pltpu.CompilerParams(vmem_limit_bytes=56 * MIB),
        name="highway_backward",
    )(place, select, core, grad, h, transform, gating, *flat)


def weight_kernel(which_ref, left_ref, right_ref, out_ref):
    value = dot(left_ref[...], right_ref[0]).astype(BF16)
    width = out_ref.shape[2]
    out_ref[0] = value[:, :width]
    out_ref[1] = value[:, width:]


def highway_weight_gradient(which, turned, mixed, first, rows, width):
    words, features = mixed.shape[1:]
    return pl.pallas_call(
        weight_kernel,
        grid_spec=pltpu.PrefetchScalarGridSpec(
            num_scalar_prefetch=1,
            grid=(features // (2 * width),),
            in_specs=[
                pl.BlockSpec((rows, words), lambda j, which: (first // rows, 0)),
                pl.BlockSpec((1, words, 2 * width), lambda j, which: (which[0], 0, j)),
            ],
            out_specs=pl.BlockSpec((2, rows, width), lambda j, which: (j, 0, 0)),
        ),
        out_shape=jax.ShapeDtypeStruct((features // width, rows, width), BF16),
        compiler_params=pltpu.CompilerParams(vmem_limit_bytes=32 * MIB),
        name="highway_weight",
    )(which, turned, mixed)


def turn_kernel(value_ref, out_ref):
    out_ref[...] = value_ref[...].T.astype(BF16)


def turn(value):
    rows, columns = value.shape
    return pl.pallas_call(
        turn_kernel,
        grid=(columns // 256,),
        in_specs=[pl.BlockSpec((rows, 256), lambda j: (0, j))],
        out_specs=pl.BlockSpec((256, rows), lambda j: (j, 0)),
        out_shape=jax.ShapeDtypeStruct((columns, rows), BF16),
        compiler_params=pltpu.CompilerParams(vmem_limit_bytes=32 * MIB),
        name="turn",
    )(value)


def place_rows_kernel(splits, place_ref, core_ref, *refs):
    arrays = (len(refs) - len(splits) - 1) // 2
    own_refs, other_refs = refs[:arrays], refs[arrays : 2 * arrays]
    out_refs, whole_ref = refs[2 * arrays : -1], refs[-1]
    step = pl.program_id(0)
    half_rows = own_refs[0].shape[1]
    core = core_ref[0]
    for array in range(arrays):

        @pl.when(step // 4 == array)
        def _(array=array):
            align = lambda start: pl.ds(pl.multiple_of(start, 16), half_rows)
            whole_ref[align(core * half_rows), :] = own_refs[array][0]
            whole_ref[align((1 - core) * half_rows), :] = other_refs[array][0]

    start = 0
    for rows, out_ref in zip(splits, out_refs):
        out_ref[...] = whole_ref[start : start + rows, :]
        start += rows


def place_rows(own, other, place, core, splits):
    half_rows, columns = own[0].shape[1:]

    def index(number):
        return lambda j, *_: (jnp.clip(j - 4 * number, 0, 3), 0, 0)

    specs = [pl.BlockSpec((1, half_rows, columns), index(number)) for number in range(len(own))]
    return pl.pallas_call(
        partial(place_rows_kernel, splits),
        grid_spec=pltpu.PrefetchScalarGridSpec(
            num_scalar_prefetch=2,
            grid=(4 * len(own),),
            in_specs=specs + specs,
            out_specs=[
                pl.BlockSpec((rows, columns), lambda j, place, *_: (place[j], 0)) for rows in splits
            ],
            scratch_shapes=[pltpu.VMEM((2 * half_rows, columns), BF16)],
        ),
        out_shape=[
            jax.ShapeDtypeStruct((4 * len(own) * rows, columns), BF16) for rows in splits
        ],
        compiler_params=pltpu.CompilerParams(vmem_limit_bytes=32 * MIB),
        name="place_rows",
    )(place, core, *own, *other)


X_PAIRS = [(w, w ^ 1) for w in range(16)]
Y_PAIRS = [(w, w ^ 2) for w in range(16)]
Z_RING = [(w, (w + 4) % 16) for w in range(16)]
CORES = [(0, 1), (1, 0)]


def swap_cores(value):
    return lax.ppermute(value, "narrow", CORES)


def along(value, pairs):
    return lax.ppermute(value, "wide", pairs)


def ring_gather(value):
    received = [value]
    for _ in range(3):
        received.append(along(received[-1], Z_RING))
    return received


def gather_ring_first(value, order):
    own = jnp.stack(ring_gather(value))
    if order == "zxy":
        over_x = along(own, X_PAIRS)
        return [own, over_x, along(own, Y_PAIRS), along(over_x, Y_PAIRS)]
    over_y = along(own, Y_PAIRS)
    return [own, along(own, X_PAIRS), over_y, along(over_y, X_PAIRS)]


def gather_ring_last(value):
    over_x = along(value, X_PAIRS)
    return ring_gather(
        jnp.stack([value, over_x, along(value, Y_PAIRS), along(over_x, Y_PAIRS)])
    )


def total_of(terms):
    return sum((term.astype(F32) for term in terms[1:]), terms[0].astype(F32))


def pick(terms, index, axis):
    return [lax.dynamic_index_in_dim(term, index, axis, keepdims=False) for term in terms]


def halve(terms, coordinate, axis, pairs):
    sent = total_of(pick(terms, 1 - coordinate, axis)).astype(BF16)
    return pick(terms, coordinate, axis) + [along(sent, pairs)]


def ring_reduce(terms, z):
    running = []
    for distance in (3, 2, 1):
        sent = total_of(pick(terms, (z + distance) % 4, 0) + running).astype(BF16)
        running = [along(sent, Z_RING)]
    return pick(terms, z, 0) + running


def scatter_sum(keep, send, coords, order):
    z, y, x = coords
    shape = (4, 2, 2) + keep.shape[1:]
    terms = [keep.reshape(shape), swap_cores(send).reshape(shape)]
    if order == "zyx":
        terms = ring_reduce(terms, z)
        terms = halve(terms, y, 0, Y_PAIRS)
        terms = halve(terms, x, 0, X_PAIRS)
    elif order == "yxz":
        terms = halve(terms, y, 1, Y_PAIRS)
        terms = halve(terms, x, 1, X_PAIRS)
        terms = ring_reduce(terms, z)
    else:
        terms = halve(terms, x, 2, X_PAIRS)
        terms = halve(terms, y, 1, Y_PAIRS)
        terms = ring_reduce(terms, z)
    return total_of(terms)


def scatter_vectors(parts, devices):
    packed = [
        jnp.moveaxis(part.reshape(part.shape[:-1] + (devices, -1)), -2, 0).reshape(devices, -1)
        for part in parts
    ]
    total = lax.psum_scatter(
        jnp.concatenate(packed, axis=1), ("narrow", "wide"), scatter_dimension=0, tiled=True
    )[0]
    results, start = [], 0
    for part in parts:
        shape = part.shape[:-1] + (part.shape[-1] // devices,)
        size = part.size // devices
        results.append(total[start : start + size].reshape(shape))
        start += size
    return results


def gather_vectors(parts, wide):
    packed = jnp.concatenate(parts)
    packed = jnp.pad(packed, (0, -packed.shape[0] % 1024))
    whole = lax.all_gather(packed, "wide", axis=0, tiled=False)
    results, start = [], 0
    for part in parts:
        results.append(whole[:, start : start + part.shape[0]].reshape(-1))
        start += part.shape[0]
    return results


class Exchange:
    def __init__(self):
        self.core = lax.axis_index("narrow")
        index = lax.axis_index("wide")
        self.z, self.y, self.x = index // 4, (index // 2) % 2, index % 2

    def half(self, value, rows, offset=0):
        start = self.core * (value.shape[0] // 2) + offset
        return lax.dynamic_slice_in_dim(value, start, rows, 0)

    def highway_pieces(self, weight, chunks):
        rows = weight.shape[0] // (2 * chunks)
        own, other = [], []
        for chunk in range(chunks):
            block = self.half(weight, rows, chunk * rows)
            arrays = gather_ring_first(block, "zxy" if chunk % 2 == 0 else "zyx")
            arrays = [array.reshape((2, 2) + block.shape) for array in arrays]
            own.append(arrays)
            other.append([swap_cores(array) for array in arrays])
        return own, other

    def rows(self, values, order):
        value = jnp.concatenate(values, axis=0)
        splits = [value.shape[0] for value in values]
        half = self.half(value, value.shape[0] // 2)
        arrays = gather_ring_last(half) if order == "xyz" else gather_ring_first(half, order)
        others = [swap_cores(array) for array in arrays]
        step = jnp.arange(16)
        near, slot = (step % 4, step // 4) if order == "xyz" else (step // 4, step % 4)
        place = (
            (self.z - slot) % 4 * 4 + (self.y ^ (near >> 1)) * 2 + (self.x ^ (near & 1))
        ).astype(jnp.int32)
        return place_rows(arrays, others, place, self.core[None].astype(jnp.int32), splits)

    def turned_pos(self, value):
        return value.T.reshape(-1, 768)

    def sum_columns(self, keep, send, order):
        return scatter_sum(keep, send, (self.z, self.y, self.x), order)

    def sum_rows(self, grads, order):
        columns = grads[0].shape[1]
        blocks = [grad.astype(BF16).reshape(2, 16, -1, columns) for grad in grads]
        packed = jnp.concatenate(blocks, axis=2)
        keep = lax.dynamic_index_in_dim(packed, self.core, 0, keepdims=False)
        send = lax.dynamic_index_in_dim(packed, 1 - self.core, 0, keepdims=False)
        total = scatter_sum(keep, send, (self.z, self.y, self.x), order)
        results, start = [], 0
        for block in blocks:
            results.append(total[start : start + block.shape[2]])
            start += block.shape[2]
        return results


class PlainExchange:
    def __init__(self):
        self.core = self.z = self.y = self.x = jnp.zeros((), jnp.int32)

    def highway_pieces(self, weight, chunks):
        whole = lax.all_gather(weight, "wide", axis=1, tiled=True)
        rows = whole.shape[0] // (2 * chunks)
        width = whole.shape[1] // 16
        halves = []
        for half in range(2):
            pieces = []
            for chunk in range(chunks):
                start = (half * chunks + chunk) * rows
                arrays = []
                for near in range(4):
                    slots = []
                    for slot in range(4):
                        block = (-slot % 4) * 4 + near
                        slots.append(
                            whole[start : start + rows, block * width : (block + 1) * width]
                        )
                    arrays.append(jnp.stack(slots).reshape(2, 2, rows, width))
                pieces.append(arrays)
            halves.append(pieces)
        return halves

    def rows(self, values, order):
        return [lax.all_gather(value, "wide", axis=0, tiled=True) for value in values]

    def turned_pos(self, value):
        return value.T

    def sum_columns(self, keep, send, order):
        whole = jnp.concatenate([keep, send], axis=0)
        rows = whole.shape[1]
        whole = jnp.moveaxis(whole, 1, 0).reshape(rows, -1)
        return lax.psum_scatter(
            whole, ("narrow", "wide"), scatter_dimension=1, tiled=True
        ).astype(F32)

    def sum_rows(self, grads, order):
        return [
            lax.psum_scatter(
                grad.astype(BF16), ("narrow", "wide"), scatter_dimension=0, tiled=True
            ).astype(F32)
            for grad in grads
        ]


def norm_rows(value, norm_gain, norm_shift):
    center = jnp.mean(value, axis=-1, keepdims=True)
    offsets = value - center
    spread = jnp.mean(offsets * offsets, axis=-1, keepdims=True)
    return offsets * lax.rsqrt(spread + EPSILON) * norm_gain + norm_shift


def norm_back(value, norm_gain, grad_rows):
    center = jnp.mean(value, axis=-1, keepdims=True)
    offsets = value - center
    spread = jnp.mean(offsets * offsets, axis=-1, keepdims=True)
    scale = lax.rsqrt(spread + EPSILON)
    normal = offsets * scale
    inner = grad_rows * norm_gain
    grad = scale * (
        inner
        - jnp.mean(inner, axis=-1, keepdims=True)
        - normal * jnp.mean(inner * normal, axis=-1, keepdims=True)
    )
    return grad, jnp.sum(grad_rows * normal, axis=0), jnp.sum(grad_rows, axis=0)


def softmax_parts(query, key):
    scores = dot_nt(query, key) * HEAD_DIM ** (-0.5)
    exponent = jnp.exp(scores - jnp.max(scores, axis=-1, keepdims=True))
    return exponent, 1.0 / jnp.sum(exponent, axis=-1, keepdims=True)


def attend_kernel(query_ref, key_ref, value_ref, out_ref):
    for start in range(0, LANES, HEAD_DIM):
        head = slice(start, start + HEAD_DIM)
        exponent, scale = softmax_parts(query_ref[:, head], key_ref[:, head])
        attention = (exponent * scale).astype(BF16)
        out_ref[:, head] = dot(attention, value_ref[:, head]).astype(BF16)


def third(number, words, thirds):
    return pl.BlockSpec((words, LANES), lambda j: (0, number * thirds + j))


def attend(qkv):
    words = qkv.shape[0]
    pairs = qkv.shape[1] // (3 * LANES)
    return pl.pallas_call(
        attend_kernel,
        grid=(pairs,),
        in_specs=[third(number, words, pairs) for number in range(3)],
        out_specs=third(0, words, pairs),
        out_shape=jax.ShapeDtypeStruct((words, pairs * LANES), BF16),
        compiler_params=pltpu.CompilerParams(vmem_limit_bytes=32 * MIB),
        name="attend",
    )(qkv, qkv, qkv)


def attend_back_kernel(
    query_ref, key_ref, value_ref, grad_ref, grad_query_ref, grad_key_ref, grad_value_ref
):
    scaling = HEAD_DIM ** (-0.5)
    for start in range(0, LANES, HEAD_DIM):
        head = slice(start, start + HEAD_DIM)
        query, key = query_ref[:, head], key_ref[:, head]
        grad = grad_ref[:, head]
        exponent, scale = softmax_parts(query, key)
        attention = exponent * scale
        grad_attention = dot_nt(grad, value_ref[:, head])
        inner = jnp.sum(grad_attention * attention, axis=-1, keepdims=True)
        grad_scores = (attention * (grad_attention - inner)).astype(BF16)
        grad_value_ref[:, head] = dot_tn(attention.astype(BF16), grad).astype(BF16)
        grad_query_ref[:, head] = (dot(grad_scores, key) * scaling).astype(BF16)
        grad_key_ref[:, head] = (dot_tn(grad_scores, query) * scaling).astype(BF16)


def attend_back(qkv, grad_context):
    words = qkv.shape[0]
    pairs = qkv.shape[1] // (3 * LANES)
    out = third(0, words, pairs)
    return jnp.concatenate(
        pl.pallas_call(
            attend_back_kernel,
            grid=(pairs,),
            in_specs=[third(number, words, pairs) for number in range(3)] + [out],
            out_specs=(out, out, out),
            out_shape=(jax.ShapeDtypeStruct(grad_context.shape, BF16),) * 3,
            compiler_params=pltpu.CompilerParams(vmem_limit_bytes=32 * MIB),
            name="attend_back",
        )(qkv, qkv, qkv, grad_context),
        axis=1,
    )


def body(
    permutes,
    wide,
    devices,
    char_ids,
    word_lengths,
    type_ids,
    cotangent,
    character_embedding_table,
    conv_weight,
    conv_bias,
    high_weight,
    high_bias,
    proj_weight,
    proj_bias,
    pos_table,
    type_table,
    embed_gain,
    embed_shift,
    qkv_weight,
    attn_bias,
    out_weight,
    out_bias,
    attn_gain,
    attn_shift,
    up_weight,
    up_bias,
    down_weight,
    down_bias,
    ffn_gain,
    ffn_shift,
):
    net = Exchange() if permutes else PlainExchange()
    layers = high_weight.shape[0]
    words, chars = char_ids.shape[1:]
    lengths = word_lengths[0]
    row_chunks = 2

    vectors = gather_vectors(
        [high_bias[layer] for layer in range(layers)]
        + [
            attn_bias,
            type_table[0],
            type_table[1],
            proj_bias,
            embed_gain,
            embed_shift,
            out_bias,
            attn_gain,
            attn_shift,
            up_bias,
            down_bias,
            ffn_gain,
            ffn_shift,
        ],
        wide,
    )
    high_bias_all, attn_bias_all = vectors[:layers], vectors[layers]
    (
        type_zero,
        type_one,
        proj_bias_all,
        gain_zero,
        shift_zero,
        out_bias_all,
        gain_one,
        shift_one,
        up_bias_all,
        down_bias_all,
        gain_two,
        shift_two,
    ) = (value.astype(F32) for value in vectors[layers + 1 :])
    conv_rows = conv_weight.shape[0]
    conv_blocks = lax.all_gather(
        jnp.pad(
            jnp.concatenate([conv_weight, conv_bias[None]], axis=0),
            ((0, LANES - conv_rows - 1), (0, 0)),
        ),
        "wide",
        axis=0,
        tiled=False,
    )
    conv_all = jnp.concatenate([conv_blocks[w] for w in range(wide)], axis=1)
    pieces = [net.highway_pieces(high_weight[layer], row_chunks) for layer in range(layers)]
    turned_pos = net.turned_pos(pos_table)
    proj_all, pos_all = net.rows([proj_weight, turned_pos], "zxy")
    qkv_all, out_all = net.rows([qkv_weight.T, out_weight], "zyx")
    up_all, down_all = net.rows([up_weight.T, down_weight], "xyz")
    model_width = proj_all.shape[1]
    pos_rows = pos_all.reshape(model_width, words).T.astype(F32)

    filters = conv_all.shape[1]
    row = jnp.arange(LANES)[:, None]
    usable = row // CHAR_DIM < filter_widths(filters)[None, :]
    half_matrix = jnp.where(usable | (row >= conv_rows), conv_all * BF16(0.5), BF16(0.0))
    prep = sort_words(char_ids[0], lengths, chars // GROUP + 2)
    perm, sorted_lengths = prep[0], prep[2]
    pooled, char_groups = conv_forward(prep, table_lanes(character_embedding_table), half_matrix)
    features = pooled.shape[1]
    width = 2 * features // 16
    step = jnp.arange(8)
    near, low_slot = step // 2, step % 2
    slot_z = (net.z - low_slot) % 4
    place = ((slot_z & 1) * 4 + (net.y ^ (near >> 1)) * 2 + (net.x ^ (near & 1))).astype(jnp.int32)
    select = (slot_z // 2).astype(jnp.int32)
    core = net.core[None].astype(jnp.int32)
    bias_blocks = [bias.astype(F32).reshape(16, 1, width) for bias in high_bias_all]
    states, lows, transforms, gatings = [pooled], [], [], []
    for layer in range(layers):
        after, transform, gating, low = highway_forward(
            states[-1], pieces[layer], bias_blocks[layer], place, select, core
        )
        states.append(after)
        lows.append(low)
        transforms.append(transform)
        gatings.append(gating)
    turned = [turn(low) for low in lows]
    last = dot_tn(perm, states[-1].astype(BF16)).astype(BF16)
    word_vec = dot(last, proj_all) + proj_bias_all
    type_rows = jnp.where(type_ids[0][:, None] == 1, type_one[None], type_zero[None])
    summed = word_vec + pos_rows + type_rows
    embedded = norm_rows(summed, gain_zero, shift_zero)
    low_embedded = embedded.astype(BF16)

    bias_three = jnp.concatenate(
        [
            attn_bias_all[:model_width],
            jnp.zeros((model_width,), BF16),
            attn_bias_all[model_width:],
        ]
    ).astype(F32)
    qkv = (dot_nt(low_embedded, qkv_all) + bias_three).astype(BF16)
    context = attend(qkv)
    first_in = embedded + (dot(context, out_all) + out_bias_all)
    first = norm_rows(first_in, gain_one, shift_one)
    low_first = first.astype(BF16)
    inner = dot_nt(low_first, up_all) + up_bias_all
    activation = jax.nn.gelu(inner, approximate=False).astype(BF16)
    second_in = first + (dot(activation, down_all) + down_bias_all)
    hidden_out = norm_rows(second_in, gain_two, shift_two).astype(BF16)

    grad_second, grad_ffn_gain, grad_ffn_shift = norm_back(
        second_in, gain_two, cotangent[0].astype(F32)
    )
    grad_ffn = grad_second.astype(BF16)
    grad_down = dot_tn(activation, grad_ffn)
    grad_down_bias = column_sum(grad_ffn)
    _, gelu_pull = jax.vjp(partial(jax.nn.gelu, approximate=False), inner)
    grad_inner = gelu_pull(dot_nt(grad_ffn, down_all))[0].astype(BF16)
    grad_up = dot_tn(grad_inner, low_first)
    grad_up_bias = column_sum(grad_inner)
    sum_up, sum_down = net.sum_rows([grad_up, grad_down], "zyx")
    grad_resid, grad_attn_gain, grad_attn_shift = norm_back(
        first_in, gain_one, grad_second + dot(grad_inner, up_all)
    )
    grad_branch = grad_resid.astype(BF16)
    grad_out = dot_tn(context, grad_branch)
    grad_out_bias = column_sum(grad_branch)
    grad_context = dot_nt(grad_branch, out_all).astype(BF16)
    grad_qkv = attend_back(qkv, grad_context)
    grad_qkv_weight = dot_tn(grad_qkv, low_embedded)
    sum_qkv, sum_out = net.sum_rows([grad_qkv_weight, grad_out], "xyz")
    qkv_sums = column_sum(grad_qkv)
    grad_attn_bias = jnp.concatenate([qkv_sums[:model_width], qkv_sums[2 * model_width :]])

    grad_summed, grad_embed_gain, grad_embed_shift = norm_back(
        summed, gain_zero, grad_resid + dot(grad_qkv, qkv_all)
    )
    type_hot = (type_ids[0] == 1).astype(F32)[:, None]
    grad_type = jnp.stack(
        [jnp.sum((1.0 - type_hot) * grad_summed, axis=0), jnp.sum(type_hot * grad_summed, axis=0)]
    )
    grad_word = grad_summed.astype(BF16)
    grad_proj = dot_tn(last, grad_word)
    grad_proj_bias = column_sum(grad_word)
    (sum_proj,) = net.sum_rows([grad_proj], "yxz")
    (sum_pos,) = net.sum_rows([turn(grad_summed)], "zyx")
    sum_pos = sum_pos.T
    vector_sums = scatter_vectors(
        [
            grad_proj_bias,
            grad_type,
            grad_embed_gain,
            grad_embed_shift,
            grad_attn_bias,
            grad_out_bias,
            grad_attn_gain,
            grad_attn_shift,
            grad_up_bias,
            grad_down_bias,
            grad_ffn_gain,
            grad_ffn_shift,
        ],
        devices,
    )
    (
        sum_proj_bias,
        sum_type,
        sum_embed_gain,
        sum_embed_shift,
        sum_attn_bias,
        sum_out_bias,
        sum_attn_gain,
        sum_attn_shift,
        sum_up_bias,
        sum_down_bias,
        sum_ffn_gain,
        sum_ffn_shift,
    ) = vector_sums

    running = dot_nt(dot(perm, grad_word).astype(BF16), proj_all)
    chunk_rows = features // 4
    keep_half = core
    send_half = 1 - core
    high_sums, bias_sums = [None] * layers, [None] * layers
    for layer in reversed(range(layers)):
        mixed, sums, running = highway_backward(
            running,
            states[layer],
            transforms[layer],
            gatings[layer],
            pieces[layer],
            place,
            select,
            core,
        )
        bias_sums[layer] = sums.reshape(-1)
        parts = []
        for chunk in range(4):
            send, keep = (
                highway_weight_gradient(
                    which, turned[layer], mixed, chunk * chunk_rows, chunk_rows, width // 2
                )
                for which in (send_half, keep_half)
            )
            parts.append(net.sum_columns(keep, send, "yxz" if chunk % 2 == 0 else "xyz"))
        high_sums[layer] = jnp.concatenate(parts, axis=0)
    sum_high = jnp.stack(high_sums)

    grad_scaled = running * (0.5 / sorted_lengths.astype(F32))[:, None]
    grad_groups = jnp.zeros(char_groups.shape, F32)
    matrix_parts = []
    filter_part = 512
    for start in range(0, features, filter_part):
        part, grad_groups = conv_backward(
            prep, char_groups, half_matrix, grad_scaled, grad_groups, start, filter_part
        )
        matrix_parts.append(part)
    grad_matrix = jnp.concatenate(matrix_parts, axis=1)
    grad_table = table_gradient(prep, grad_groups, character_embedding_table.shape[0])
    sum_conv, sum_conv_bias, sum_high_bias = scatter_vectors(
        [
            jnp.where(usable, grad_matrix, 0.0)[:conv_rows],
            grad_matrix[conv_rows],
            jnp.stack(bias_sums),
        ],
        devices,
    )
    sum_table = lax.psum(grad_table, ("narrow", "wide"))
    return (
        hidden_out[None],
        sum_table,
        sum_conv,
        sum_conv_bias,
        sum_high,
        sum_high_bias,
        sum_proj,
        sum_proj_bias,
        sum_pos,
        sum_type,
        sum_embed_gain,
        sum_embed_shift,
        sum_qkv.T,
        sum_attn_bias,
        sum_out,
        sum_out_bias,
        sum_attn_gain,
        sum_attn_shift,
        sum_up.T,
        sum_up_bias,
        sum_down,
        sum_down_bias,
        sum_ffn_gain,
        sum_ffn_shift,
    )


def solution(mesh):
    narrow, wide = mesh.shape["narrow"], mesh.shape["wide"]
    both = ("narrow", "wide")
    placed = (
        P(both, None, None),
        P(both, None),
        P(both, None),
        P(both, None, None),
        P(),
        P(None, "wide"),
        P("wide"),
        P(None, None, "wide"),
        P(None, "wide"),
        P("wide", None),
        P("wide"),
        P(None, "wide"),
        P(None, "wide"),
        P("wide"),
        P("wide"),
        P(None, "wide"),
        P("wide"),
        P("wide", None),
        P("wide"),
        P("wide"),
        P("wide"),
        P(None, "wide"),
        P("wide"),
        P("wide", None),
        P("wide"),
        P("wide"),
        P("wide"),
    )
    return jax.shard_map(
        partial(body, (narrow, wide) == (2, 16), wide, narrow * wide),
        mesh=mesh,
        in_specs=placed,
        out_specs=(
            P(both, None, None),
            P(),
            P(None, both),
            P(both),
            P(None, None, both),
            P(None, both),
            P(both, None),
            P(both),
            P(None, both),
            P(None, both),
            P(both),
            P(both),
            P(None, both),
            P(both),
            P(both, None),
            P(both),
            P(both),
            P(both),
            P(None, both),
            P(both),
            P(both, None),
            P(both),
            P(both),
            P(both),
        ),
        check_vma=False,
    )
```

time: 5270 us -> 1320 us (0.25)
  waiting for transfers between devices: 2430 us -> 512 us
  matrix products: 983 us -> 73.3 us
  local copies, waits for them, and re-layouts: 953 us -> 133 us
  blocking collectives: 490 us -> 92.6 us
  Pallas kernels: 0 us -> 252 us
  other arithmetic: 368 us -> 127 us
  starting transfers between devices: 0.64 us -> 97.5 us
    reduce_scatter x7 -> x0, waiting for transfers between devices: 2170 us -> none  [the longest x1 1400 us: body(): lax.psum_scatter(grad_high_weight, ('narrow', 'wide'), scatter_dimension=...]
    dot_general x55 -> x17, matrix products: 983 us -> 73.3 us  [the longest x5 39.1 us: dot_nt(): lax.dot_general(left, right, (((1,), (1,)), ((), ())), preferred_element_...]
    ppermute x0 -> x142, waiting for transfers between devices: none -> 396 us  [the longest x102 396 us: along(): return lax.ppermute(value, 'wide', pairs)]
    reshape x8 -> x16, local copies, waits for them, and re-layouts: 379 us -> 17.5 us  [the longest x10 10.6 us: scatter_vectors(): part.reshape(part.shape[:-1] + (devices, -1))]
    all_gather x5 -> x2, blocking collectives: 365 us -> 92.6 us  [the longest x1 51 us: body(): lax.all_gather(jnp.pad(jnp.concatenate([conv_weight, conv_bias[None]], ax...]
    mul x8 -> x0, local copies, waits for them, and re-layouts: 268 us -> none  [convolution_pullback(): (pooling_gradient / block_size_entry[:, None].astype(jnp.float32))[:, Non...]
    pallas_call x0 -> x34, Pallas kernels: none -> 252 us  [the longest x16 51.7 us: highway_weight_gradient(): pl.pallas_call(weight_kernel, grid_spec=pltpu.PrefetchScalarGridSpec(num_...]
    reduce_sum x15 -> x10, other arithmetic: 156 us -> 8.54 us  [the longest x3 4.21 us: column_sum(): return jnp.sum(values.astype(F32), axis=0)]
  transfers between devices with their start and end apart: 16 -> 144, of which waited for: 11 -> 59; matrix products, arithmetic and copies ran while one was open for 13% -> 16% of each run, Pallas kernels for 0% -> 12%
where the time goes in v1:
time: 1320 us; the launch traced here: 1300 us
  waiting for transfers between devices  512 us (39%)
  Pallas kernels  252 us (19%)
  local copies, waits for them, and re-layouts  133 us (10%)
  other arithmetic  127 us (10%)
  starting transfers between devices  97.5 us (7%)
  blocking collectives  92.6 us (7%)
  matrix products  73.3 us (6%)
  between operations  18.5 us (1%)
    ppermute x102, waiting for transfers between devices, along(): return lax.ppermute(value, 'wide', pairs)  396 us
    unnamed x3, waiting for transfers between devices  116 us
    ppermute x102, starting transfers between devices, along(): return lax.ppermute(value, 'wide', pairs)  88.8 us
    unnamed x499, local copies, waits for them, and re-layouts  77.5 us
    pallas_call x16, Pallas kernels, highway_weight_gradient(): pl.pallas_call(weight_kernel, grid_spec=pltpu.PrefetchScalarGridSpec(num_...  51.7 us
    all_gather x1, blocking collectives, body(): lax.all_gather(jnp.pad(jnp.concatenate([conv_weight, conv_bias[None]], ax...  51 us
    pallas_call x2, Pallas kernels, highway_backward(): pl.pallas_call(partial(highway_backward_kernel, layout), grid_spec=pltpu....  47.9 us
    pallas_call x2, Pallas kernels, highway_forward(): pl.pallas_call(partial(highway_forward_kernel, layout), grid_spec=pltpu.P...  43.9 us
  transfers between devices with their start and end apart: 144, of which 59 were waited for; matrix products, arithmetic and copies ran while one was open for 16% of the time, Pallas kernels for 12%

profile of v1, /device:TPU:0, one launch (start us, length us, event | category | flops | bytes accessed | tf_op | source)
XLA Modules:
  0.0 1304.9 jit_solution(8148986120548701385)
XLA Ops:
  21.4 51.0 %all-gather = bf16[2048,128]{1,0:T(8,128)(2,1)S(1)} all-gather(bf16[128,128]{1,0:T(8,128)(2,1)S(1)} %fusion.140), channel_id=2, replica_groups=mesh['narrow'=2,'wide'=16] {'wide'}, dimensions={0}, use_global_device_ids=true | all-gather | bytes 557056 | tf_op jit(solution)/shard_map/all_gather | solution.py:881
  85.0 41.6 %all-gather.1 = bf16[32768]{0:T(1024)(128)(2,1)S(1)} all-gather(bf16[2048]{0:T(1024)(128)(2,1)S(1)} %pad.59), channel_id=3, replica_groups=mesh['narrow'=2,'wide'=16] {'wide'}, dimensions={0}, use_global_device_ids=true | all-gather | bytes 69632 | tf_op jit(solution)/shard_map/all_gather | solution.py:607
  136.1 21.6 %collective-permute-done.52 = bf16[96,768]{1,0:T(8,128)(2,1)S(1)} collective-permute-done((bf16[96,768]{1,0:T(8,128)(2,1)}, bf16[96,768]{1,0:T(8,128)(2,1)S(1)}, u32[]{:S(2)}, u32[]{:S(2)}) %collective-permute-start.52) | collective-permute-done | bytes 147488 | tf_op jit(solution)/shard_map/ppermute | solution.py:521
  224.1 9.9 collective-permute-done.3
  240.7 16.7 %collective-permute-done.4 = bf16[4,512,256]{2,1,0:T(8,128)(2,1)S(1)} collective-permute-done((bf16[4,512,256]{2,1,0:T(8,128)(2,1)}, bf16[4,512,256]{2,1,0:T(8,128)(2,1)S(1)}, u32[]{:S(2)}, u32[]{:S(2)}) %collective-permute-start.4) | collective-permute-done | bytes 1048608 | tf_op jit(solution)/shard_map/ppermute | solution.py:521
  266.4 12.7 collective-permute-done.23
  279.1 24.0 %collective-permute-done.30 = bf16[4,512,256]{2,1,0:T(8,128)(2,1)} collective-permute-done((bf16[4,512,256]{2,1,0:T(8,128)(2,1)}, bf16[4,512,256]{2,1,0:T(8,128)(2,1)}, u32[]{:S(2)}, u32[]{:S(2)}) %collective-permute-start.30) | collective-permute-done | bytes 1048608 | tf_op jit(solution)/shard_map/ppermute | solution.py:521
  313.0 10.5 collective-permute-done.5
  332.4 16.9 %collective-permute-done.25 = bf16[4,512,256]{2,1,0:T(8,128)(2,1)S(1)} collective-permute-done((bf16[4,512,256]{2,1,0:T(8,128)(2,1)}, bf16[4,512,256]{2,1,0:T(8,128)(2,1)S(1)}, u32[]{:S(2)}, u32[]{:S(2)}) %collective-permute-start.25) | collective-permute-done | bytes 1048608 | tf_op jit(solution)/shard_map/ppermute | solution.py:521
  363.6 15.4 %conv_forward.1 = (f32[512,2048]{1,0:T(8,128)S(1)}, bf16[8,512,128]{2,1,0:T(8,128)(2,1)S(1)}) custom-call(s32[8]{0:T(128)S(1)} %pad_add_fusion.scalar_ref, s32[816]{0:T(1024)S(1)} %get-tuple-element.276.tile_ref, s32[816]{0:T(1024)S(1)} %get-tuple-element.275.pos_ref, s32[512,64]{1,0:T(8,128)S(1)} %pad.48.clone.ids_ref, bf16[8,384,128]{2,1,0:T(8,128)(2,1)S(1)} %copy-done.55, ...), custom_call_target="tpu_custom_call" | custom-call | tf_op jit(solution)/shard_map/conv_forward/pallas_call | solution.py:156
  410.9 22.5 %highway_forward.2 = (f32[512,2048]{1,0:T(8,128)}, f32[512,2048]{1,0:T(8,128)}, f32[512,2048]{1,0:T(8,128)}, bf16[512,2048]{1,0:T(8,128)(2,1)}) custom-call(s32[8]{0:T(128)} %get-tuple-element.274.place_ref, s32[8]{0:T(128)} %get-tuple-element.273.select_ref, s32[1]{0:T(128)} %bitcast.1.core_ref.which_ref, f32[512,2048]{1,0:T(8,128)} %copy-done.10, ...), custom_call_target="tpu_custom_call" | custom-call | tf_op jit(solution)/shard_map/highway_forward/pallas_call | solution.py:332
  437.5 21.4 %highway_forward.3 = (f32[512,2048]{1,0:T(8,128)}, f32[512,2048]{1,0:T(8,128)}, f32[512,2048]{1,0:T(8,128)}, bf16[512,2048]{1,0:T(8,128)(2,1)}) custom-call(s32[8]{0:T(128)} %get-tuple-element.274.place_ref, s32[8]{0:T(128)} %get-tuple-element.273.select_ref, s32[1]{0:T(128)} %bitcast.1.core_ref.which_ref, f32[512,2048]{1,0:T(8,128)} %get-tuple-element.58.h_ref, ...), custom_call_target="tpu_custom_call" | custom-call | tf_op jit(solution)/shard_map/highway_forward/pallas_call | solution.py:332
  468.4 11.3 attend.1
  485.9 10.3 place_rows.5
  496.3 19.4 %multiply_convert_fusion = (bf16[512,3072]{1,0:T(8,128)(2,1)S(1)}, f32[512,3072]{1,0:T(8,128)}, f32[512,3072]{1,0:T(8,128)}) fusion(f32[3072]{0:T(1024)S(1)} %reshape.1470, bf16[3072,768]{1,0:T(8,128)(2,1)S(1)} %get-tuple-element.64, f32[512,768]{1,0:T(8,128)S(1)} %get-tuple-element.265, f32[768]{0:T(1024)S(1)} %reshape.1469, f32[768]{0:T(1024)S(1)} %reshape.1468, ...), kind=kOutput, calls=%fused_computation.8 | convolution fusion | flops 2521694208 | bytes 22042624 | tf_op jit(solution)/shard_map/dot_general | solution.py:37
  524.1 10.1 convert_reduce_fusion
  542.4 16.8 %attend_back.1 = (bf16[512,768]{1,0:T(8,128)(2,1)S(1)}, bf16[512,768]{1,0:T(8,128)(2,1)S(1)}, bf16[512,768]{1,0:T(8,128)(2,1)S(1)}) custom-call(bf16[512,2304]{1,0:T(8,128)(2,1)S(1)} %fusion.9.query_ref.key_ref.value_ref, bf16[512,2304]{1,0:T(8,128)(2,1)S(1)} %fusion.9.query_ref.key_ref.value_ref, bf16[512,2304]{1,0:T(8,128)(2,1)S(1)} %fusion.9.query_ref.key_ref.value_ref, ...), custom_call_target="tpu_custom_call" | custom-call | tf_op jit(solution)/shard_map/attend_back/pallas_call | solution.py:795
  578.1 23.8 %highway_backward.2 = (bf16[2,512,2048]{2,1,0:T(8,128)(2,1)}, f32[2,1,2048]{2,1,0:T(1,128)}, f32[512,2048]{1,0:T(8,128)}) custom-call(s32[8]{0:T(128)} %get-tuple-element.274.place_ref, s32[8]{0:T(128)} %get-tuple-element.273.select_ref, s32[1]{0:T(128)} %bitcast.1.core_ref.which_ref, f32[512,2048]{1,0:T(8,128)} %fusion.50.grad_ref, ...), custom_call_target="tpu_custom_call" | custom-call | tf_op jit(solution)/shard_map/highway_backward/pallas_call | solution.py:398
  601.9 24.1 %highway_backward.3 = (bf16[2,512,2048]{2,1,0:T(8,128)(2,1)}, f32[2,1,2048]{2,1,0:T(1,128)}, f32[512,2048]{1,0:T(8,128)}) custom-call(s32[8]{0:T(128)} %get-tuple-element.274.place_ref, s32[8]{0:T(128)} %get-tuple-element.273.select_ref, s32[1]{0:T(128)} %bitcast.1.core_ref.which_ref, f32[512,2048]{1,0:T(8,128)} %get-tuple-element.72.grad_ref, ...), custom_call_target="tpu_custom_call" | custom-call | tf_op jit(solution)/shard_map/highway_backward/pallas_call | solution.py:398
  652.6 9.8 conv_backward.4
  662.5 9.9 conv_backward.5
  672.4 9.9 conv_backward.6
  682.3 10.1 conv_backward.7
  752.1 15.4 %collective-permute-done.119 = bf16[4,2,64,768]{3,2,1,0:T(8,128)(2,1)S(1)} collective-permute-done((bf16[4,2,64,768]{3,2,1,0:T(8,128)(2,1)S(1)}, bf16[4,2,64,768]{3,2,1,0:T(8,128)(2,1)S(1)}, u32[]{:S(2)}, u32[]{:S(2)}) %collective-permute-start.119) | collective-permute-done | bytes 786464 | tf_op jit(solution)/shard_map/ppermute | solution.py:521
  883.1 115.7 %all-reduce.18.cloned.1.call-done = f32[32,7488]{1,0:T(8,128)} async-done(((f32[32,7488]{1,0:T(8,128)}), f32[32,7488]{1,0:T(8,128)}) %all-reduce.18.cloned.1.call-update) | async-done | bytes 958480
  1024.6 11.2 collective-permute-done.101
  1041.2 17.0 %collective-permute-done.113 = bf16[4,2,512,128]{3,2,1,0:T(8,128)(2,1)S(1)} collective-permute-done((bf16[4,2,512,128]{3,2,1,0:T(8,128)(2,1)S(1)}, bf16[4,2,512,128]{3,2,1,0:T(8,128)(2,1)S(1)}, u32[]{:S(2)}, u32[]{:S(2)}) %collective-permute-start.113) | collective-permute-done | bytes 1048608 | tf_op jit(solution)/shard_map/ppermute | solution.py:521
  1059.9 23.6 %collective-permute-done.131 = bf16[4,2,96,768]{3,2,1,0:T(8,128)(2,1)S(1)} collective-permute-done((bf16[4,2,96,768]{3,2,1,0:T(8,128)(2,1)S(1)}, bf16[4,2,96,768]{3,2,1,0:T(8,128)(2,1)S(1)}, u32[]{:S(2)}, u32[]{:S(2)}) %collective-permute-start.131) | collective-permute-done | bytes 1179680 | tf_op jit(solution)/shard_map/ppermute | solution.py:521
  1085.4 9.4 collective-permute-done.72
  1172.2 25.6 %collective-permute-done.110 = bf16[512,128]{1,0:T(8,128)(2,1)S(1)} collective-permute-done((bf16[512,128]{1,0:T(8,128)(2,1)S(1)}, bf16[512,128]{1,0:T(8,128)(2,1)S(1)}, u32[]{:S(2)}, u32[]{:S(2)}) %collective-permute-start.110) | collective-permute-done | bytes 131104 | tf_op jit(solution)/shard_map/ppermute | solution.py:521
  1213.2 24.1 %collective-permute-done.138 = bf16[2,2,192,768]{3,2,1,0:T(8,128)(2,1)S(1)} collective-permute-done((bf16[2,2,192,768]{3,2,1,0:T(8,128)(2,1)S(1)}, bf16[2,2,192,768]{3,2,1,0:T(8,128)(2,1)S(1)}, u32[]{:S(2)}, u32[]{:S(2)}) %collective-permute-start.138) | collective-permute-done | bytes 1179680 | tf_op jit(solution)/shard_map/ppermute | solution.py:521
  1248.6 26.4 %collective-permute-done.133 = bf16[96,768]{1,0:T(8,128)(2,1)S(1)} collective-permute-done((bf16[96,768]{1,0:T(8,128)(2,1)S(1)}, bf16[96,768]{1,0:T(8,128)(2,1)S(1)}, u32[]{:S(2)}, u32[]{:S(2)}) %collective-permute-start.133) | collective-permute-done | bytes 147488 | tf_op jit(solution)/shard_map/ppermute | solution.py:521
  (1036 shorter events, 598.1 us)
Async XLA Ops:
  7.2 869.4 %all-reduce.20.cloned.1.call-start = ((), (), s32[]{:S(2)}) async-start(), calls=%async_computation.1 | async-start | bytes 401408 | tf_op jit(solution)/shard_map/psum | solution.py:1066
  9.3 74.9 %collective-permute-start = (bf16[512,256]{1,0:T(8,128)(2,1)S(1)}, bf16[512,256]{1,0:T(8,128)(2,1)}, u32[]{:S(2)}, u32[]{:S(2)}) collective-permute-start(bf16[512,256]{1,0:T(8,128)(2,1)S(1)} %bitcast.839), channel_id=1, source_target_pairs={{0,4},{1,5},{2,6},{3,7},{4,8},{5,9},{6,10},{7,11},{8,12},{9,13},{1... | collective-permute-start | bytes 786440 | tf_op jit(solution)/shard_map/ppermute | solution.py:521
  12.4 72.0 %collective-permute-start.6 = (bf16[512,256]{1,0:T(8,128)(2,1)S(1)}, bf16[512,256]{1,0:T(8,128)(2,1)S(1)}, u32[]{:S(2)}, u32[]{:S(2)}) collective-permute-start(bf16[512,256]{1,0:T(8,128)(2,1)S(1)} %bitcast.838), channel_id=1, source_target_pairs={{0,4},{1,5},{2,6},{3,7},{4,8},{5,9},{6,10},{7,11},{8,12},{9,13},{1... | collective-permute-start | bytes 786440 | tf_op jit(solution)/shard_map/ppermute | solution.py:521
  13.9 112.8 %collective-permute-start.20 = (bf16[512,256]{1,0:T(8,128)(2,1)S(1)}, bf16[512,256]{1,0:T(8,128)(2,1)S(1)}, u32[]{:S(2)}, u32[]{:S(2)}) collective-permute-start(bf16[512,256]{1,0:T(8,128)(2,1)S(1)} %bitcast.837), channel_id=1, source_target_pairs={{0,4},{1,5},{2,6},{3,7},{4,8},{5,9},{6,10},{7,11},{8,12},{9,13},{1... | collective-permute-start | bytes 786440 | tf_op jit(solution)/shard_map/ppermute | solution.py:521
  17.3 59.2 %collective-permute-start.40 = (bf16[80,768]{1,0:T(8,128)(2,1)S(1)}, bf16[80,768]{1,0:T(8,128)(2,1)S(1)}, u32[]{:S(2)}, u32[]{:S(2)}) collective-permute-start(bf16[80,768]{1,0:T(8,128)(2,1)S(1)} %fusion.125), channel_id=1, source_target_pairs={{0,4},{1,5},{2,6},{3,7},{4,8},{5,9},{6,10},{7,11},{8,12},{9,13},{1... | collective-permute-start | bytes 368648 | tf_op jit(solution)/shard_map/ppermute | solution.py:521
  18.4 58.1 %collective-permute-start.50 = (bf16[96,768]{1,0:T(8,128)(2,1)S(1)}, bf16[96,768]{1,0:T(8,128)(2,1)}, u32[]{:S(2)}, u32[]{:S(2)}) collective-permute-start(bf16[96,768]{1,0:T(8,128)(2,1)S(1)} %fusion.123), channel_id=1, source_target_pairs={{0,4},{1,5},{2,6},{3,7},{4,8},{5,9},{6,10},{7,11},{8,12},{9,13},{1... | collective-permute-start | bytes 442376 | tf_op jit(solution)/shard_map/ppermute | solution.py:521
  76.5 50.3 %collective-permute-start.26 = (bf16[512,256]{1,0:T(8,128)(2,1)S(1)}, bf16[512,256]{1,0:T(8,128)(2,1)}, u32[]{:S(2)}, u32[]{:S(2)}) collective-permute-start(bf16[512,256]{1,0:T(8,128)(2,1)S(1)} %bitcast.836), channel_id=1, source_target_pairs={{0,4},{1,5},{2,6},{3,7},{4,8},{5,9},{6,10},{7,11},{8,12},{9,13},{1... | collective-permute-start | bytes 786440 | tf_op jit(solution)/shard_map/ppermute | solution.py:521
  356.2 78.4 %collective-permute-start.64 = (bf16[4,192,768]{2,1,0:T(8,128)(2,1)}, bf16[4,192,768]{2,1,0:T(8,128)(2,1)}, u32[]{:S(2)}, u32[]{:S(2)}) collective-permute-start(bf16[4,192,768]{2,1,0:T(8,128)(2,1)} %collective-permute-done.63.refs_1_), channel_id=1, source_target_pairs={{0,4},{1,5},{2,6},{3,7},{4,8},{5,9},{6,10},{7,11},{8,12},{9,13},{1... | collective-permute-start | bytes 3538952 | tf_op jit(solution)/shard_map/ppermute | solution.py:521
  358.0 75.5 %collective-permute-start.34 = (bf16[2,2,512,256]{3,2,1,0:T(8,128)(2,1)}, bf16[2,2,512,256]{3,2,1,0:T(8,128)(2,1)}, u32[]{:S(2)}, u32[]{:S(2)}) collective-permute-start(bf16[2,2,512,256]{3,2,1,0:T(8,128)(2,1)} %bitcast.42.refs_2_), channel_id=1, source_target_pairs={{0,16},{16,0},{1,17},{17,1},{2,18},{18,2},{3,19},{19,3},{4,20},{20... | collective-permute-start | bytes 3145736 | tf_op jit(solution)/shard_map/ppermute | solution.py:517
  358.0 76.6 %collective-permute-start.37 = (bf16[2,2,512,256]{3,2,1,0:T(8,128)(2,1)}, bf16[2,2,512,256]{3,2,1,0:T(8,128)(2,1)}, u32[]{:S(2)}, u32[]{:S(2)}) collective-permute-start(bf16[2,2,512,256]{3,2,1,0:T(8,128)(2,1)} %bitcast.800), channel_id=1, source_target_pairs={{0,16},{16,0},{1,17},{17,1},{2,18},{18,2},{3,19},{19,3},{4,20},{20... | collective-permute-start | bytes 3145736 | tf_op jit(solution)/shard_map/ppermute | solution.py:517
  358.5 79.0 %collective-permute-start.35 = (bf16[2,2,512,256]{3,2,1,0:T(8,128)(2,1)}, bf16[2,2,512,256]{3,2,1,0:T(8,128)(2,1)}, u32[]{:S(2)}, u32[]{:S(2)}) collective-permute-start(bf16[2,2,512,256]{3,2,1,0:T(8,128)(2,1)} %bitcast.803), channel_id=1, source_target_pairs={{0,16},{16,0},{1,17},{17,1},{2,18},{18,2},{3,19},{19,3},{4,20},{20... | collective-permute-start | bytes 3145736 | tf_op jit(solution)/shard_map/ppermute | solution.py:517
  358.6 78.9 %collective-permute-start.39 = (bf16[2,2,512,256]{3,2,1,0:T(8,128)(2,1)}, bf16[2,2,512,256]{3,2,1,0:T(8,128)(2,1)}, u32[]{:S(2)}, u32[]{:S(2)}) collective-permute-start(bf16[2,2,512,256]{3,2,1,0:T(8,128)(2,1)} %bitcast.806), channel_id=1, source_target_pairs={{0,16},{16,0},{1,17},{17,1},{2,18},{18,2},{3,19},{19,3},{4,20},{20... | collective-permute-start | bytes 3145736 | tf_op jit(solution)/shard_map/ppermute | solution.py:517
  433.5 50.9 %collective-permute-start.66 = (bf16[4,192,768]{2,1,0:T(8,128)(2,1)S(1)}, bf16[4,192,768]{2,1,0:T(8,128)(2,1)}, u32[]{:S(2)}, u32[]{:S(2)}) collective-permute-start(bf16[4,192,768]{2,1,0:T(8,128)(2,1)S(1)} %copy-done.36), channel_id=1, source_target_pairs={{0,16},{16,0},{1,17},{17,1},{2,18},{18,2},{3,19},{19,3},{4,20},{20... | collective-permute-start | bytes 3538952 | tf_op jit(solution)/shard_map/ppermute | solution.py:517
  647.4 57.4 %collective-permute-start.124 = (bf16[16,24,512]{2,1,0:T(8,128)(2,1)}, bf16[16,24,512]{2,1,0:T(8,128)(2,1)}, u32[]{:S(2)}, u32[]{:S(2)}) collective-permute-start(bf16[16,24,512]{2,1,0:T(8,128)(2,1)} %get-tuple-element.226), channel_id=1, source_target_pairs={{0,16},{16,0},{1,17},{17,1},{2,18},{18,2},{3,19},{19,3},{4,20},{20... | collective-permute-start | bytes 1179656 | tf_op jit(solution)/shard_map/ppermute | solution.py:517
  649.9 91.3 %collective-permute-start.118 = (bf16[16,64,768]{2,1,0:T(8,128)(2,1)}, bf16[16,64,768]{2,1,0:T(8,128)(2,1)}, u32[]{:S(2)}, u32[]{:S(2)}) collective-permute-start(bf16[16,64,768]{2,1,0:T(8,128)(2,1)} %get-tuple-element.218), channel_id=1, source_target_pairs={{0,16},{16,0},{1,17},{17,1},{2,18},{18,2},{3,19},{19,3},{4,20},{20... | collective-permute-start | bytes 4718600 | tf_op jit(solution)/shard_map/ppermute | solution.py:517
  649.9 135.7 %collective-permute-start.70 = (bf16[16,512,128]{2,1,0:T(8,128)(2,1)}, bf16[16,512,128]{2,1,0:T(8,128)(2,1)}, u32[]{:S(2)}, u32[]{:S(2)}) collective-permute-start(bf16[16,512,128]{2,1,0:T(8,128)(2,1)} %highway_weight.17), channel_id=1, source_target_pairs={{0,16},{16,0},{1,17},{17,1},{2,18},{18,2},{3,19},{19,3},{4,20},{20... | collective-permute-start | bytes 6291464 | tf_op jit(solution)/shard_map/ppermute | solution.py:517
  650.4 142.4 %collective-permute-start.76 = (bf16[16,512,128]{2,1,0:T(8,128)(2,1)}, bf16[16,512,128]{2,1,0:T(8,128)(2,1)}, u32[]{:S(2)}, u32[]{:S(2)}) collective-permute-start(bf16[16,512,128]{2,1,0:T(8,128)(2,1)} %highway_weight.19), channel_id=1, source_target_pairs={{0,16},{16,0},{1,17},{17,1},{2,18},{18,2},{3,19},{19,3},{4,20},{20... | collective-permute-start | bytes 6291464 | tf_op jit(solution)/shard_map/ppermute | solution.py:517
  650.4 180.5 %collective-permute-start.82 = (bf16[16,512,128]{2,1,0:T(8,128)(2,1)}, bf16[16,512,128]{2,1,0:T(8,128)(2,1)}, u32[]{:S(2)}, u32[]{:S(2)}) collective-permute-start(bf16[16,512,128]{2,1,0:T(8,128)(2,1)} %highway_weight.21), channel_id=1, source_target_pairs={{0,16},{16,0},{1,17},{17,1},{2,18},{18,2},{3,19},{19,3},{4,20},{20... | collective-permute-start | bytes 6291464 | tf_op jit(solution)/shard_map/ppermute | solution.py:517
  740.1 258.8 %all-reduce.18.cloned.1.call-start = ((), (), s32[]{:S(2)}) async-start(), calls=%async_computation | async-start | bytes 1933312
  740.1 91.4 %collective-permute-start.88 = (bf16[16,512,128]{2,1,0:T(8,128)(2,1)}, bf16[16,512,128]{2,1,0:T(8,128)(2,1)}, u32[]{:S(2)}, u32[]{:S(2)}) collective-permute-start(bf16[16,512,128]{2,1,0:T(8,128)(2,1)} %copy-done.48), channel_id=1, source_target_pairs={{0,16},{16,0},{1,17},{17,1},{2,18},{18,2},{3,19},{19,3},{4,20},{20... | collective-permute-start | bytes 6291464 | tf_op jit(solution)/shard_map/ppermute | solution.py:517
  785.7 72.3 %collective-permute-start.130 = (bf16[16,96,768]{2,1,0:T(8,128)(2,1)}, bf16[16,96,768]{2,1,0:T(8,128)(2,1)}, u32[]{:S(2)}, u32[]{:S(2)}) collective-permute-start(bf16[16,96,768]{2,1,0:T(8,128)(2,1)} %get-tuple-element.216), channel_id=1, source_target_pairs={{0,16},{16,0},{1,17},{17,1},{2,18},{18,2},{3,19},{19,3},{4,20},{20... | collective-permute-start | bytes 7077896 | tf_op jit(solution)/shard_map/ppermute | solution.py:517
  791.2 60.2 %collective-permute-start.94 = (bf16[16,512,128]{2,1,0:T(8,128)(2,1)}, bf16[16,512,128]{2,1,0:T(8,128)(2,1)}, u32[]{:S(2)}, u32[]{:S(2)}) collective-permute-start(bf16[16,512,128]{2,1,0:T(8,128)(2,1)} %highway_weight.25), channel_id=1, source_target_pairs={{0,16},{16,0},{1,17},{17,1},{2,18},{18,2},{3,19},{19,3},{4,20},{20... | collective-permute-start | bytes 6291464 | tf_op jit(solution)/shard_map/ppermute | solution.py:517
  854.2 155.5 %collective-permute-start.71 = (bf16[4,2,512,128]{3,2,1,0:T(8,128)(2,1)}, bf16[4,2,512,128]{3,2,1,0:T(8,128)(2,1)}, u32[]{:S(2)}, u32[]{:S(2)}) collective-permute-start(bf16[4,2,512,128]{3,2,1,0:T(8,128)(2,1)} %fusion.32), channel_id=1, source_target_pairs={{0,2},{1,3},{2,0},{3,1},{4,6},{5,7},{6,4},{7,5},{8,10},{9,11},{10,... | collective-permute-start | bytes 3145736 | tf_op jit(solution)/shard_map/ppermute | solution.py:521
  854.7 156.8 %collective-permute-start.77 = (bf16[4,2,512,128]{3,2,1,0:T(8,128)(2,1)}, bf16[4,2,512,128]{3,2,1,0:T(8,128)(2,1)}, u32[]{:S(2)}, u32[]{:S(2)}) collective-permute-start(bf16[4,2,512,128]{3,2,1,0:T(8,128)(2,1)} %fusion.33), channel_id=1, source_target_pairs={{0,1},{1,0},{2,3},{3,2},{4,5},{5,4},{6,7},{7,6},{8,9},{9,8},{10,11... | collective-permute-start | bytes 3145736 | tf_op jit(solution)/shard_map/ppermute | solution.py:521
  856.4 158.0 %collective-permute-start.83 = (bf16[4,2,512,128]{3,2,1,0:T(8,128)(2,1)}, bf16[4,2,512,128]{3,2,1,0:T(8,128)(2,1)}, u32[]{:S(2)}, u32[]{:S(2)}) collective-permute-start(bf16[4,2,512,128]{3,2,1,0:T(8,128)(2,1)} %fusion.34), channel_id=1, source_target_pairs={{0,2},{1,3},{2,0},{3,1},{4,6},{5,7},{6,4},{7,5},{8,10},{9,11},{10,... | collective-permute-start | bytes 3145736 | tf_op jit(solution)/shard_map/ppermute | solution.py:521
  858.0 156.6 %collective-permute-start.89 = (bf16[4,2,512,128]{3,2,1,0:T(8,128)(2,1)S(1)}, bf16[4,2,512,128]{3,2,1,0:T(8,128)(2,1)}, u32[]{:S(2)}, u32[]{:S(2)}) collective-permute-start(bf16[4,2,512,128]{3,2,1,0:T(8,128)(2,1)S(1)} %fusion.35), channel_id=1, source_target_pairs={{0,1},{1,0},{2,3},{3,2},{4,5},{5,4},{6,7},{7,6},{8,9},{9,8},{10,11... | collective-permute-start | bytes 3145736 | tf_op jit(solution)/shard_map/ppermute | solution.py:521
  858.9 156.7 %collective-permute-start.95 = (bf16[4,2,512,128]{3,2,1,0:T(8,128)(2,1)}, bf16[4,2,512,128]{3,2,1,0:T(8,128)(2,1)}, u32[]{:S(2)}, u32[]{:S(2)}) collective-permute-start(bf16[4,2,512,128]{3,2,1,0:T(8,128)(2,1)} %fusion.36), channel_id=1, source_target_pairs={{0,2},{1,3},{2,0},{3,1},{4,6},{5,7},{6,4},{7,5},{8,10},{9,11},{10,... | collective-permute-start | bytes 3145736 | tf_op jit(solution)/shard_map/ppermute | solution.py:521
  1014.4 145.7 %collective-permute-start.136 = (bf16[16,192,768]{2,1,0:T(8,128)(2,1)}, bf16[16,192,768]{2,1,0:T(8,128)(2,1)S(1)}, u32[]{:S(2)}, u32[]{:S(2)}) collective-permute-start(bf16[16,192,768]{2,1,0:T(8,128)(2,1)} %get-tuple-element.214), channel_id=1, source_target_pairs={{0,16},{16,0},{1,17},{17,1},{2,18},{18,2},{3,19},{19,3},{4,20},{20... | collective-permute-start | bytes 14155784 | tf_op jit(solution)/shard_map/ppermute | solution.py:517
  1015.5 68.0 %collective-permute-start.131 = (bf16[4,2,96,768]{3,2,1,0:T(8,128)(2,1)S(1)}, bf16[4,2,96,768]{3,2,1,0:T(8,128)(2,1)S(1)}, u32[]{:S(2)}, u32[]{:S(2)}) collective-permute-start(bf16[4,2,96,768]{3,2,1,0:T(8,128)(2,1)S(1)} %fusion.28), channel_id=1, source_target_pairs={{0,1},{1,0},{2,3},{3,2},{4,5},{5,4},{6,7},{7,6},{8,9},{9,8},{10,11... | collective-permute-start | bytes 3538952 | tf_op jit(solution)/shard_map/ppermute | solution.py:521
  1035.8 59.0 %collective-permute-start.72 = (bf16[4,512,128]{2,1,0:T(8,128)(2,1)S(1)}, bf16[4,512,128]{2,1,0:T(8,128)(2,1)S(1)}, u32[]{:S(2)}, u32[]{:S(2)}) collective-permute-start(bf16[4,512,128]{2,1,0:T(8,128)(2,1)S(1)} %fusion.47), channel_id=1, source_target_pairs={{0,1},{1,0},{2,3},{3,2},{4,5},{5,4},{6,7},{7,6},{8,9},{9,8},{10,11... | collective-permute-start | bytes 1572872 | tf_op jit(solution)/shard_map/ppermute | solution.py:521
  1038.6 59.0 %collective-permute-start.78 = (bf16[4,512,128]{2,1,0:T(8,128)(2,1)S(1)}, bf16[4,512,128]{2,1,0:T(8,128)(2,1)S(1)}, u32[]{:S(2)}, u32[]{:S(2)}) collective-permute-start(bf16[4,512,128]{2,1,0:T(8,128)(2,1)S(1)} %fusion.46), channel_id=1, source_target_pairs={{0,2},{1,3},{2,0},{3,1},{4,6},{5,7},{6,4},{7,5},{8,10},{9,11},{10,... | collective-permute-start | bytes 1572872 | tf_op jit(solution)/shard_map/ppermute | solution.py:521
  1117.2 128.5 %collective-permute-start.132 = (bf16[4,96,768]{2,1,0:T(8,128)(2,1)S(1)}, bf16[4,96,768]{2,1,0:T(8,128)(2,1)S(1)}, u32[]{:S(2)}, u32[]{:S(2)}) collective-permute-start(bf16[4,96,768]{2,1,0:T(8,128)(2,1)S(1)} %fusion.31), channel_id=1, source_target_pairs={{0,2},{1,3},{2,0},{3,1},{4,6},{5,7},{6,4},{7,5},{8,10},{9,11},{10,... | collective-permute-start | bytes 1769480 | tf_op jit(solution)/shard_map/ppermute | solution.py:521
  (346 other events, 8809.5 us)
Sparse Core Ops, SparseCore 0:
  740.2 123.6 all-reduce.19
  869.1 129.6 all-reduce.17

commit v2 on v1

v2 whole, which is shorter than its diff:
```python
from functools import partial

import jax
import jax.numpy as jnp
from jax import lax
from jax.experimental import pallas as pl
from jax.experimental.pallas import tpu as pltpu
from jax.sharding import PartitionSpec as P

HEADS = 12
HEAD_DIM = 64
CHAR_DIM = 16
TAPS = 7
EPSILON = 1e-12

LANES = 128
GROUP = LANES // CHAR_DIM
BLOCK_WORDS = 32
CHUNK_BLOCKS = 16
CHUNK = BLOCK_WORDS * CHUNK_BLOCKS
TABLE_PAD = 384
ROW_TILE = 128
BIAS_LANE = TAPS * CHAR_DIM

F32 = jnp.float32
BF16 = jnp.bfloat16
VMEM = pl.BlockSpec(memory_space=pltpu.VMEM)
SMEM = pl.BlockSpec(memory_space=pltpu.SMEM)
MIB = 1024 * 1024


def cost(microseconds):
    return pl.CostEstimate(
        flops=int(microseconds * 1.1e9), bytes_accessed=int(microseconds * 3e6), transcendentals=0
    )


def dot(left, right):
    return lax.dot_general(left, right, (((1,), (0,)), ((), ())), preferred_element_type=F32)


def dot_nt(left, right):
    return lax.dot_general(left, right, (((1,), (1,)), ((), ())), preferred_element_type=F32)


def dot_tn(left, right):
    return lax.dot_general(left, right, (((0,), (0,)), ((), ())), preferred_element_type=F32)


def column_sum(values):
    return jnp.sum(values.astype(F32), axis=0)


def filter_widths(filter_count):
    column = jnp.arange(filter_count)
    widths = jnp.ones((filter_count,), jnp.int32)
    for exponent in range(6):
        widths = widths + (column >= filter_count * 2**exponent // 64).astype(jnp.int32)
    return widths


def sort_words(char_ids, lengths, groups):
    words, chars = char_ids.shape
    index = jnp.arange(words)
    longer = lengths[None, :] > lengths[:, None]
    tie = (lengths[None, :] == lengths[:, None]) & (index[None, :] < index[:, None])
    rank = jnp.sum((longer | tie).astype(jnp.int32), axis=1)
    perm = (rank[None, :] == index[:, None]).astype(BF16)
    live = jnp.arange(chars)[None, :] < lengths[:, None]
    shifted = jnp.where(live, char_ids + 1, 0)
    packed = jnp.concatenate(
        [shifted >> 4, shifted & 15, lengths[:, None]], axis=1
    ).astype(BF16)
    sorted_packed = dot(perm, packed).astype(jnp.int32)
    ids = (sorted_packed[:, :chars] << 4) + sorted_packed[:, chars : 2 * chars] - 1
    ids = jnp.pad(ids, ((0, 0), (0, GROUP * groups - chars)), constant_values=-1)
    sorted_lengths = sorted_packed[:, 2 * chars]
    tile_count = words // BLOCK_WORDS
    tile_max = jnp.max(sorted_lengths.reshape(tile_count, BLOCK_WORDS), axis=1)
    cum = jnp.cumsum(tile_max)
    total = cum[-1]
    block = jnp.arange(tile_count * chars + CHUNK_BLOCKS)
    tile = jnp.sum((block[:, None] >= cum[None, :]).astype(jnp.int32), axis=1)
    start = jnp.sum(
        jnp.where(tile[:, None] == jnp.arange(tile_count)[None, :], (cum - tile_max)[None, :], 0),
        axis=1,
    )
    valid = block < total
    position = jnp.where(valid, block - start, chars).astype(jnp.int32)
    tile = jnp.where(valid, tile, 0).astype(jnp.int32)
    chunks = (total + CHUNK_BLOCKS - 1) // CHUNK_BLOCKS
    reach = jnp.sum(
        (sorted_lengths[None, :] > GROUP * jnp.arange(groups - 1)[:, None]).astype(jnp.int32), axis=1
    )
    scalars = jnp.concatenate([chunks[None], (reach + ROW_TILE - 1) // ROW_TILE]).astype(jnp.int32)
    return perm, ids, sorted_lengths, scalars, tile, position


def build_windows(chunk, tile_ref, pos_ref, g_ref, len_ref, x_ref):
    lane = lax.broadcasted_iota(jnp.int32, (BLOCK_WORDS, LANES), 1)
    for b in range(CHUNK_BLOCKS):
        block = chunk * CHUNK_BLOCKS + b
        row = pl.multiple_of(tile_ref[block] * BLOCK_WORDS, BLOCK_WORDS)
        position = pos_ref[block]
        group = position >> 3
        offset = (position & 7) * CHAR_DIM
        shift = lax.rem(LANES - offset, LANES)
        here = pltpu.roll(g_ref[group, pl.ds(row, BLOCK_WORDS), :].astype(F32), shift, 1)
        after = pltpu.roll(g_ref[group + 1, pl.ds(row, BLOCK_WORDS), :].astype(F32), shift, 1)
        live = (len_ref[pl.ds(row, BLOCK_WORDS), :] > position).astype(F32)
        value = jnp.where(lane < LANES - offset, here, after)
        value = jnp.where(lane < BIAS_LANE, value, jnp.where(lane == BIAS_LANE, live, 0.0))
        x_ref[b * BLOCK_WORDS : (b + 1) * BLOCK_WORDS, :] = value.astype(BF16)


def embed_kernel(scalar_ref, ids_ref, table_ref, g_ref):
    groups = g_ref.shape[0]
    g_ref[...] = jnp.zeros_like(g_ref)
    identity = lax.broadcasted_iota(jnp.int32, (ROW_TILE, TABLE_PAD), 1)
    for group in range(groups - 1):

        def embed(step, carry, group=group):
            row = pl.multiple_of(step * ROW_TILE, ROW_TILE)
            total = jnp.zeros((ROW_TILE, LANES), F32)
            for k in range(GROUP):
                column = group * GROUP + k
                hot = (ids_ref[pl.ds(row, ROW_TILE), column : column + 1] == identity).astype(F32)
                total = total + dot(hot.astype(BF16), table_ref[k])
            g_ref[group, pl.ds(row, ROW_TILE), :] = total.astype(BF16)
            return carry

        lax.fori_loop(0, scalar_ref[1 + group], embed, 0)


def embed_characters(prep, table_blocks):
    _, ids, _, scalars, _, _ = prep
    return pl.pallas_call(
        embed_kernel,
        out_shape=jax.ShapeDtypeStruct((ids.shape[1] // GROUP, ids.shape[0], LANES), BF16),
        in_specs=[SMEM, VMEM, VMEM],
        out_specs=VMEM,
        compiler_params=pltpu.CompilerParams(vmem_limit_bytes=32 * MIB),
        cost_estimate=cost(5),
        name="embed_characters",
    )(scalars, ids, table_blocks)


def conv_forward_kernel(
    scalar_ref, tile_ref, pos_ref, g_ref, w_ref, len_ref, kept_ref, pooled_ref, x_ref, pre_ref
):
    filters = w_ref.shape[1]
    part = pre_ref.shape[1]
    pooled_ref[...] = jnp.zeros_like(pooled_ref)

    def step(chunk, carry):
        build_windows(chunk, tile_ref, pos_ref, g_ref, len_ref, x_ref)
        for first in range(0, filters, part):
            half = dot(x_ref[...], w_ref[:, first : first + part])
            pre_ref[...] = half + half * jnp.tanh(half)
            for b in range(CHUNK_BLOCKS):
                row = pl.multiple_of(
                    tile_ref[chunk * CHUNK_BLOCKS + b] * BLOCK_WORDS, BLOCK_WORDS
                )
                pooled_ref[pl.ds(row, BLOCK_WORDS), first : first + part] += pre_ref[
                    b * BLOCK_WORDS : (b + 1) * BLOCK_WORDS, :
                ]
        return carry

    lax.fori_loop(0, scalar_ref[0], step, 0)
    pooled_ref[...] = pooled_ref[...] / len_ref[...].astype(F32)


def conv_forward(prep, char_groups, half_matrix, pooled, first, part):
    _, ids, lengths, scalars, tile, position = prep
    words = ids.shape[0]
    return pl.pallas_call(
        conv_forward_kernel,
        grid=(1,),
        out_shape=jax.ShapeDtypeStruct((words, half_matrix.shape[1]), F32),
        in_specs=[
            SMEM,
            SMEM,
            SMEM,
            VMEM,
            pl.BlockSpec((LANES, part), lambda i: (0, first // part)),
            VMEM,
            pl.BlockSpec(memory_space=pl.ANY),
        ],
        out_specs=pl.BlockSpec((words, part), lambda i: (0, first // part)),
        scratch_shapes=[pltpu.VMEM((CHUNK, LANES), BF16), pltpu.VMEM((CHUNK, 512), F32)],
        input_output_aliases={6: 0},
        compiler_params=pltpu.CompilerParams(vmem_limit_bytes=32 * MIB),
        cost_estimate=cost(8),
        name="conv_forward",
    )(scalars, tile, position, char_groups, half_matrix, lengths[:, None], pooled)


def conv_backward_kernel(
    scalar_ref, tile_ref, pos_ref, g_ref, w_ref, len_ref, gp_ref, out_ref, gg_ref, x_ref, d_ref, dw_ref
):
    filters = w_ref.shape[1]
    part = 512
    lane = lax.broadcasted_iota(jnp.int32, (BLOCK_WORDS, LANES), 1)
    dw_ref[...] = jnp.zeros_like(dw_ref)
    gg_ref[...] = jnp.zeros_like(gg_ref)

    def step(chunk, carry):
        build_windows(chunk, tile_ref, pos_ref, g_ref, len_ref, x_ref)
        for first in range(0, filters, part):
            columns = slice(first, first + part)
            half = dot(x_ref[...], w_ref[:, columns])
            tanh = jnp.tanh(half)
            slope = (1.0 + tanh) * (1.0 + (half - half * tanh))
            for b in range(CHUNK_BLOCKS):
                rows = slice(b * BLOCK_WORDS, (b + 1) * BLOCK_WORDS)
                row = pl.multiple_of(
                    tile_ref[chunk * CHUNK_BLOCKS + b] * BLOCK_WORDS, BLOCK_WORDS
                )
                d_ref[rows, columns] = (
                    gp_ref[pl.ds(row, BLOCK_WORDS), columns] * slope[rows]
                ).astype(BF16)
            dw_ref[:, columns] += dot_tn(x_ref[...], d_ref[:, columns])
        gx = dot_nt(d_ref[...], w_ref[...])
        for b in range(CHUNK_BLOCKS):
            block = chunk * CHUNK_BLOCKS + b
            row = pl.multiple_of(tile_ref[block] * BLOCK_WORDS, BLOCK_WORDS)
            position = pos_ref[block]
            group = position >> 3
            offset = (position & 7) * CHAR_DIM
            value = gx[b * BLOCK_WORDS : (b + 1) * BLOCK_WORDS, :]
            value = pltpu.roll(jnp.where(lane < BIAS_LANE, value, 0.0), offset, 1)
            gg_ref[group, pl.ds(row, BLOCK_WORDS), :] += jnp.where(lane >= offset, value, 0.0)
            gg_ref[group + 1, pl.ds(row, BLOCK_WORDS), :] += jnp.where(lane < offset, value, 0.0)
        return carry

    lax.fori_loop(0, scalar_ref[0], step, 0)
    out_ref[...] = dw_ref[...].T.astype(BF16)


def conv_backward(prep, char_groups, half_matrix, grad_scaled):
    _, ids, lengths, scalars, tile, position = prep
    filters = half_matrix.shape[1]
    return pl.pallas_call(
        conv_backward_kernel,
        out_shape=(
            jax.ShapeDtypeStruct((filters, LANES), BF16),
            jax.ShapeDtypeStruct(char_groups.shape, F32),
        ),
        in_specs=[SMEM, SMEM, SMEM, VMEM, VMEM, VMEM, VMEM],
        out_specs=(VMEM, VMEM),
        scratch_shapes=[
            pltpu.VMEM((CHUNK, LANES), BF16),
            pltpu.VMEM((CHUNK, filters), BF16),
            pltpu.VMEM((LANES, filters), F32),
        ],
        compiler_params=pltpu.CompilerParams(vmem_limit_bytes=48 * MIB),
        cost_estimate=cost(35),
        name="conv_backward",
    )(scalars, tile, position, char_groups, half_matrix, lengths[:, None], grad_scaled)


def table_kernel(scalar_ref, ids_ref, gg_ref, out_ref):
    groups = gg_ref.shape[0]
    out_ref[...] = jnp.zeros_like(out_ref)
    identity = lax.broadcasted_iota(jnp.int32, (TABLE_PAD, ROW_TILE), 0)
    for group in range(groups - 1):

        def step(index, carry, group=group):
            row = pl.multiple_of(index * ROW_TILE, ROW_TILE)
            grad = (2.0 * gg_ref[group, pl.ds(row, ROW_TILE), :]).astype(BF16)
            for k in range(GROUP):
                column = group * GROUP + k
                hot = (ids_ref[column : column + 1, pl.ds(row, ROW_TILE)] == identity).astype(F32)
                out_ref[k] += dot(hot.astype(BF16), grad)
            return carry

        lax.fori_loop(0, scalar_ref[1 + group], step, 0)


def table_gradient(prep, grad_groups, vocabulary):
    ids, scalars = prep[1], prep[3]
    total = pl.pallas_call(
        table_kernel,
        out_shape=jax.ShapeDtypeStruct((GROUP, TABLE_PAD, LANES), F32),
        in_specs=[SMEM, VMEM, VMEM],
        out_specs=VMEM,
        compiler_params=pltpu.CompilerParams(vmem_limit_bytes=32 * MIB),
        cost_estimate=cost(4),
        name="table_gradient",
    )(scalars, ids.T, grad_groups)
    parts = [total[k, :vocabulary, k * CHAR_DIM : (k + 1) * CHAR_DIM] for k in range(GROUP)]
    return sum(parts[1:], parts[0])


def table_lanes(table):
    padded = jnp.pad(table, ((0, TABLE_PAD - table.shape[0]), (0, 0)))
    return jnp.stack(
        [
            jnp.pad(padded, ((0, 0), (k * CHAR_DIM, LANES - (k + 1) * CHAR_DIM)))
            for k in range(GROUP)
        ]
    )


ANY = pl.BlockSpec(memory_space=pl.ANY)


def flat_pieces(pieces):
    return [array for half in pieces for chunk in half for array in chunk]


def piece_copies(layout, array, slot, first, own, pieces, whole_ref, sems, buffer):
    halves, chunks, arrays, rows = layout
    width = whole_ref.shape[2] // 2
    copies = []
    for half in range(halves):
        for chunk in range(chunks):
            ref = pieces[(half * chunks + chunk) * arrays + array]
            start = (own if half == 0 else 1 - own) * (chunks * rows) + chunk * rows
            start = pl.multiple_of(start, rows)
            for side in range(2):
                copies.append(
                    pltpu.make_async_copy(
                        ref.at[first if side == 0 else 1 - first, slot],
                        whole_ref.at[
                            buffer, pl.ds(start, rows), side * width : (side + 1) * width
                        ],
                        sems.at[buffer, len(copies)],
                    )
                )
    return copies


def fetch_pieces(layout, select_ref, own, pieces, whole_ref, sems):
    step = pl.program_id(0)

    def start(index):
        for array in range(layout[2]):

            @pl.when(index // 2 == array)
            def _(array=array):
                for copy in piece_copies(
                    layout, array, index % 2, select_ref[index], own, pieces, whole_ref, sems, index % 2
                ):
                    copy.start()

    @pl.when(step == 0)
    def _():
        start(0)

    @pl.when(step + 1 < pl.num_programs(0))
    def _():
        start(step + 1)

    buffer = step % 2
    for copy in piece_copies(layout, 0, 0, 0, own, pieces, whole_ref, sems, buffer):
        copy.wait()
    return buffer


def half_tanh(value):
    return 0.5 + 0.5 * jnp.tanh(0.5 * value)


def highway_forward_kernel(layout, place_ref, select_ref, core_ref, h_ref, bias_ref, *refs):
    count = layout[0] * layout[1] * layout[2]
    pieces = refs[:count]
    next_ref, transform_ref, gating_ref, low_ref, whole_ref, sems = refs[count:]
    step = pl.program_id(0)
    width = next_ref.shape[1]

    @pl.when(step == 0)
    def _():
        low_ref[...] = h_ref[...].astype(BF16)

    block = place_ref[step]
    blocks = bias_ref.shape[0] // 2
    buffer = fetch_pieces(layout, select_ref, core_ref[0], pieces, whole_ref, sems)
    mixed = dot(low_ref[...], whole_ref[buffer])
    transform = mixed[:, :width] + bias_ref[block]
    gating = half_tanh(mixed[:, width:] + bias_ref[block + blocks])
    h = h_ref[:, pl.ds(pl.multiple_of(block * width, width), width)]
    activated = transform * half_tanh(transform)
    transform_ref[...] = transform
    gating_ref[...] = gating
    next_ref[...] = activated + gating * (h - activated)


def highway_forward(h, pieces, bias_blocks, place, select, core):
    words, features = h.shape
    width = bias_blocks.shape[2]
    flat = flat_pieces(pieces)
    layout = (len(pieces), len(pieces[0]), len(pieces[0][0]), flat[0].shape[2])
    column = pl.BlockSpec((words, width), lambda j, place, *_: (0, place[j]))
    whole = lambda shape: pl.BlockSpec(shape, lambda j, *_: (0,) * len(shape))
    return pl.pallas_call(
        partial(highway_forward_kernel, layout),
        grid_spec=pltpu.PrefetchScalarGridSpec(
            num_scalar_prefetch=3,
            grid=(features // width,),
            in_specs=[whole(h.shape), whole(bias_blocks.shape)] + [ANY] * len(flat),
            out_specs=[column, column, column, whole(h.shape)],
            scratch_shapes=[
                pltpu.VMEM((2, features, 2 * width), BF16),
                pltpu.SemaphoreType.DMA((2, 2 * layout[0] * layout[1])),
            ],
        ),
        out_shape=(
            jax.ShapeDtypeStruct(h.shape, F32),
            jax.ShapeDtypeStruct(h.shape, F32),
            jax.ShapeDtypeStruct(h.shape, F32),
            jax.ShapeDtypeStruct(h.shape, BF16),
        ),
        compiler_params=pltpu.CompilerParams(vmem_limit_bytes=56 * MIB),
        cost_estimate=cost(19),
        name="highway_forward",
    )(place, select, core, h, bias_blocks, *flat)


def highway_backward_kernel(layout, place_ref, select_ref, core_ref, grad_ref, h_ref, t_ref, g_ref, *refs):
    count = layout[0] * layout[1] * layout[2]
    pieces = refs[:count]
    mixed_ref, sums_ref, out_ref, whole_ref, sems = refs[count:]
    step = pl.program_id(0)
    width = grad_ref.shape[1]
    features = out_ref.shape[1]

    @pl.when(step == 0)
    def _():
        out_ref[...] = jnp.zeros_like(out_ref)

    block = place_ref[step]
    buffer = fetch_pieces(layout, select_ref, core_ref[0], pieces, whole_ref, sems)
    grad = grad_ref[...]
    transform = t_ref[...]
    gating = g_ref[...]
    sigmoid = half_tanh(transform)
    activated = transform * sigmoid
    rest = grad * (1.0 - gating)
    low_t = (rest * (sigmoid + activated * (1.0 - sigmoid))).astype(BF16)
    low_g = (rest * gating * (h_ref[...] - activated)).astype(BF16)
    mixed_ref[0] = low_t
    mixed_ref[1] = low_g
    sums_ref[0] = jnp.sum(low_t.astype(F32), axis=0, keepdims=True)
    sums_ref[1] = jnp.sum(low_g.astype(F32), axis=0, keepdims=True)
    low = jnp.concatenate([low_t, low_g], axis=1)
    for start in range(0, features, 512):
        out_ref[:, start : start + 512] += dot_nt(
            low, whole_ref[buffer, start : start + 512, :]
        )
    out_ref[:, pl.ds(pl.multiple_of(block * width, width), width)] += grad * gating


def highway_backward(grad, h, transform, gating, pieces, place, select, core):
    words, features = h.shape
    flat = flat_pieces(pieces)
    width = flat[0].shape[3]
    layout = (len(pieces), len(pieces[0]), len(pieces[0][0]), flat[0].shape[2])
    column = pl.BlockSpec((words, width), lambda j, place, *_: (0, place[j]))
    return pl.pallas_call(
        partial(highway_backward_kernel, layout),
        grid_spec=pltpu.PrefetchScalarGridSpec(
            num_scalar_prefetch=3,
            grid=(features // width,),
            in_specs=[column] * 4 + [ANY] * len(flat),
            out_specs=[
                pl.BlockSpec((2, words, width), lambda j, place, *_: (0, 0, place[j])),
                pl.BlockSpec((2, 1, width), lambda j, place, *_: (0, 0, place[j])),
                pl.BlockSpec(h.shape, lambda j, *_: (0, 0)),
            ],
            scratch_shapes=[
                pltpu.VMEM((2, features, 2 * width), BF16),
                pltpu.SemaphoreType.DMA((2, 2 * layout[0] * layout[1])),
            ],
        ),
        out_shape=(
            jax.ShapeDtypeStruct((2, words, features), BF16),
            jax.ShapeDtypeStruct((2, 1, features), F32),
            jax.ShapeDtypeStruct(h.shape, F32),
        ),
        compiler_params=pltpu.CompilerParams(vmem_limit_bytes=56 * MIB),
        cost_estimate=cost(21),
        name="highway_backward",
    )(place, select, core, grad, h, transform, gating, *flat)


def weight_kernel(which_ref, left_ref, right_ref, *refs):
    out_ref = refs[-1]
    value = dot(left_ref[...], right_ref[0])
    width = out_ref.shape[2]
    for number in range(out_ref.shape[0]):
        block = value[:, number * width : (number + 1) * width]
        if len(refs) == 2:
            block = block + refs[0][number].astype(F32)
        out_ref[number] = block.astype(BF16)


def highway_weight_gradient(which, turned, mixed, first, rows, width, added=None, part=0):
    words, features = mixed.shape[1:]
    blocks = 8
    out = pl.BlockSpec((blocks, rows, width), lambda j, which: (j, 0, 0))
    return pl.pallas_call(
        weight_kernel,
        grid_spec=pltpu.PrefetchScalarGridSpec(
            num_scalar_prefetch=1,
            grid=(features // (blocks * width),),
            in_specs=[
                pl.BlockSpec((rows, words), lambda j, which: (first // rows, 0)),
                pl.BlockSpec((1, words, blocks * width), lambda j, which: (which[0], 0, j)),
            ]
            + (
                []
                if added is None
                else [pl.BlockSpec((blocks, rows, width), lambda j, which: (j, part, 0))]
            ),
            out_specs=out,
        ),
        out_shape=jax.ShapeDtypeStruct((features // width, rows, width), BF16),
        compiler_params=pltpu.CompilerParams(vmem_limit_bytes=32 * MIB),
        cost_estimate=cost(3),
        name="highway_weight",
    )(which, turned, mixed, *([] if added is None else [added]))


def turn_kernel(value_ref, out_ref):
    out_ref[...] = value_ref[...].T.astype(BF16)


def turn(value):
    rows, columns = value.shape
    return pl.pallas_call(
        turn_kernel,
        grid=(columns // 256,),
        in_specs=[pl.BlockSpec((rows, 256), lambda j: (0, j))],
        out_specs=pl.BlockSpec((256, rows), lambda j: (j, 0)),
        out_shape=jax.ShapeDtypeStruct((columns, rows), BF16),
        compiler_params=pltpu.CompilerParams(vmem_limit_bytes=32 * MIB),
        cost_estimate=cost(1),
        name="turn",
    )(value)


def place_rows_kernel(splits, place_ref, core_ref, *refs):
    arrays = (len(refs) - len(splits) - 1) // 2
    own_refs, other_refs = refs[:arrays], refs[arrays : 2 * arrays]
    out_refs, whole_ref = refs[2 * arrays : -1], refs[-1]
    step = pl.program_id(0)
    half_rows = own_refs[0].shape[1]
    core = core_ref[0]
    for array in range(arrays):

        @pl.when(step // 4 == array)
        def _(array=array):
            align = lambda start: pl.ds(pl.multiple_of(start, 16), half_rows)
            whole_ref[align(core * half_rows), :] = own_refs[array][0]
            whole_ref[align((1 - core) * half_rows), :] = other_refs[array][0]

    start = 0
    for rows, out_ref in zip(splits, out_refs):
        out_ref[...] = whole_ref[start : start + rows, :]
        start += rows


def place_rows(own, other, place, core, splits):
    half_rows, columns = own[0].shape[1:]

    def index(number):
        return lambda j, *_: (jnp.clip(j - 4 * number, 0, 3), 0, 0)

    specs = [pl.BlockSpec((1, half_rows, columns), index(number)) for number in range(len(own))]
    return pl.pallas_call(
        partial(place_rows_kernel, splits),
        grid_spec=pltpu.PrefetchScalarGridSpec(
            num_scalar_prefetch=2,
            grid=(4 * len(own),),
            in_specs=specs + specs,
            out_specs=[
                pl.BlockSpec((rows, columns), lambda j, place, *_: (place[j], 0)) for rows in splits
            ],
            scratch_shapes=[pltpu.VMEM((2 * half_rows, columns), BF16)],
        ),
        out_shape=[
            jax.ShapeDtypeStruct((4 * len(own) * rows, columns), BF16) for rows in splits
        ],
        compiler_params=pltpu.CompilerParams(vmem_limit_bytes=32 * MIB),
        cost_estimate=cost(7),
        name="place_rows",
    )(place, core, *own, *other)


def place_small_kernel(place_ref, *refs):
    inputs, (conv_ref, *row_refs) = refs[:4], refs[4:]
    step = pl.program_id(0)
    for number, ref in enumerate(inputs):

        @pl.when(step // 4 == number)
        def _(ref=ref):
            start = conv_ref.shape[0]
            conv_ref[...] = ref[0, :start, :]
            for row_ref in row_refs:
                row_ref[0] = ref[0, start : start + row_ref.shape[1], :]
                start += row_ref.shape[1]


def place_small(arrays, place, conv_rows, splits):
    rows, columns = arrays[0].shape[1:]

    def index(number):
        return lambda j, *_: (jnp.clip(j - 4 * number, 0, 3), 0, 0)

    return pl.pallas_call(
        place_small_kernel,
        grid_spec=pltpu.PrefetchScalarGridSpec(
            num_scalar_prefetch=1,
            grid=(16,),
            in_specs=[pl.BlockSpec((1, rows, columns), index(number)) for number in range(4)],
            out_specs=[pl.BlockSpec((conv_rows, columns), lambda j, place: (0, place[j]))]
            + [
                pl.BlockSpec((1, count, columns), lambda j, place: (place[j], 0, 0))
                for count in splits
            ],
        ),
        out_shape=[jax.ShapeDtypeStruct((conv_rows, 16 * columns), BF16)]
        + [jax.ShapeDtypeStruct((16, count, columns), BF16) for count in splits],
        compiler_params=pltpu.CompilerParams(vmem_limit_bytes=32 * MIB),
        cost_estimate=cost(2),
        name="place_small",
    )(place, *arrays)


LINKS = {
    "x": [(w, w ^ 1) for w in range(16)],
    "y": [(w, w ^ 2) for w in range(16)],
    "z": [(w, (w + 4) % 16) for w in range(16)],
    "z1": [(w, w ^ 4) for w in range(16)],
    "z2": [(w, w ^ 8) for w in range(16)],
}
CORES = [(0, 1), (1, 0)]


def send(value, link):
    if link == "c":
        return lax.ppermute(value, "narrow", CORES)
    return lax.ppermute(value, "wide", LINKS[link])


def total_of(terms):
    return sum((term.astype(F32) for term in terms[1:]), terms[0].astype(F32))


class Exchange:
    windows = True

    def __init__(self):
        self.core = lax.axis_index("narrow")
        index = lax.axis_index("wide")
        self.z, self.y, self.x = index // 4, (index // 2) % 2, index % 2
        self.state, self.fresh, self.count, self.planned = {}, [], 0, []

    def put(self, key, value):
        self.state[key] = value
        self.fresh.append(key)

    def move(self, key, source, link):
        self.put(key, send(self.state[source], link))

    def plan(self, key, value, link, shape=None):
        self.planned.append((key, value, link, shape))

    def plan_move(self, source, *links):
        for link in links:
            self.plan(source + link, self.state[source], link)

    def plan_ring(self, name, step):
        self.plan(f"{name}r{step}", self.state[f"{name}r{step - 1}" if step > 1 else name], "z")

    def plan_swap(self, *names):
        for name in names:
            self.plan(name + "c", self.state[name], "c")

    def launch(self, values):
        leaves, tree = jax.tree.flatten(values)
        held = lax.optimization_barrier(
            tuple(value for _, value, _, _ in self.planned) + tuple(leaves)
        )
        for (key, _, link, shape), value in zip(self.planned, held):
            value = send(value, link)
            self.put(key, value if shape is None else value.reshape(shape))
        leaves = held[len(self.planned) :]
        self.planned = []
        return jax.tree.unflatten(tree, leaves)

    def window(self, values, hold=()):
        held_keys = [key for key in self.fresh if key in hold]
        self.fresh = [key for key in self.fresh if key not in hold]
        leaves, tree = jax.tree.flatten(values)
        held = lax.optimization_barrier(
            tuple(self.state[key] for key in self.fresh) + tuple(leaves)
        )
        for key, value in zip(self.fresh, held):
            self.state[key] = value
        leaves = held[len(self.fresh) :]
        self.fresh = held_keys
        return jax.tree.unflatten(tree, leaves)

    def swap_chain(self, *names):
        before = None
        for name in names:
            value = self.state[name]
            if before is not None:
                value, self.state[before] = lax.optimization_barrier((value, self.state[before]))
            before = name + "c"
            self.put(before, send(value, "c"))

    def stage(self, values=(), hold=()):
        return self.window(self.launch(values), hold)


    def load(self, name, value, rows=None, offset=0, whole=False):
        if not whole:
            rows = rows or value.shape[0] // 2
            value = lax.dynamic_slice_in_dim(
                value, self.core * (value.shape[0] // 2) + offset, rows, 0
            )
        self.state[name] = value

    def ring(self, name):
        received = [self.state[name]]
        for _ in range(3):
            received.append(send(received[-1], "z"))
        self.put(name + "o", jnp.stack(received))

    def ring_step(self, name, step):
        self.move(f"{name}r{step}", f"{name}r{step - 1}" if step > 1 else name, "z")

    def ring_done(self, name):
        self.state[name + "o"] = jnp.stack(
            [self.state[name]] + [self.state[f"{name}r{step}"] for step in (1, 2, 3)]
        )

    def square(self, name):
        value = self.state[name]
        over_x = send(value, "x")
        self.put(name + "o0", jnp.stack([value, over_x, send(value, "y"), send(over_x, "y")]))

    def turn_ring(self, name, step):
        self.move(f"{name}o{step}", f"{name}o{step - 1}", "z")

    def swap(self, *names):
        for name in names:
            self.move(name + "c", name, "c")

    def near(self, name, suffix=""):
        return [self.state[name + part + suffix] for part in ("o", "ox", "oy", "oxy")]

    def layer(self, name, chunks):
        halves = []
        for suffix in ("", "c"):
            halves.append(
                [
                    [
                        array.reshape((2, 2) + array.shape[1:])
                        for array in self.near(f"{name}{chunk}", suffix)
                    ]
                    for chunk in range(chunks)
                ]
            )
        return halves

    def place(self, ring_last):
        step = jnp.arange(16)
        near, slot = (step % 4, step // 4) if ring_last else (step // 4, step % 4)
        return (
            (self.z - slot) % 4 * 4 + (self.y ^ (near >> 1)) * 2 + (self.x ^ (near & 1))
        ).astype(jnp.int32)

    def rows(self, own, other, splits, ring_last):
        core = self.core[None].astype(jnp.int32)
        return place_rows(own, other, self.place(ring_last), core, splits)


    def split(self, grads):
        blocks = [grad.astype(BF16).reshape(2, 16, -1, grad.shape[1]) for grad in grads]
        return tuple(
            jnp.concatenate(
                [lax.dynamic_index_in_dim(block, which, 0, keepdims=False) for block in blocks],
                axis=1,
            )
            for which in (self.core, 1 - self.core)
        )


class Reduction:
    def __init__(self, net, keep, sent, order):
        shape = (4, 2, 2) + keep.shape[1:]
        self.net, self.order, self.done = net, list(order), 0
        net.count += 1
        self.name = f"sum{net.count}"
        self.terms = [keep.reshape(shape)]
        self.keys, self.running, self.axes = [], None, ["z", "y", "x"]
        self.sent, self.shape = sent, shape

    def all_terms(self):
        return self.terms + [self.net.state[key] for key in self.keys]

    def pick(self, terms, index, axis):
        return [lax.dynamic_index_in_dim(term, index, axis, keepdims=False) for term in terms]

    def keep_only(self, index, axis):
        self.terms = self.pick(self.all_terms(), index, axis)
        self.keys = []

    def step(self, put=None):
        net, link = self.net, self.order[self.done]
        put = put or (lambda key, value, link, shape=None: net.put(
            key, send(value, link) if shape is None else send(value, link).reshape(shape)
        ))
        self.key = key = f"{self.name}_{self.done}"
        self.done += 1
        if link == "c":
            put(key, self.sent, "c", self.shape)
            self.keys.append(key)
        elif link in ("x", "y"):
            axis = self.axes.index(link)
            index = net.x if link == "x" else net.y
            sent = total_of(self.pick(self.all_terms(), 1 - index, axis)).astype(BF16)
            self.keep_only(index, axis)
            self.axes.remove(link)
            put(key, sent, link)
            self.keys.append(key)
        else:
            axis = self.axes.index("z")
            index = (net.z + int(link)) % 4
            terms = self.pick(self.all_terms(), index, axis)
            if self.running is not None:
                terms.append(net.state[self.running])
            put(key, total_of(terms).astype(BF16), "z")
            self.running = key
            if link == "1":
                self.keep_only(net.z, axis)
                self.axes.remove("z")
                self.keys = [key]
        return self

    def result(self):
        assert self.done == len(self.order)
        return total_of(self.all_terms())


class Ring:
    def __init__(self, net, sums):
        self.net, self.sums, self.done, self.running = net, sums, 0, None
        net.count += 1
        self.name = f"ring{net.count}"

    def part(self, distance):
        index = (self.net.z + distance) % 4
        parts = [total_of(item.pick(item.all_terms(), index, 0)) for item in self.sums]
        value = parts[0] if len(parts) == 1 else jnp.concatenate(parts, axis=0)
        if self.running is not None:
            value = value + self.net.state[self.running].astype(F32)
        return value

    def step(self, put=None):
        value = self.part(3 - self.done).astype(BF16)
        self.done += 1
        self.key = key = f"{self.name}_{self.done}"
        if put:
            put(key, value, "z")
        else:
            self.net.put(key, send(value, "z"))
        self.running = key
        return self

    def result(self):
        assert self.done == 3
        return self.part(0)


class Small:
    def __init__(self, net, value):
        self.net, self.value, self.done, self.key = net, value, 0, None
        net.count += 1
        self.name = f"small{net.count}"

    def result(self):
        return self.value if self.key is None else self.value + self.net.state[self.key]

    def step(self, put):
        self.value = self.result()
        self.key = f"{self.name}_{self.done}"
        put(self.key, self.value, ("c", "x", "y", "z1", "z2")[self.done])
        self.done += 1
        return self


class PlainReduction:
    def __init__(self, grads, axis):
        self.grads, self.axis = grads, axis

    def step(self):
        return self

    def result(self):
        return [
            lax.psum_scatter(
                grad.astype(BF16), ("narrow", "wide"), scatter_dimension=self.axis, tiled=True
            ).astype(F32)
            for grad in self.grads
        ]


def norm_rows(value, norm_gain, norm_shift):
    center = jnp.mean(value, axis=-1, keepdims=True)
    offsets = value - center
    spread = jnp.mean(offsets * offsets, axis=-1, keepdims=True)
    return offsets * lax.rsqrt(spread + EPSILON) * norm_gain + norm_shift


def norm_back(value, norm_gain, grad_rows):
    center = jnp.mean(value, axis=-1, keepdims=True)
    offsets = value - center
    spread = jnp.mean(offsets * offsets, axis=-1, keepdims=True)
    scale = lax.rsqrt(spread + EPSILON)
    normal = offsets * scale
    inner = grad_rows * norm_gain
    grad = scale * (
        inner
        - jnp.mean(inner, axis=-1, keepdims=True)
        - normal * jnp.mean(inner * normal, axis=-1, keepdims=True)
    )
    return grad, jnp.sum(grad_rows * normal, axis=0), jnp.sum(grad_rows, axis=0)


def row_copies(slots, own, arrays, array, up_refs, down_refs, up_ref, down_ref, sems, buffer):
    rows = up_refs[0].shape[1]
    copies = []
    for refs, whole_ref in ((up_refs, up_ref), (down_refs, down_ref)):
        for half in range(2):
            ref = refs[half * arrays + array]
            for number, slot in enumerate(slots):
                start = pl.multiple_of((own if half == 0 else 1 - own) * rows, rows)
                copies.append(
                    pltpu.make_async_copy(
                        ref.at[slot],
                        whole_ref.at[buffer, pl.ds(number * 2 * rows + start, rows), :],
                        sems.at[buffer, len(copies)],
                    )
                )
    return copies


def fetch_rows(slot_ref, own, up_refs, down_refs, up_ref, down_ref, sems):
    arrays = len(up_refs) // 2
    step = pl.program_id(0)

    def start(index):
        for array in range(arrays):

            @pl.when(index // 2 == array)
            def _(array=array):
                slots = [slot_ref[index, number] for number in range(2)]
                for copy in row_copies(
                    slots, own, arrays, array, up_refs, down_refs, up_ref, down_ref, sems, index % 2
                ):
                    copy.start()

    @pl.when(step == 0)
    def _():
        start(0)

    @pl.when(step + 1 < pl.num_programs(0))
    def _():
        start(step + 1)

    buffer = step % 2
    for copy in row_copies(
        (0, 0), own, arrays, 0, up_refs, down_refs, up_ref, down_ref, sems, buffer
    ):
        copy.wait()
    return buffer


def normal_share(value, bell):
    t = 1.0 / (1.0 + (0.3275911 * 2**-0.5) * jnp.abs(value))
    series = 1.061405429
    for term in (-1.453152027, 1.421413741, -0.284496736, 0.254829592):
        series = series * t + term
    tail = (0.5 * series) * (t * bell)
    return jnp.where(value < 0.0, tail, 1.0 - tail)


def feed_forward_kernel(
    count, slot_ref, block_ref, core_ref, first_ref, bias_ref, vectors_ref, cotangent_ref, *refs
):
    up_refs, down_refs = refs[:count], refs[count : 2 * count]
    act_ref, slope_ref, hidden_ref, grad_ref, sums_ref, up_ref, down_ref, low_ref, total_ref, sems = refs[
        2 * count :
    ]
    step = pl.program_id(0)

    @pl.when(step == 0)
    def _():
        low_ref[...] = first_ref[...].astype(BF16)
        total_ref[...] = first_ref[...] + vectors_ref[0:1, :]

    buffer = fetch_rows(slot_ref, core_ref[0], up_refs, down_refs, up_ref, down_ref, sems)
    inner = dot_nt(low_ref[...], up_ref[buffer]) + bias_ref[block_ref[step]]
    bell = jnp.exp(-0.5 * inner * inner)
    share = normal_share(inner, bell)
    act = (inner * share).astype(BF16)
    act_ref[0] = act
    slope_ref[0] = (
        share + inner * (bell * (2.0 * jnp.pi) ** -0.5)
    ).astype(BF16)
    total_ref[...] += dot(act, down_ref[buffer])

    @pl.when(step == pl.num_programs(0) - 1)
    def _():
        value = total_ref[...]
        gain, shift = vectors_ref[1:2, :], vectors_ref[2:3, :]
        offsets = value - jnp.mean(value, axis=-1, keepdims=True)
        scale = lax.rsqrt(jnp.mean(offsets * offsets, axis=-1, keepdims=True) + EPSILON)
        normal = offsets * scale
        hidden_ref[...] = (normal * gain + shift).astype(BF16)
        cotangent = cotangent_ref[...].astype(F32)
        pulled = cotangent * gain
        grad = scale * (
            pulled
            - jnp.mean(pulled, axis=-1, keepdims=True)
            - normal * jnp.mean(pulled * normal, axis=-1, keepdims=True)
        )
        grad_ref[...] = grad
        sums_ref[0:1, :] = jnp.sum(cotangent * normal, axis=0, keepdims=True)
        sums_ref[1:2, :] = jnp.sum(cotangent, axis=0, keepdims=True)
        sums_ref[2:3, :] = jnp.sum(grad.astype(BF16).astype(F32), axis=0, keepdims=True)
        sums_ref[3:8, :] = jnp.zeros((5, sums_ref.shape[1]), F32)


def feed_forward(first, pieces, bias_blocks, vectors, cotangent, slots, block, core):
    words, columns = first.shape
    steps, width = bias_blocks.shape[0], bias_blocks.shape[2]
    up, down = pieces
    whole = lambda shape: pl.BlockSpec(shape, lambda j, *_: (0,) * len(shape))
    tile = pl.BlockSpec((1, words, width), lambda j, *_: (j, 0, 0))
    return pl.pallas_call(
        partial(feed_forward_kernel, len(up)),
        grid_spec=pltpu.PrefetchScalarGridSpec(
            num_scalar_prefetch=3,
            grid=(steps,),
            in_specs=[
                whole(first.shape),
                whole(bias_blocks.shape),
                whole(vectors.shape),
                whole(cotangent.shape),
            ]
            + [ANY] * (len(up) + len(down)),
            out_specs=[tile, tile, whole(first.shape), whole(first.shape), whole((8, columns))],
            scratch_shapes=[
                pltpu.VMEM((2, width, columns), BF16),
                pltpu.VMEM((2, width, columns), BF16),
                pltpu.VMEM((words, columns), BF16),
                pltpu.VMEM((words, columns), F32),
                pltpu.SemaphoreType.DMA((2, 8)),
            ],
        ),
        out_shape=(
            jax.ShapeDtypeStruct((steps, words, width), BF16),
            jax.ShapeDtypeStruct((steps, words, width), BF16),
            jax.ShapeDtypeStruct((words, columns), BF16),
            jax.ShapeDtypeStruct((words, columns), F32),
            jax.ShapeDtypeStruct((8, columns), F32),
        ),
        compiler_params=pltpu.CompilerParams(vmem_limit_bytes=48 * MIB),
        cost_estimate=cost(20),
        name="feed_forward",
    )(slots, block, core, first, bias_blocks, vectors, cotangent, *up, *down)


def feed_forward_back_kernel(
    count,
    slot_ref,
    block_ref,
    core_ref,
    grad_ref,
    first_ref,
    act_ref,
    slope_ref,
    value_ref,
    gain_ref,
    *refs,
):
    up_refs, down_refs = refs[:count], refs[count : 2 * count]
    (
        up_keep_ref,
        up_sent_ref,
        down_keep_ref,
        down_sent_ref,
        bias_ref,
        out_ref,
        sums_ref,
        up_ref,
        down_ref,
        low_ref,
        low_first_ref,
        total_ref,
        sems,
    ) = refs[2 * count :]
    step = pl.program_id(0)

    @pl.when(step == 0)
    def _():
        total_ref[...] = grad_ref[...]
        low_ref[...] = grad_ref[...].astype(BF16)
        low_first_ref[...] = first_ref[...].astype(BF16)

    buffer = fetch_rows(slot_ref, core_ref[0], up_refs, down_refs, up_ref, down_ref, sems)
    low = low_ref[...]
    inner = (dot_nt(low, down_ref[buffer]) * slope_ref[0].astype(F32)).astype(BF16)
    bias_ref[0] = jnp.sum(inner.astype(F32), axis=0, keepdims=True)
    grad_down = dot_tn(act_ref[0], low).astype(BF16)
    grad_up = dot_tn(inner, low_first_ref[...]).astype(BF16)
    total_ref[...] += dot(inner, up_ref[buffer])
    rows = up_keep_ref.shape[3]

    def store(value, ref):
        for number in range(4):
            ref[number // 2, 0, number % 2] = value[number * rows : (number + 1) * rows, :]

    @pl.when(step % 2 == 0)
    def _():
        store(grad_up, up_sent_ref)
        store(grad_down, down_sent_ref)

    @pl.when(step % 2 == 1)
    def _():
        store(grad_up, up_keep_ref)
        store(grad_down, down_keep_ref)

    @pl.when(step == pl.num_programs(0) - 1)
    def _():
        value = value_ref[...]
        pulling = total_ref[...]
        offsets = value - jnp.mean(value, axis=-1, keepdims=True)
        scale = lax.rsqrt(jnp.mean(offsets * offsets, axis=-1, keepdims=True) + EPSILON)
        normal = offsets * scale
        pulled = pulling * gain_ref[...]
        grad = scale * (
            pulled
            - jnp.mean(pulled, axis=-1, keepdims=True)
            - normal * jnp.mean(pulled * normal, axis=-1, keepdims=True)
        )
        out_ref[...] = grad
        sums_ref[0:1, :] = jnp.sum(pulling * normal, axis=0, keepdims=True)
        sums_ref[1:2, :] = jnp.sum(pulling, axis=0, keepdims=True)
        sums_ref[2:3, :] = jnp.sum(grad.astype(BF16).astype(F32), axis=0, keepdims=True)
        sums_ref[3:8, :] = jnp.zeros((5, sums_ref.shape[1]), F32)


def feed_forward_back(grad, first, act, slope, value, gain, pieces, slots, block, core):
    words, columns = first.shape
    steps, _, width = act.shape
    up, down = pieces
    rows = width // 4
    whole = lambda shape: pl.BlockSpec(shape, lambda j, *_: (0,) * len(shape))
    tile = pl.BlockSpec((1, words, width), lambda j, *_: (j, 0, 0))
    out = pl.BlockSpec(
        (2, 1, 2, rows, columns), lambda j, slots, block, core: (0, block[j] % (steps // 2), 0, 0, 0)
    )
    part = jax.ShapeDtypeStruct((2, steps // 2, 2, rows, columns), BF16)
    return pl.pallas_call(
        partial(feed_forward_back_kernel, len(up)),
        grid_spec=pltpu.PrefetchScalarGridSpec(
            num_scalar_prefetch=3,
            grid=(steps,),
            in_specs=[
                whole(grad.shape),
                whole(first.shape),
                tile,
                tile,
                whole(value.shape),
                whole(gain.shape),
            ]
            + [ANY] * (len(up) + len(down)),
            out_specs=[
                out,
                out,
                out,
                out,
                pl.BlockSpec((1, 1, width), lambda j, slots, block, core: (block[j], 0, 0)),
                whole(first.shape),
                whole((8, columns)),
            ],
            scratch_shapes=[
                pltpu.VMEM((2, width, columns), BF16),
                pltpu.VMEM((2, width, columns), BF16),
                pltpu.VMEM((words, columns), BF16),
                pltpu.VMEM((words, columns), BF16),
                pltpu.VMEM((words, columns), F32),
                pltpu.SemaphoreType.DMA((2, 8)),
            ],
        ),
        out_shape=(
            part,
            part,
            part,
            part,
            jax.ShapeDtypeStruct((steps, 1, width), F32),
            jax.ShapeDtypeStruct((words, columns), F32),
            jax.ShapeDtypeStruct((8, columns), F32),
        ),
        compiler_params=pltpu.CompilerParams(vmem_limit_bytes=48 * MIB),
        cost_estimate=cost(25),
        name="feed_forward_back",
    )(slots, block, core, grad, first, act, slope, value, gain, *up, *down)


def softmax_parts(query, key):
    scores = dot_nt(query, key)
    scaling = HEAD_DIM ** (-0.5) * 1.4426950408889634
    exponent = jnp.exp2((scores - jnp.max(scores, axis=-1, keepdims=True)) * scaling)
    return exponent, 1.0 / jnp.sum(exponent, axis=-1, keepdims=True)


def attend_kernel(query_ref, key_ref, value_ref, out_ref):
    for start in range(0, LANES, HEAD_DIM):
        head = slice(start, start + HEAD_DIM)
        exponent, scale = softmax_parts(query_ref[:, head], key_ref[:, head])
        attention = (exponent * scale).astype(BF16)
        out_ref[:, head] = dot(attention, value_ref[:, head]).astype(BF16)


def third(number, words, thirds):
    return pl.BlockSpec((words, LANES), lambda j: (0, number * thirds + j))


def attend(qkv):
    words = qkv.shape[0]
    pairs = qkv.shape[1] // (3 * LANES)
    return pl.pallas_call(
        attend_kernel,
        grid=(pairs,),
        in_specs=[third(number, words, pairs) for number in range(3)],
        out_specs=third(0, words, pairs),
        out_shape=jax.ShapeDtypeStruct((words, pairs * LANES), BF16),
        compiler_params=pltpu.CompilerParams(vmem_limit_bytes=32 * MIB),
        cost_estimate=cost(12),
        name="attend",
    )(qkv, qkv, qkv)


def attend_back_kernel(
    query_ref, key_ref, value_ref, grad_ref, grad_query_ref, grad_key_ref, grad_value_ref
):
    scaling = HEAD_DIM ** (-0.5)
    for start in range(0, LANES, HEAD_DIM):
        head = slice(start, start + HEAD_DIM)
        query, key = query_ref[:, head], key_ref[:, head]
        grad = grad_ref[:, head]
        exponent, scale = softmax_parts(query, key)
        attention = exponent * scale
        grad_attention = dot_nt(grad, value_ref[:, head])
        inner = jnp.sum(grad_attention * attention, axis=-1, keepdims=True)
        grad_scores = (attention * (grad_attention - inner)).astype(BF16)
        grad_value_ref[:, head] = dot_tn(attention.astype(BF16), grad).astype(BF16)
        grad_query_ref[:, head] = (dot(grad_scores, key) * scaling).astype(BF16)
        grad_key_ref[:, head] = (dot_tn(grad_scores, query) * scaling).astype(BF16)


def attend_back(qkv, grad_context):
    words = qkv.shape[0]
    pairs = qkv.shape[1] // (3 * LANES)
    out = third(0, words, pairs)
    return jnp.concatenate(
        pl.pallas_call(
            attend_back_kernel,
            grid=(pairs,),
            in_specs=[third(number, words, pairs) for number in range(3)] + [out],
            out_specs=(out, out, out),
            out_shape=(jax.ShapeDtypeStruct(grad_context.shape, BF16),) * 3,
            compiler_params=pltpu.CompilerParams(vmem_limit_bytes=32 * MIB),
            cost_estimate=cost(17),
        name="attend_back",
        )(qkv, qkv, qkv, grad_context),
        axis=1,
    )


def gather_plain(value, axis):
    return lax.all_gather(value, "wide", axis=axis, tiled=True)


def plain_pieces(weight, chunks):
    whole = gather_plain(weight, 1)
    rows = whole.shape[0] // (2 * chunks)
    width = whole.shape[1] // 16
    halves = []
    for half in range(2):
        pieces = []
        for chunk in range(chunks):
            start = (half * chunks + chunk) * rows
            arrays = []
            for near in range(4):
                slots = []
                for slot in range(4):
                    block = (-slot % 4) * 4 + near
                    slots.append(whole[start : start + rows, block * width : (block + 1) * width])
                arrays.append(jnp.stack(slots).reshape(2, 2, rows, width))
            pieces.append(arrays)
        halves.append(pieces)
    return halves


def vector_rows(vectors):
    rows, places, start = [], [], 0
    for vector in vectors:
        count = -(-vector.shape[0] // LANES)
        padded = jnp.pad(vector, (0, count * LANES - vector.shape[0]))
        rows.append(padded.reshape(count, LANES))
        places.append((start, count, vector.shape[0]))
        start += count
    return jnp.pad(jnp.concatenate(rows, axis=0), ((0, -start % 16), (0, 0))), places


def plain_rows(whole):
    rows = whole.shape[0] // 16
    arrays = []
    for half in range(2):
        for near in range(4):
            starts = [((-slot % 4) * 4 + near) * rows + half * rows // 2 for slot in range(4)]
            arrays.append(jnp.stack([whole[start : start + rows // 2] for start in starts]))
    return arrays


def body(
    permutes,
    wide,
    devices,
    char_ids,
    word_lengths,
    type_ids,
    cotangent,
    character_embedding_table,
    conv_weight,
    conv_bias,
    high_weight,
    high_bias,
    proj_weight,
    proj_bias,
    pos_table,
    type_table,
    embed_gain,
    embed_shift,
    qkv_weight,
    attn_bias,
    out_weight,
    out_bias,
    attn_gain,
    attn_shift,
    up_weight,
    up_bias,
    down_weight,
    down_bias,
    ffn_gain,
    ffn_shift,
):
    layers, features = high_weight.shape[:2]
    words, chars = char_ids.shape[1:]
    model_width = proj_weight.shape[1]
    conv_rows = conv_weight.shape[0]
    lengths = word_lengths[0]
    vectors = [high_bias[layer] for layer in range(layers)] + [
        attn_bias,
        type_table[0],
        type_table[1],
        proj_bias,
        embed_gain,
        embed_shift,
        out_bias,
        attn_gain,
        attn_shift,
        up_bias,
        down_bias,
        ffn_gain,
        ffn_shift,
    ]
    conv_block = jnp.pad(
        jnp.concatenate([conv_weight, conv_bias[None]], axis=0),
        ((0, LANES - conv_rows - 1), (0, 0)),
    )
    vector_block, places = vector_rows(vectors)

    if permutes:
        net = Exchange()
        window, launch = net.window, net.launch
        core_index, z, y, x = net.core, net.z, net.y, net.x
        net.load(
            "small",
            jnp.concatenate([conv_block, vector_block, pos_table.T.reshape(-1, LANES)], axis=0),
            whole=True,
        )
        chunk_rows = features // 4
        net.load("L00", high_weight[0], chunk_rows, 0)
        (
            net.state["L00"],
            net.state["small"],
            char_ids,
            lengths,
            high_weight,
            qkv_weight,
            up_weight,
        ) = lax.optimization_barrier(
            (
                net.state["L00"],
                net.state["small"],
                char_ids,
                lengths,
                high_weight,
                qkv_weight,
                up_weight,
            )
        )
        for layer, chunk in ((0, 1), (1, 0), (1, 1)):
            net.load(f"L{layer}{chunk}", high_weight[layer], chunk_rows, chunk * chunk_rows)
        encoder_splits = [
            qkv_weight.shape[1],
            out_weight.shape[0],
            proj_weight.shape[0],
        ]
        net.load(
            "e",
            jnp.concatenate(
                [qkv_weight.T, out_weight, proj_weight],
                axis=0,
            ),
        )
        net.load("up", up_weight.T)
        net.load("down", down_weight)
        net.ring_step("L00", 1)
        net.move("smallx", "small", "x")
        net.move("smally", "small", "y")
    else:
        window = lambda values, hold=(): values
        launch = window
        core_index = z = y = x = jnp.zeros((), jnp.int32)
    prep = sort_words(char_ids[0], lengths, chars // GROUP + 2)
    table_blocks = table_lanes(character_embedding_table)
    prep, table_blocks = window((prep, table_blocks))
    if permutes:
        net.ring_step("L00", 2)
        net.move("smallxy", "smallx", "y")
        net.move("ex", "e", "x")
        net.move("ey", "e", "y")
        window(())
        net.ring_step("L00", 3)
        net.put("smallo0", jnp.stack([net.state["small" + part] for part in ("", "x", "y", "xy")]))
        net.turn_ring("small", 1)
        net.move("exy", "ex", "y")
        window(())
        net.ring_done("L00")
        net.plan_move("L00o", "x", "y")
        net.plan_ring("L01", 1)
        net.plan("smallo2", net.state["smallo1"], "z")
        launch(())
        net.state["eo0"] = jnp.stack([net.state["e" + part] for part in ("", "x", "y", "xy")])
        net.ring_step("L01", 2)
        net.turn_ring("small", 3)
        net.ring_step("L01", 3)
        conv_all, whole_vectors, pos_all = place_small(
            [net.state[f"smallo{step}"] for step in range(4)],
            net.place(True),
            LANES,
            [vector_block.shape[0], pos_table.size // LANES],
        )
        conv_all, whole_vectors, pos_all = window((conv_all, whole_vectors, pos_all))
        net.ring_done("L01")
        net.plan_move("L01o", "x", "y")
        net.plan_ring("L10", 1)
        prep, table_blocks, conv_all, whole_vectors, pos_all = launch(
            (prep, table_blocks, conv_all, whole_vectors, pos_all)
        )
        net.ring_step("L10", 2)
        net.ring_step("L10", 3)
        net.swap_chain("L00o", "L00ox", "L00oy")
    else:
        conv_all = gather_plain(conv_block, 1)
        whole_vectors = lax.all_gather(vector_block, "wide", axis=0, tiled=False)
        pos_all = gather_plain(pos_table.T, 0)
    pos_rows = pos_all.reshape(model_width, words).T.astype(F32)
    whole = [
        whole_vectors[:, start : start + count].reshape(wide, -1)[:, :size].reshape(-1)
        for start, count, size in places
    ]
    filters = conv_all.shape[1]
    row = jnp.arange(LANES)[:, None]
    usable = row // CHAR_DIM < filter_widths(filters)[None, :]
    half_matrix = jnp.where(usable | (row >= conv_rows), conv_all * BF16(0.5), BF16(0.0))
    char_groups = embed_characters(prep, table_blocks)
    pooled = jnp.zeros((words, filters), F32)
    pooled = conv_forward(prep, char_groups, half_matrix, pooled, 0, filters // 2)
    pooled, char_groups, half_matrix, whole, pos_rows = window(
        (pooled, char_groups, half_matrix, whole, pos_rows)
    )
    high_bias_all, attn_bias_all = whole[:layers], whole[layers]
    (
        type_zero,
        type_one,
        proj_bias_all,
        gain_zero,
        shift_zero,
        out_bias_all,
        gain_one,
        shift_one,
        up_bias_all,
        down_bias_all,
        gain_two,
        shift_two,
    ) = (value.astype(F32) for value in whole[layers + 1 :])

    if permutes:
        net.ring_done("L10")
        net.plan("L00oxy", net.state["L00ox"], "y")
        net.plan("L01oxy", net.state["L01oy"], "x")
        net.plan("eo1", net.state["eo0"], "z")
        pooled = launch(pooled)
        net.swap_chain("L01o", "L01ox", "L01oy")
    pooled = conv_forward(prep, char_groups, half_matrix, pooled, filters // 2, filters // 2)
    if permutes:
        pooled = window(pooled)
        net.plan_move("L10o", "x", "y")
        net.plan_ring("L11", 1)
        launch(())
        net.ring_step("L11", 2)
        net.ring_step("L11", 3)
        net.swap_chain("L00oxy", "L01oxy", "eo0")
        pooled = window(pooled)
        net.ring_done("L11")
        net.plan_move("L11o", "x", "y")
        net.plan("eo2", net.state["eo1"], "z")
        pooled = launch(pooled)
        net.swap_chain("L10o", "L10ox", "L10oy")
        pieces = [net.layer("L0", 2)]
    else:
        pieces = [plain_pieces(high_weight[layer], 2) for layer in range(layers)]
    width = 2 * features // 16
    order = jnp.arange(8)
    near, low_slot = order // 2, order % 2
    slot_z = (z - low_slot) % 4
    place = ((slot_z & 1) * 4 + (y ^ (near >> 1)) * 2 + (x ^ (near & 1))).astype(jnp.int32)
    select = (slot_z // 2).astype(jnp.int32)
    core = core_index[None].astype(jnp.int32)
    bias_blocks = [bias.astype(F32).reshape(16, 1, width) for bias in high_bias_all]
    first_layer = highway_forward(pooled, pieces[0], bias_blocks[0], place, select, core)
    first_layer = window(first_layer)

    if permutes:
        net.plan("L10oxy", net.state["L10ox"], "y")
        net.plan("L11oxy", net.state["L11oy"], "x")
        net.plan("eo3", net.state["eo2"], "z")
        first_layer = launch(first_layer)
        net.swap_chain("L11o", "L11ox", "L11oy", "eo1", "eo2")
    turned = [turn(first_layer[3])]
    turned = window(turned)
    if permutes:
        net.plan_swap("L10oxy", "L11oxy", "eo3")
        net.plan_ring("up", 1)
        net.plan_ring("down", 1)
        first_layer = launch(first_layer)
        for step in (2, 3):
            net.ring_step("up", step)
            net.ring_step("down", step)
        pieces.append(net.layer("L1", 2))
        qkv_all, out_all, proj_all = net.rows(
            [net.state[f"eo{step}"] for step in range(4)],
            [net.state[f"eo{step}c"] for step in range(4)],
            encoder_splits,
            True,
        )
    else:
        qkv_all, out_all, proj_all = (
            gather_plain(value, 0) for value in (qkv_weight.T, out_weight, proj_weight)
        )
    second_layer = highway_forward(first_layer[0], pieces[1], bias_blocks[1], place, select, core)
    states = [pooled, first_layer[0], second_layer[0]]
    transforms = [first_layer[1], second_layer[1]]
    gatings = [first_layer[2], second_layer[2]]
    perm, sorted_lengths = prep[0], prep[2]
    last = dot_tn(perm, states[2].astype(BF16)).astype(BF16)
    word_vec = dot(last, proj_all) + proj_bias_all
    type_rows = jnp.where(type_ids[0][:, None] == 1, type_one[None], type_zero[None])
    summed = word_vec + pos_rows + type_rows
    embedded = norm_rows(summed, gain_zero, shift_zero)
    turned.append(turn(second_layer[3]))
    summed, embedded, last, turned = window((summed, embedded, last, turned))

    if permutes:
        net.ring_done("up")
        net.ring_done("down")
        net.plan_move("upo", "x", "y")
        net.plan_move("downo", "x", "y")
        embedded = launch(embedded)
        net.swap_chain("upo", "downo")
    low_embedded = embedded.astype(BF16)
    bias_three = jnp.concatenate(
        [
            attn_bias_all[:model_width],
            jnp.zeros((model_width,), BF16),
            attn_bias_all[model_width:],
        ]
    ).astype(F32)
    qkv = (dot_nt(low_embedded, qkv_all) + bias_three).astype(BF16)
    context = attend(qkv)
    if permutes:
        context = window(context)
        net.plan("upoxy", net.state["upox"], "y")
        net.plan("downoxy", net.state["downoy"], "x")
        context = launch(context)
        net.swap_chain("upox", "upoy", "downox", "downoy")
    first_in = embedded + (dot(context, out_all) + out_bias_all)
    first = norm_rows(first_in, gain_one, shift_one)
    if permutes:
        first_in, first = window((first_in, first))
        net.plan_swap("upoxy", "downoxy")
        first = launch(first)
        feed_pieces = [net.near(name) + net.near(name, "c") for name in ("up", "down")]
    else:
        feed_pieces = [
            plain_rows(gather_plain(value, 0)) for value in (up_weight.T, down_weight)
        ]
    half_of = jnp.where(order % 2 == 0, 1 - core_index, core_index)
    slots = (z - (2 * half_of[:, None] + jnp.arange(2)[None, :])) % 4
    slots = slots.astype(jnp.int32)
    feed_block = (half_of * 4 + (y ^ (near >> 1)) * 2 + (x ^ (near & 1))).astype(jnp.int32)
    feed_rows = up_bias_all.shape[0] // 16
    feed_bias = jnp.moveaxis(up_bias_all.reshape(2, 2, 4, feed_rows), 1, 2).reshape(8, 1, -1)
    act, slope, hidden_out, grad_second, last_sums = feed_forward(
        first,
        feed_pieces,
        feed_bias,
        jnp.stack([down_bias_all, gain_two, shift_two]),
        cotangent[0],
        slots,
        feed_block,
        core,
    )
    grad_ffn_gain, grad_ffn_shift, grad_down_bias = last_sums[0], last_sums[1], last_sums[2]

    def sum_rows(grads, order):
        if permutes:
            return Reduction(net, *net.split(grads), order)
        return PlainReduction(grads, 0)

    def send_layer(layer, mixed, first, rows):
        sent = highway_weight_gradient(1 - core, turned[layer], mixed, first, rows, width // 2)
        key = f"layer{layer}_{first}"
        if permutes:
            net.plan(key, sent, "c")
        return layer, mixed, first, rows, (key if permutes else sent, 0)

    def keep_layer(job, order):
        layer, mixed, first, rows, (key, part) = job
        keep = highway_weight_gradient(
            core,
            turned[layer],
            mixed,
            first,
            rows,
            width // 2,
            net.state[key] if permutes else None,
            part,
        )
        if permutes:
            return Reduction(net, keep, None, order)
        other = key[:, part * rows : (part + 1) * rows]
        whole = jnp.moveaxis(jnp.concatenate([keep, other], axis=0), 1, 0).reshape(rows, -1)
        return PlainReduction([whole], 1)

    def sum_feed(keep, sent, order):
        keep, sent = (value.reshape((16,) + value.shape[3:]) for value in (keep, sent))
        if permutes:
            return Reduction(net, keep, sent, order)
        return sum_rows([jnp.concatenate([keep, sent], axis=0).reshape(-1, model_width)], "")

    def ring_of(*sums):
        return Ring(net, sums) if permutes else sums

    def advance(*sums):
        if permutes:
            for item in sums:
                item.step()

    def ready(*sums):
        if permutes:
            for item in sums:
                item.step(net.plan)

    def held(*sums):
        return tuple(item.key for item in sums) if permutes else ()

    def together(*sums, hold=()):
        if permutes:
            ready(*sums)
            launch(())
            window((), held(*hold))

    up_keep, up_sent, down_keep, down_sent, bias_sums, grad_resid, norm_sums = feed_forward_back(
        grad_second,
        first,
        act,
        slope,
        first_in,
        gain_one[None],
        feed_pieces,
        slots,
        feed_block,
        core,
    )
    grad_up_bias = jnp.moveaxis(bias_sums.reshape(2, 4, 2, feed_rows), 2, 1).reshape(-1)
    grad_attn_gain, grad_attn_shift, grad_out_bias = norm_sums[0], norm_sums[1], norm_sums[2]
    up_keep, up_sent, down_keep, down_sent, grad_resid = window(
        (up_keep, up_sent, down_keep, down_sent, grad_resid)
    )

    sum_up = sum_feed(up_keep, up_sent, "cxy")
    sum_down = sum_feed(down_keep, down_sent, "cyx")
    ready(sum_down, sum_up)
    grad_resid = launch(grad_resid)
    grad_branch = grad_resid.astype(BF16)
    grad_out = dot_tn(context, grad_branch).astype(BF16)
    grad_context = dot_nt(grad_branch, out_all).astype(BF16)
    grad_qkv = attend_back(qkv, grad_context)
    grad_resid, grad_out, grad_qkv = window((grad_resid, grad_out, grad_qkv))

    ready(sum_down, sum_up)
    grad_qkv, grad_resid = launch((grad_qkv, grad_resid))
    grad_qkv_weight = dot_tn(grad_qkv, low_embedded)
    qkv_sums = column_sum(grad_qkv)
    grad_attn_bias = jnp.concatenate([qkv_sums[:model_width], qkv_sums[2 * model_width :]])
    grad_summed, grad_embed_gain, grad_embed_shift = norm_back(
        summed, gain_zero, grad_resid + dot(grad_qkv, qkv_all)
    )
    grad_word = grad_summed.astype(BF16)
    grad_proj_bias = column_sum(grad_word)
    running = dot_nt(dot(perm, grad_word).astype(BF16), proj_all)
    running = window(running)
    ready(sum_down, sum_up)
    running = launch(running)
    mixed_one, sums_one, running = highway_backward(
        running, states[1], transforms[1], gatings[1], pieces[1], place, select, core
    )
    grad_pos = turn(grad_summed)
    if permutes:
        grad_pos = grad_pos.reshape(-1, model_width)
    grad_proj = dot_tn(last, grad_word)
    encoder_grads = [grad_qkv_weight, grad_out, grad_proj]
    type_hot = (type_ids[0] == 1).astype(F32)[:, None]
    vector_grads = [
        grad_proj_bias,
        jnp.sum((1.0 - type_hot) * grad_summed, axis=0),
        jnp.sum(type_hot * grad_summed, axis=0),
        grad_embed_gain,
        grad_embed_shift,
        grad_attn_bias,
        grad_out_bias,
        grad_attn_gain,
        grad_attn_shift,
        grad_up_bias,
        grad_down_bias,
        grad_ffn_gain,
        grad_ffn_shift,
    ]
    if permutes:
        sum_encoder = sum_rows(encoder_grads + [grad_pos], "c321xy")
        mixed_one, running, sum_encoder.terms, sum_encoder.sent = window(
            (mixed_one, running, sum_encoder.terms, sum_encoder.sent)
        )
    else:
        sum_encoder = sum_rows(encoder_grads, "")
        sum_pos = sum_rows([grad_pos], "")

    half_rows, quarter = features // 2, features // 4
    jobs = [send_layer(1, mixed_one, start, half_rows) for start in (0, half_rows)]
    ring_feed = ring_of(sum_up, sum_down)
    ready(sum_encoder, ring_feed)
    running = launch(running)
    mixed_zero, sums_zero, running = highway_backward(
        running, states[0], transforms[0], gatings[0], pieces[0], place, select, core
    )
    mixed_one, mixed_zero, running = window((mixed_one, mixed_zero, running))

    one = [keep_layer(job, order_) for job, order_ in zip(jobs, ("yx", "xy"))]
    jobs = [send_layer(0, mixed_zero, start, half_rows) for start in (0, half_rows)]
    grad_scaled = running * (0.5 / sorted_lengths.astype(F32))[:, None]
    ready(*one, sum_encoder, ring_feed)
    grad_scaled = launch(grad_scaled)
    matrix_turned, grad_groups = conv_backward(prep, char_groups, half_matrix, grad_scaled)
    mixed_zero, matrix_turned, grad_groups = window((mixed_zero, matrix_turned, grad_groups))

    ready(*one, sum_encoder, ring_feed)
    mixed_zero, grad_groups = launch((mixed_zero, grad_groups))
    jobs = [
        (0, mixed_zero, start * quarter, quarter, (jobs[start // 2][-1][0], start % 2))
        for start in range(4)
    ]
    zero = [keep_layer(job, order_) for job, order_ in zip(jobs, ("yx", "yx", "xy", "xy"))]
    first_two = (zero[0], zero[2])
    terms = [item.terms for item in zero] if permutes else ()
    terms, grad_groups = window((terms, grad_groups))
    for item, value in zip(zero, terms):
        item.terms = value

    ready(*first_two, sum_encoder)
    grad_groups = launch(grad_groups)
    grad_table = table_gradient(prep, grad_groups, character_embedding_table.shape[0])
    last_sum, vector_places = vector_rows(
        vector_grads + [sums_zero.reshape(-1), sums_one.reshape(-1), grad_table.reshape(-1)]
    )
    last_sum = window(last_sum)
    last_sum = Small(net, last_sum) if permutes else lax.psum(last_sum, ("narrow", "wide"))

    ring_one = ring_of(*one)
    together(zero[1], zero[3], *first_two, ring_one)
    sum_conv = sum_rows([matrix_turned], "cxy321")
    ring_first = ring_of(*first_two)
    together(zero[1], zero[3], ring_first, ring_one, sum_conv)
    together(ring_first, ring_one, sum_encoder, last_sum, sum_conv)
    together(ring_first, sum_encoder, last_sum, sum_conv)
    ring_last = ring_of(zero[1], zero[3])
    together(ring_last, last_sum, sum_conv)
    together(ring_last, last_sum, sum_conv)
    together(ring_last, last_sum, sum_conv)
    total = last_sum.result() if permutes else last_sum

    device = lax.axis_index("narrow") * wide + lax.axis_index("wide")

    def whole_vector(total, where):
        start, count, size = where
        return total[start : start + count].reshape(-1)[:size]

    def own_part(total, where):
        piece = where[2] // devices
        return lax.dynamic_slice_in_dim(whole_vector(total, where), device * piece, piece, 0)

    results = [own_part(total, where) for where in vector_places[: len(vector_grads)]]
    high_places = vector_places[len(vector_grads) :]
    (
        sum_proj_bias,
        sum_type_zero,
        sum_type_one,
        sum_embed_gain,
        sum_embed_shift,
        sum_attn_bias,
        sum_out_bias,
        sum_attn_gain,
        sum_attn_shift,
        sum_up_bias,
        sum_down_bias,
        sum_ffn_gain,
        sum_ffn_shift,
    ) = results
    sum_high_bias = jnp.stack([own_part(total, where) for where in high_places[:layers]])
    sum_table = whole_vector(total, high_places[layers]).reshape(
        character_embedding_table.shape
    )

    def rows_of(item, sizes):
        total = item.result()
        if not permutes:
            return total
        pieces, start = [], 0
        for size in sizes:
            pieces.append(total[start : start + size])
            start += size
        return pieces

    qkv_rows, sum_out, sum_proj, *rest = rows_of(
        sum_encoder,
        [
            qkv_all.shape[0] // devices,
            out_all.shape[0] // devices,
            proj_all.shape[0] // devices,
            words * model_width // devices // model_width,
        ],
    )
    if permutes:
        pos_rows = rest[0].reshape(-1, words)
    else:
        (pos_rows,) = sum_pos.result()
    if permutes:
        up_rows, down_rows = jnp.split(ring_feed.result(), 2)
    else:
        (up_rows,), (down_rows,) = sum_up.result(), sum_down.result()
    (conv_turned,) = rows_of(sum_conv, [filters // devices])
    own_filters = lax.dynamic_slice_in_dim(
        filter_widths(filters), device * (filters // devices), filters // devices
    )
    taps = jnp.arange(conv_rows)[:, None] // CHAR_DIM
    sum_conv_weight = jnp.where(taps < own_filters[None, :], conv_turned[:, :conv_rows].T, 0.0)

    if permutes:
        first_rows, last_rows = ring_first.result(), ring_last.result()
        parts = [first_rows[:quarter], last_rows[:quarter], first_rows[quarter:], last_rows[quarter:]]
        high_rows = [jnp.concatenate(parts, axis=0), ring_one.result()]
    else:
        high_rows = [
            jnp.concatenate([part for item in sums for part in item.result()], axis=0)
            for sums in (zero, one)
        ]

    return (
        hidden_out[None],
        sum_table,
        sum_conv_weight,
        conv_turned[:, conv_rows],
        jnp.stack(high_rows),
        sum_high_bias,
        sum_proj,
        sum_proj_bias,
        pos_rows.T,
        jnp.stack([sum_type_zero, sum_type_one]),
        sum_embed_gain,
        sum_embed_shift,
        qkv_rows.T,
        sum_attn_bias,
        sum_out,
        sum_out_bias,
        sum_attn_gain,
        sum_attn_shift,
        up_rows.T,
        sum_up_bias,
        down_rows,
        sum_down_bias,
        sum_ffn_gain,
        sum_ffn_shift,
    )


def solution(mesh):
    narrow, wide = mesh.shape["narrow"], mesh.shape["wide"]
    both = ("narrow", "wide")
    placed = (
        P(both, None, None),
        P(both, None),
        P(both, None),
        P(both, None, None),
        P(),
        P(None, "wide"),
        P("wide"),
        P(None, None, "wide"),
        P(None, "wide"),
        P("wide", None),
        P("wide"),
        P(None, "wide"),
        P(None, "wide"),
        P("wide"),
        P("wide"),
        P(None, "wide"),
        P("wide"),
        P("wide", None),
        P("wide"),
        P("wide"),
        P("wide"),
        P(None, "wide"),
        P("wide"),
        P("wide", None),
        P("wide"),
        P("wide"),
        P("wide"),
    )
    return jax.shard_map(
        partial(body, (narrow, wide) == (2, 16), wide, narrow * wide),
        mesh=mesh,
        in_specs=placed,
        out_specs=(
            P(both, None, None),
            P(),
            P(None, both),
            P(both),
            P(None, None, both),
            P(None, both),
            P(both, None),
            P(both),
            P(None, both),
            P(None, both),
            P(both),
            P(both),
            P(None, both),
            P(both),
            P(both, None),
            P(both),
            P(both),
            P(both),
            P(None, both),
            P(both),
            P(both, None),
            P(both),
            P(both),
            P(both),
        ),
        check_vma=False,
    )
```

time: 1320 us -> 886 us (0.67)
  waiting for transfers between devices: 512 us -> 308 us
  blocking collectives: 92.6 us -> 0 us
  matrix products: 73.3 us -> 28 us
  local copies, waits for them, and re-layouts: 133 us -> 97.3 us
  other arithmetic: 127 us -> 96.5 us
  starting transfers between devices: 97.5 us -> 76.4 us
  between operations: 18.5 us -> 5.2 us
    unnamed x3 -> x0, waiting for transfers between devices: 116 us -> none
    all_gather x2 -> x0, blocking collectives: 92.6 us -> none  [the longest x1 51 us: body(): lax.all_gather(jnp.pad(jnp.concatenate([conv_weight, conv_bias[None]], ax...]
    ppermute x142 -> x127, waiting for transfers between devices: 396 us -> 308 us  [the longest x90 292 us: send(): return lax.ppermute(value, 'wide', LINKS[link])]
    pallas_call x5 -> x7, Pallas kernels: 55.1 us -> 103 us  [the longest x1 31.6 us: conv_backward(): pl.pallas_call(conv_backward_kernel, out_shape=(jax.ShapeDtypeStruct((fil...]
    unnamed x499 -> x422, local copies, waits for them, and re-layouts: 77.5 us -> 46.8 us
    dot_general x5 -> x3, matrix products: 39.1 us -> 9.57 us  [dot_nt(): lax.dot_general(left, right, (((1,), (1,)), ((), ())), preferred_element_...]
    convert_element_type x61 -> x29, other arithmetic: 65.3 us -> 39.7 us  [the longest x14 21.3 us: step(): sent = total_of(self.pick(self.all_terms(), 1 - index, axis)).astype(BF16)]
    ppermute x142 -> x127, starting transfers between devices: 97.4 us -> 76.4 us  [the longest x90 69.8 us: send(): return lax.ppermute(value, 'wide', LINKS[link])]
  transfers between devices with their start and end apart: 144 -> 127, of which waited for: 59 -> 53; matrix products, arithmetic and copies ran while one was open for 16% -> 10% of each run, Pallas kernels for 12% -> 22%
where the time goes in v2:
time: 886 us; the launch traced here: 876 us
  waiting for transfers between devices  308 us (35%)
  Pallas kernels  264 us (30%)
  local copies, waits for them, and re-layouts  97.3 us (11%)
  other arithmetic  96.5 us (11%)
  starting transfers between devices  76.4 us (9%)
  matrix products  28 us (3%)
    ppermute x90, waiting for transfers between devices, send(): return lax.ppermute(value, 'wide', LINKS[link])  292 us
    ppermute x90, starting transfers between devices, send(): return lax.ppermute(value, 'wide', LINKS[link])  69.8 us
    unnamed x422, local copies, waits for them, and re-layouts  46.8 us
    pallas_call x2, Pallas kernels, highway_backward(): pl.pallas_call(partial(highway_backward_kernel, layout), grid_spec=pltpu....  43 us
    pallas_call x2, Pallas kernels, highway_forward(): pl.pallas_call(partial(highway_forward_kernel, layout), grid_spec=pltpu.P...  39 us
    pallas_call x10, Pallas kernels, highway_weight_gradient(): pl.pallas_call(weight_kernel, grid_spec=pltpu.PrefetchScalarGridSpec(num_...  36.4 us
    pallas_call x1, Pallas kernels, conv_backward(): pl.pallas_call(conv_backward_kernel, out_shape=(jax.ShapeDtypeStruct((fil...  31.6 us
    pallas_call x1, Pallas kernels, feed_forward_back(): pl.pallas_call(partial(feed_forward_back_kernel, len(up)), grid_spec=pltp...  26.6 us
  transfers between devices with their start and end apart: 127, of which 53 were waited for; matrix products, arithmetic and copies ran while one was open for 10% of the time, Pallas kernels for 22%

profile of v2, /device:TPU:0, one launch (start us, length us, event | category | flops | bytes accessed | tf_op | source)
XLA Modules:
  0.0 875.7 jit_solution(8514580606566449682)
XLA Ops:
  35.3 7.7 collective-permute-done.7
  47.2 18.3 %collective-permute-done.12 = bf16[512,256]{1,0:T(8,128)(2,1)} collective-permute-done((bf16[512,256]{1,0:T(8,128)(2,1)S(1)}, bf16[512,256]{1,0:T(8,128)(2,1)}, u32[]{:S(2)}, u32[]{:S(2)}) %collective-permute-start.12) | collective-permute-done | bytes 262176 | tf_op jit(solution)/shard_map/ppermute | solution.py:644
  68.5 8.3 collective-permute-done.14
  76.9 7.6 collective-permute-done.15.refs_3_
  105.2 7.3 conv_forward.2.kept_ref
  136.3 7.3 conv_forward.3.h_ref
  143.7 14.8 %collective-permute-done.32.refs_1_ = bf16[4,160,768]{2,1,0:T(8,128)(2,1)S(1)} collective-permute-done((bf16[4,160,768]{2,1,0:T(8,128)(2,1)S(1)}, bf16[4,160,768]{2,1,0:T(8,128)(2,1)S(1)}, u32[]{:S(2)}, u32[]{:S(2)}) %collective-permute-start.32) | collective-permute-done | bytes 983072 | tf_op jit(solution)/shard_map/ppermute | solution.py:644
  164.8 9.7 %collective-permute-done.27 = bf16[512,256]{1,0:T(8,128)(2,1)S(1)} collective-permute-done((bf16[512,256]{1,0:T(8,128)(2,1)S(1)}, bf16[512,256]{1,0:T(8,128)(2,1)S(1)}, u32[]{:S(2)}, u32[]{:S(2)}) %collective-permute-start.27) | collective-permute-done | bytes 262176 | tf_op jit(solution)/shard_map/ppermute | solution.py:644
  174.6 9.2 %collective-permute-done.28 = bf16[512,256]{1,0:T(8,128)(2,1)S(1)} collective-permute-done((bf16[512,256]{1,0:T(8,128)(2,1)S(1)}, bf16[512,256]{1,0:T(8,128)(2,1)S(1)}, u32[]{:S(2)}, u32[]{:S(2)}) %collective-permute-start.28) | collective-permute-done | bytes 262176 | tf_op jit(solution)/shard_map/ppermute | solution.py:644
  183.8 8.3 collective-permute-done.29
  198.0 19.5 %highway_forward.2 = (f32[512,2048]{1,0:T(8,128)}, f32[512,2048]{1,0:T(8,128)}, f32[512,2048]{1,0:T(8,128)}, bf16[512,2048]{1,0:T(8,128)(2,1)}) custom-call(s32[8]{0:T(128)} %get-tuple-element.944.place_ref, s32[8]{0:T(128)} %get-tuple-element.943.select_ref, s32[1]{0:T(128)} %bitcast.core_ref.which_ref, f32[512,2048]{1,0:T(8,128)} %copy-done.20, ...), custom_call_target="tpu_custom_call" | custom-call | flops 20899999744 | bytes 57000000 | tf_op jit(solution)/shard_map/highway_forward/pallas_call | solution.py:396
  235.7 19.7 %collective-permute-done.47.refs_3_ = bf16[4,160,768]{2,1,0:T(8,128)(2,1)} collective-permute-done((bf16[4,160,768]{2,1,0:T(8,128)(2,1)}, bf16[4,160,768]{2,1,0:T(8,128)(2,1)}, u32[]{:S(2)}, u32[]{:S(2)}) %collective-permute-start.47) | collective-permute-done | bytes 983072 | tf_op jit(solution)/shard_map/ppermute | solution.py:644
  256.3 7.7 collective-permute-done.56
  274.8 7.3 place_rows.1
  286.3 19.5 %highway_forward.3 = (f32[512,2048]{1,0:T(8,128)}, f32[512,2048]{1,0:T(8,128)}, f32[512,2048]{1,0:T(8,128)}, bf16[512,2048]{1,0:T(8,128)(2,1)}) custom-call(s32[8]{0:T(128)} %get-tuple-element.944.place_ref, s32[8]{0:T(128)} %get-tuple-element.943.select_ref, s32[1]{0:T(128)} %bitcast.core_ref.which_ref, f32[512,2048]{1,0:T(8,128)} %get-tuple-element.544.h_ref, ...), custom_call_target="tpu_custom_call" | custom-call | flops 20899999744 | bytes 57000000 | tf_op jit(solution)/shard_map/highway_forward/pallas_call | solution.py:396
  325.4 11.1 %attend.1 = bf16[512,768]{1,0:T(8,128)(2,1)S(1)} custom-call(bf16[512,2304]{1,0:T(8,128)(2,1)S(1)} %fusion.query_ref.key_ref.value_ref, bf16[512,2304]{1,0:T(8,128)(2,1)S(1)} %fusion.query_ref.key_ref.value_ref, bf16[512,2304]{1,0:T(8,128)(2,1)S(1)} %fusion.query_ref.key_ref.value_ref), custom_call_target="tpu_custom_call" | custom-call | flops 13200000000 | bytes 36000000 | tf_op jit(solution)/shard_map/attend/pallas_call | solution.py:1240
  337.9 8.8 %collective-permute-done.64.refs_9_ = bf16[4,96,768]{2,1,0:T(8,128)(2,1)} collective-permute-done((bf16[4,96,768]{2,1,0:T(8,128)(2,1)S(1)}, bf16[4,96,768]{2,1,0:T(8,128)(2,1)}, u32[]{:S(2)}, u32[]{:S(2)}) %collective-permute-start.64) | collective-permute-done | bytes 589856 | tf_op jit(solution)/shard_map/ppermute | solution.py:644
  363.2 8.3 collective-permute-done.68.refs_3_
  376.7 23.8 %feed_forward.1 = (bf16[8,512,384]{2,1,0:T(8,128)(2,1)}, bf16[8,512,384]{2,1,0:T(8,128)(2,1)}, bf16[512,768]{1,0:T(8,128)(2,1)}, f32[512,768]{1,0:T(8,128)}, f32[8,768]{1,0:T(8,128)S(1)}) custom-call(s32[8,2]{1,0:T(8,128)S(1)} %add_select_fusion.slot_ref, s32[8]{0:T(128)S(1)} %add_add_fusion.2.block_ref, s32[1]{0:T(128)} %bitcast.core_ref.which_ref, ...), custom_call_target="tpu_custom_call" | custom-call | flops 22000001024 | bytes 60000000 | tf_op jit(solution)/shard_map/feed_forward/pallas_call | solution.py:1046
  400.5 26.6 %feed_forward_back.1 = (bf16[2,4,2,96,768]{4,3,2,1,0:T(8,128)(2,1)}, bf16[2,4,2,96,768]{4,3,2,1,0:T(8,128)(2,1)}, bf16[2,4,2,96,768]{4,3,2,1,0:T(8,128)(2,1)}, b...) custom-call(s32[8,2]{1,0:T(8,128)S(1)} %add_select_fusion.slot_ref, ...), custom_call_target="tpu_custom_call" | custom-call | flops 27499999232 | bytes 75000000 | tf_op jit(solution)/shard_map/feed_forward_back/pallas_call | solution.py:1171
  432.1 16.8 %attend_back.1 = (bf16[512,768]{1,0:T(8,128)(2,1)S(1)}, bf16[512,768]{1,0:T(8,128)(2,1)S(1)}, bf16[512,768]{1,0:T(8,128)(2,1)S(1)}) custom-call(bf16[512,2304]{1,0:T(8,128)(2,1)S(1)} %copy-done.61, bf16[512,2304]{1,0:T(8,128)(2,1)S(1)} %copy-done.61, bf16[512,2304]{1,0:T(8,128)(2,1)S(1)} %copy-done.61, bf16[512,768]{1,0:T(8,128)(2,1)S(1)} %convolution_convert_fusion.4.grad_ref), custom_call_target="tpu_custom_call" | custom-call | flops 18699999232 | bytes 51000000 | tf_op jit(solution)/shard_map/attend_back/pallas_call | solution.py:1275
  488.0 14.4 %collective-permute-done.78 = bf16[4,2,96,768]{3,2,1,0:T(8,128)(2,1)} collective-permute-done((bf16[4,2,96,768]{3,2,1,0:T(8,128)(2,1)}, bf16[4,2,96,768]{3,2,1,0:T(8,128)(2,1)}, u32[]{:S(2)}, u32[]{:S(2)}) %collective-permute-start.78) | collective-permute-done | bytes 1179680 | tf_op jit(solution)/shard_map/ppermute | solution.py:644
  510.0 21.6 %highway_backward.2 = (bf16[2,512,2048]{2,1,0:T(8,128)(2,1)}, f32[2,1,2048]{2,1,0:T(1,128)}, f32[512,2048]{1,0:T(8,128)}) custom-call(s32[8]{0:T(128)} %get-tuple-element.944.place_ref, s32[8]{0:T(128)} %get-tuple-element.943.select_ref, s32[1]{0:T(128)} %bitcast.core_ref.which_ref, f32[512,2048]{1,0:T(8,128)} %fusion.22.grad_ref, ...), custom_call_target="tpu_custom_call" | custom-call | flops 23100000256 | bytes 63000000 | tf_op jit(solution)/shard_map/highway_backward/pallas_call | solution.py:460
  547.8 21.4 %highway_backward.3 = (bf16[2,512,2048]{2,1,0:T(8,128)(2,1)}, f32[2,1,2048]{2,1,0:T(1,128)}, f32[512,2048]{1,0:T(8,128)}) custom-call(s32[8]{0:T(128)} %get-tuple-element.944.place_ref, s32[8]{0:T(128)} %get-tuple-element.943.select_ref, s32[1]{0:T(128)} %bitcast.core_ref.which_ref, f32[512,2048]{1,0:T(8,128)} %get-tuple-element.667.grad_ref, ...), custom_call_target="tpu_custom_call" | custom-call | flops 23100000256 | bytes 63000000 | tf_op jit(solution)/shard_map/highway_backward/pallas_call | solution.py:460
  614.6 31.6 %conv_backward.1 = (bf16[2048,128]{1,0:T(8,128)(2,1)S(1)}, f32[8,512,128]{2,1,0:T(8,128)S(1)}) custom-call(s32[8]{0:T(128)S(1)} %copy-done.53, s32[816]{0:T(1024)S(1)} %copy-done.35, s32[816]{0:T(1024)S(1)} %copy-done.37, bf16[8,512,128]{2,1,0:T(8,128)(2,1)S(1)} %copy-done.64, bf16[128,2048]{1,0:T(8,128)(2,1)S(1)} %copy-done.29, s32[512,1]{1,0:T(8,128)S(1)} %copy-done.33, ...), custom_call_target="tpu_custom_call" | custom-call | flops 38499999744 | bytes 105000000 | tf_op jit(solution)/shard_map/conv_backward/pallas_call | solution.py:243
  646.2 7.8 collective-permute-done.88
  681.0 12.8 %collective-permute-done.95 = bf16[192,768]{1,0:T(8,128)(2,1)S(1)} collective-permute-done((bf16[192,768]{1,0:T(8,128)(2,1)S(1)}, bf16[192,768]{1,0:T(8,128)(2,1)S(1)}, u32[]{:S(2)}, u32[]{:S(2)}) %collective-permute-start.95) | collective-permute-done | bytes 294944 | tf_op jit(solution)/shard_map/ppermute | solution.py:644
  716.6 7.4 collective-permute-done.96
  732.7 28.6 %collective-permute-done.101 = bf16[4,512,128]{2,1,0:T(8,128)(2,1)S(1)} collective-permute-done((bf16[4,512,128]{2,1,0:T(8,128)(2,1)S(1)}, bf16[4,512,128]{2,1,0:T(8,128)(2,1)S(1)}, u32[]{:S(2)}, u32[]{:S(2)}) %collective-permute-start.101) | collective-permute-done | bytes 524320 | tf_op jit(solution)/shard_map/ppermute | solution.py:644
  776.0 12.7 %collective-permute-done.106 = bf16[1024,128]{1,0:T(8,128)(2,1)} collective-permute-done((bf16[1024,128]{1,0:T(8,128)(2,1)}, bf16[1024,128]{1,0:T(8,128)(2,1)}, u32[]{:S(2)}, u32[]{:S(2)}) %collective-permute-start.106) | collective-permute-done | bytes 262176 | tf_op jit(solution)/shard_map/ppermute | solution.py:644
  827.7 9.6 %collective-permute-done.120 = bf16[64,128]{1,0:T(8,128)(2,1)S(1)} collective-permute-done((bf16[64,128]{1,0:T(8,128)(2,1)S(1)}, bf16[64,128]{1,0:T(8,128)(2,1)S(1)}, u32[]{:S(2)}, u32[]{:S(2)}) %collective-permute-start.120) | collective-permute-done | bytes 16416 | tf_op jit(solution)/shard_map/ppermute | solution.py:644
  841.6 10.1 %collective-permute-done.123 = bf16[64,128]{1,0:T(8,128)(2,1)S(1)} collective-permute-done((bf16[64,128]{1,0:T(8,128)(2,1)S(1)}, bf16[64,128]{1,0:T(8,128)(2,1)S(1)}, u32[]{:S(2)}, u32[]{:S(2)}) %collective-permute-start.123) | collective-permute-done | bytes 16416 | tf_op jit(solution)/shard_map/ppermute | solution.py:644
  (928 shorter events, 425.0 us)
Async XLA Ops:
  45.2 44.5 %collective-permute-start.10 = (bf16[4,512,256]{2,1,0:T(8,128)(2,1)}, bf16[4,512,256]{2,1,0:T(8,128)(2,1)}, u32[]{:S(2)}, u32[]{:S(2)}) collective-permute-start(bf16[4,512,256]{2,1,0:T(8,128)(2,1)} %pad_maximum_fusion.4), channel_id=1, source_target_pairs={{0,1},{1,0},{2,3},{3,2},{4,5},{5,4},{6,7},{7,6},{8,9},{9,8},{10,11... | collective-permute-start | bytes 3145736 | tf_op jit(solution)/shard_map/ppermute | solution.py:644
  46.6 43.0 %collective-permute-start.11 = (bf16[4,512,256]{2,1,0:T(8,128)(2,1)}, bf16[4,512,256]{2,1,0:T(8,128)(2,1)}, u32[]{:S(2)}, u32[]{:S(2)}) collective-permute-start(bf16[4,512,256]{2,1,0:T(8,128)(2,1)} %pad_maximum_fusion.4), channel_id=1, source_target_pairs={{0,2},{1,3},{2,0},{3,1},{4,6},{5,7},{6,4},{7,5},{8,10},{9,11},{10,... | collective-permute-start | bytes 3145736 | tf_op jit(solution)/shard_map/ppermute | solution.py:644
  47.2 42.5 %collective-permute-start.22 = (bf16[4,512,256]{2,1,0:T(8,128)(2,1)}, bf16[4,512,256]{2,1,0:T(8,128)(2,1)}, u32[]{:S(2)}, u32[]{:S(2)}) collective-permute-start(bf16[4,512,256]{2,1,0:T(8,128)(2,1)} %pad_maximum_fusion.4), channel_id=1, source_target_pairs={{0,16},{16,0},{1,17},{17,1},{2,18},{18,2},{3,19},{19,3},{4,20},{20... | collective-permute-start | bytes 3145736 | tf_op jit(solution)/shard_map/ppermute | solution.py:643
  91.9 35.6 %collective-permute-start.33 = (bf16[4,512,256]{2,1,0:T(8,128)(2,1)}, bf16[4,512,256]{2,1,0:T(8,128)(2,1)}, u32[]{:S(2)}, u32[]{:S(2)}) collective-permute-start(bf16[4,512,256]{2,1,0:T(8,128)(2,1)} %pad_maximum_fusion.5), channel_id=1, source_target_pairs={{0,16},{16,0},{1,17},{17,1},{2,18},{18,2},{3,19},{19,3},{4,20},{20... | collective-permute-start | bytes 3145736 | tf_op jit(solution)/shard_map/ppermute | solution.py:643
  92.7 34.8 %collective-permute-start.17 = (bf16[4,512,256]{2,1,0:T(8,128)(2,1)}, bf16[4,512,256]{2,1,0:T(8,128)(2,1)}, u32[]{:S(2)}, u32[]{:S(2)}) collective-permute-start(bf16[4,512,256]{2,1,0:T(8,128)(2,1)} %pad_maximum_fusion.5), channel_id=1, source_target_pairs={{0,1},{1,0},{2,3},{3,2},{4,5},{5,4},{6,7},{7,6},{8,9},{9,8},{10,11... | collective-permute-start | bytes 3145736 | tf_op jit(solution)/shard_map/ppermute | solution.py:644
  93.3 34.2 %collective-permute-start.18 = (bf16[4,512,256]{2,1,0:T(8,128)(2,1)}, bf16[4,512,256]{2,1,0:T(8,128)(2,1)}, u32[]{:S(2)}, u32[]{:S(2)}) collective-permute-start(bf16[4,512,256]{2,1,0:T(8,128)(2,1)} %pad_maximum_fusion.5), channel_id=1, source_target_pairs={{0,2},{1,3},{2,0},{3,1},{4,6},{5,7},{6,4},{7,5},{8,10},{9,11},{10,... | collective-permute-start | bytes 3145736 | tf_op jit(solution)/shard_map/ppermute | solution.py:644
  129.9 28.6 %collective-permute-start.30 = (bf16[4,512,256]{2,1,0:T(8,128)(2,1)}, bf16[4,512,256]{2,1,0:T(8,128)(2,1)S(1)}, u32[]{:S(2)}, u32[]{:S(2)}) collective-permute-start(bf16[4,512,256]{2,1,0:T(8,128)(2,1)} %collective-permute-done.10), channel_id=1, source_target_pairs={{0,2},{1,3},{2,0},{3,1},{4,6},{5,7},{6,4},{7,5},{8,10},{9,11},{10,... | collective-permute-start | bytes 3145736 | tf_op jit(solution)/shard_map/ppermute | solution.py:644
  161.6 30.5 %collective-permute-start.25 = (bf16[4,512,256]{2,1,0:T(8,128)(2,1)S(1)}, bf16[4,512,256]{2,1,0:T(8,128)(2,1)}, u32[]{:S(2)}, u32[]{:S(2)}) collective-permute-start(bf16[4,512,256]{2,1,0:T(8,128)(2,1)S(1)} %pad_maximum_fusion.6), channel_id=1, source_target_pairs={{0,1},{1,0},{2,3},{3,2},{4,5},{5,4},{6,7},{7,6},{8,9},{9,8},{10,11... | collective-permute-start | bytes 3145736 | tf_op jit(solution)/shard_map/ppermute | solution.py:644
  162.1 30.1 %collective-permute-start.26 = (bf16[4,512,256]{2,1,0:T(8,128)(2,1)S(1)}, bf16[4,512,256]{2,1,0:T(8,128)(2,1)S(1)}, u32[]{:S(2)}, u32[]{:S(2)}) collective-permute-start(bf16[4,512,256]{2,1,0:T(8,128)(2,1)S(1)} %pad_maximum_fusion.6), channel_id=1, source_target_pairs={{0,2},{1,3},{2,0},{3,1},{4,6},{5,7},{6,4},{7,5},{8,10},{9,11},{10,... | collective-permute-start | bytes 3145736 | tf_op jit(solution)/shard_map/ppermute | solution.py:644
  164.0 28.2 %collective-permute-start.42 = (bf16[4,512,256]{2,1,0:T(8,128)(2,1)S(1)}, bf16[4,512,256]{2,1,0:T(8,128)(2,1)S(1)}, u32[]{:S(2)}, u32[]{:S(2)}) collective-permute-start(bf16[4,512,256]{2,1,0:T(8,128)(2,1)S(1)} %pad_maximum_fusion.6), channel_id=1, source_target_pairs={{0,16},{16,0},{1,17},{17,1},{2,18},{18,2},{3,19},{19,3},{4,20},{20... | collective-permute-start | bytes 3145736 | tf_op jit(solution)/shard_map/ppermute | solution.py:643
  164.0 28.2 %collective-permute-start.38 = (bf16[4,160,768]{2,1,0:T(8,128)(2,1)S(1)}, bf16[4,160,768]{2,1,0:T(8,128)(2,1)S(1)}, u32[]{:S(2)}, u32[]{:S(2)}) collective-permute-start(bf16[4,160,768]{2,1,0:T(8,128)(2,1)S(1)} %pad_maximum_fusion.8.refs_0_), channel_id=1, source_target_pairs={{0,16},{16,0},{1,17},{17,1},{2,18},{18,2},{3,19},{19,3},{4,20},{20... | collective-permute-start | bytes 2949128 | tf_op jit(solution)/shard_map/ppermute | solution.py:643
  193.9 28.5 %collective-permute-start.48 = (bf16[4,512,256]{2,1,0:T(8,128)(2,1)S(1)}, bf16[4,512,256]{2,1,0:T(8,128)(2,1)}, u32[]{:S(2)}, u32[]{:S(2)}) collective-permute-start(bf16[4,512,256]{2,1,0:T(8,128)(2,1)S(1)} %pad_maximum_fusion.7), channel_id=1, source_target_pairs={{0,16},{16,0},{1,17},{17,1},{2,18},{18,2},{3,19},{19,3},{4,20},{20... | collective-permute-start | bytes 3145736 | tf_op jit(solution)/shard_map/ppermute | solution.py:643
  194.1 28.3 %collective-permute-start.39 = (bf16[4,512,256]{2,1,0:T(8,128)(2,1)S(1)}, bf16[4,512,256]{2,1,0:T(8,128)(2,1)}, u32[]{:S(2)}, u32[]{:S(2)}) collective-permute-start(bf16[4,512,256]{2,1,0:T(8,128)(2,1)S(1)} %pad_maximum_fusion.7), channel_id=1, source_target_pairs={{0,1},{1,0},{2,3},{3,2},{4,5},{5,4},{6,7},{7,6},{8,9},{9,8},{10,11... | collective-permute-start | bytes 3145736 | tf_op jit(solution)/shard_map/ppermute | solution.py:644
  255.7 29.2 %collective-permute-start.53 = (bf16[4,512,256]{2,1,0:T(8,128)(2,1)}, bf16[4,512,256]{2,1,0:T(8,128)(2,1)S(1)}, u32[]{:S(2)}, u32[]{:S(2)}) collective-permute-start(bf16[4,512,256]{2,1,0:T(8,128)(2,1)} %collective-permute-done.45), channel_id=1, source_target_pairs={{0,16},{16,0},{1,17},{17,1},{2,18},{18,2},{3,19},{19,3},{4,20},{20... | collective-permute-start | bytes 3145736 | tf_op jit(solution)/shard_map/ppermute | solution.py:643
  256.2 28.8 %collective-permute-start.54 = (bf16[4,512,256]{2,1,0:T(8,128)(2,1)}, bf16[4,512,256]{2,1,0:T(8,128)(2,1)S(1)}, u32[]{:S(2)}, u32[]{:S(2)}) collective-permute-start(bf16[4,512,256]{2,1,0:T(8,128)(2,1)} %collective-permute-done.46), channel_id=1, source_target_pairs={{0,16},{16,0},{1,17},{17,1},{2,18},{18,2},{3,19},{19,3},{4,20},{20... | collective-permute-start | bytes 3145736 | tf_op jit(solution)/shard_map/ppermute | solution.py:643
  271.2 44.4 %collective-permute-start.60 = (bf16[96,768]{1,0:T(8,128)(2,1)}, bf16[96,768]{1,0:T(8,128)(2,1)}, u32[]{:S(2)}, u32[]{:S(2)}) collective-permute-start(bf16[96,768]{1,0:T(8,128)(2,1)} %collective-permute-done.58), channel_id=1, source_target_pairs={{0,4},{1,5},{2,6},{3,7},{4,8},{5,9},{6,10},{7,11},{8,12},{9,13},{1... | collective-permute-start | bytes 442376 | tf_op jit(solution)/shard_map/ppermute | solution.py:644
  274.5 41.0 %collective-permute-start.61 = (bf16[96,768]{1,0:T(8,128)(2,1)}, bf16[96,768]{1,0:T(8,128)(2,1)}, u32[]{:S(2)}, u32[]{:S(2)}) collective-permute-start(bf16[96,768]{1,0:T(8,128)(2,1)} %collective-permute-done.59), channel_id=1, source_target_pairs={{0,4},{1,5},{2,6},{3,7},{4,8},{5,9},{6,10},{7,11},{8,12},{9,13},{1... | collective-permute-start | bytes 442376 | tf_op jit(solution)/shard_map/ppermute | solution.py:644
  474.0 28.4 %collective-permute-start.78 = (bf16[4,2,96,768]{3,2,1,0:T(8,128)(2,1)}, bf16[4,2,96,768]{3,2,1,0:T(8,128)(2,1)}, u32[]{:S(2)}, u32[]{:S(2)}) collective-permute-start(bf16[4,2,96,768]{3,2,1,0:T(8,128)(2,1)} %fusion.6), channel_id=1, source_target_pairs={{0,2},{1,3},{2,0},{3,1},{4,6},{5,7},{6,4},{7,5},{8,10},{9,11},{10,... | collective-permute-start | bytes 3538952 | tf_op jit(solution)/shard_map/ppermute | solution.py:644
  474.4 28.1 %collective-permute-start.79 = (bf16[4,2,96,768]{3,2,1,0:T(8,128)(2,1)}, bf16[4,2,96,768]{3,2,1,0:T(8,128)(2,1)}, u32[]{:S(2)}, u32[]{:S(2)}) collective-permute-start(bf16[4,2,96,768]{3,2,1,0:T(8,128)(2,1)} %fusion.7), channel_id=1, source_target_pairs={{0,1},{1,0},{2,3},{3,2},{4,5},{5,4},{6,7},{7,6},{8,9},{9,8},{10,11... | collective-permute-start | bytes 3538952 | tf_op jit(solution)/shard_map/ppermute | solution.py:644
  601.8 52.3 %collective-permute-start.86 = (bf16[16,1024,128]{2,1,0:T(8,128)(2,1)}, bf16[16,1024,128]{2,1,0:T(8,128)(2,1)}, u32[]{:S(2)}, u32[]{:S(2)}) collective-permute-start(bf16[16,1024,128]{2,1,0:T(8,128)(2,1)} %highway_weight.13), channel_id=1, source_target_pairs={{0,16},{16,0},{1,17},{17,1},{2,18},{18,2},{3,19},{19,3},{4,20},{20... | collective-permute-start | bytes 12582920 | tf_op jit(solution)/shard_map/ppermute | solution.py:643
  602.2 51.9 %collective-permute-start.87 = (bf16[16,1024,128]{2,1,0:T(8,128)(2,1)}, bf16[16,1024,128]{2,1,0:T(8,128)(2,1)}, u32[]{:S(2)}, u32[]{:S(2)}) collective-permute-start(bf16[16,1024,128]{2,1,0:T(8,128)(2,1)} %highway_weight.14), channel_id=1, source_target_pairs={{0,16},{16,0},{1,17},{17,1},{2,18},{18,2},{3,19},{19,3},{4,20},{20... | collective-permute-start | bytes 12582920 | tf_op jit(solution)/shard_map/ppermute | solution.py:643
  606.3 47.7 %collective-permute-start.88 = (bf16[4,2,1024,128]{3,2,1,0:T(8,128)(2,1)}, bf16[4,2,1024,128]{3,2,1,0:T(8,128)(2,1)S(1)}, u32[]{:S(2)}, u32[]{:S(2)}) collective-permute-start(bf16[4,2,1024,128]{3,2,1,0:T(8,128)(2,1)} %dynamic-slice_bitcast_fusion.1), channel_id=1, source_target_pairs={{0,2},{1,3},{2,0},{3,1},{4,6},{5,7},{6,4},{7,5},{8,10},{9,11},{10,... | collective-permute-start | bytes 6291464 | tf_op jit(solution)/shard_map/ppermute | solution.py:644
  606.7 47.3 %collective-permute-start.89 = (bf16[4,2,1024,128]{3,2,1,0:T(8,128)(2,1)}, bf16[4,2,1024,128]{3,2,1,0:T(8,128)(2,1)S(1)}, u32[]{:S(2)}, u32[]{:S(2)}) collective-permute-start(bf16[4,2,1024,128]{3,2,1,0:T(8,128)(2,1)} %dynamic-slice_bitcast_fusion), channel_id=1, source_target_pairs={{0,1},{1,0},{2,3},{3,2},{4,5},{5,4},{6,7},{7,6},{8,9},{9,8},{10,11... | collective-permute-start | bytes 6291464 | tf_op jit(solution)/shard_map/ppermute | solution.py:644
  614.1 32.0 %collective-permute-start.90 = (bf16[2,2,176,768]{3,2,1,0:T(8,128)(2,1)S(1)}, bf16[2,2,176,768]{3,2,1,0:T(8,128)(2,1)}, u32[]{:S(2)}, u32[]{:S(2)}) collective-permute-start(bf16[2,2,176,768]{3,2,1,0:T(8,128)(2,1)S(1)} %copy-done.93), channel_id=1, source_target_pairs={{0,4},{1,5},{2,6},{3,7},{4,8},{5,9},{6,10},{7,11},{8,12},{9,13},{1... | collective-permute-start | bytes 3244040 | tf_op jit(solution)/shard_map/ppermute | solution.py:644
  660.8 33.0 %collective-permute-start.94 = (bf16[2,2,176,768]{3,2,1,0:T(8,128)(2,1)S(1)}, bf16[2,2,176,768]{3,2,1,0:T(8,128)(2,1)S(1)}, u32[]{:S(2)}, u32[]{:S(2)}) collective-permute-start(bf16[2,2,176,768]{3,2,1,0:T(8,128)(2,1)S(1)} %fusion.2), channel_id=1, source_target_pairs={{0,4},{1,5},{2,6},{3,7},{4,8},{5,9},{6,10},{7,11},{8,12},{9,13},{1... | collective-permute-start | bytes 3244040 | tf_op jit(solution)/shard_map/ppermute | solution.py:644
  664.1 29.6 %collective-permute-start.92 = (bf16[4,1024,128]{2,1,0:T(8,128)(2,1)S(1)}, bf16[4,1024,128]{2,1,0:T(8,128)(2,1)S(1)}, u32[]{:S(2)}, u32[]{:S(2)}) collective-permute-start(bf16[4,1024,128]{2,1,0:T(8,128)(2,1)S(1)} %fusion.4), channel_id=1, source_target_pairs={{0,1},{1,0},{2,3},{3,2},{4,5},{5,4},{6,7},{7,6},{8,9},{9,8},{10,11... | collective-permute-start | bytes 3145736 | tf_op jit(solution)/shard_map/ppermute | solution.py:644
  665.1 28.7 %collective-permute-start.93 = (bf16[4,1024,128]{2,1,0:T(8,128)(2,1)S(1)}, bf16[4,1024,128]{2,1,0:T(8,128)(2,1)S(1)}, u32[]{:S(2)}, u32[]{:S(2)}) collective-permute-start(bf16[4,1024,128]{2,1,0:T(8,128)(2,1)S(1)} %fusion.3), channel_id=1, source_target_pairs={{0,2},{1,3},{2,0},{3,1},{4,6},{5,7},{6,4},{7,5},{8,10},{9,11},{10,... | collective-permute-start | bytes 3145736 | tf_op jit(solution)/shard_map/ppermute | solution.py:644
  727.7 34.2 %collective-permute-start.100 = (bf16[4,2,512,128]{3,2,1,0:T(8,128)(2,1)S(1)}, bf16[4,2,512,128]{3,2,1,0:T(8,128)(2,1)S(1)}, u32[]{:S(2)}, u32[]{:S(2)}) collective-permute-start(bf16[4,2,512,128]{3,2,1,0:T(8,128)(2,1)S(1)} %dynamic-slice_bitcast_fusion.4), channel_id=1, source_target_pairs={{0,1},{1,0},{2,3},{3,2},{4,5},{5,4},{6,7},{7,6},{8,9},{9,8},{10,11... | collective-permute-start | bytes 3145736 | tf_op jit(solution)/shard_map/ppermute | solution.py:644
  728.7 33.2 %collective-permute-start.99 = (bf16[4,2,512,128]{3,2,1,0:T(8,128)(2,1)S(1)}, bf16[4,2,512,128]{3,2,1,0:T(8,128)(2,1)S(1)}, u32[]{:S(2)}, u32[]{:S(2)}) collective-permute-start(bf16[4,2,512,128]{3,2,1,0:T(8,128)(2,1)S(1)} %dynamic-slice_bitcast_fusion.5), channel_id=1, source_target_pairs={{0,2},{1,3},{2,0},{3,1},{4,6},{5,7},{6,4},{7,5},{8,10},{9,11},{10,... | collective-permute-start | bytes 3145736 | tf_op jit(solution)/shard_map/ppermute | solution.py:644
  729.2 32.1 %collective-permute-start.101 = (bf16[4,512,128]{2,1,0:T(8,128)(2,1)S(1)}, bf16[4,512,128]{2,1,0:T(8,128)(2,1)S(1)}, u32[]{:S(2)}, u32[]{:S(2)}) collective-permute-start(bf16[4,512,128]{2,1,0:T(8,128)(2,1)S(1)} %fusion.18), channel_id=1, source_target_pairs={{0,1},{1,0},{2,3},{3,2},{4,5},{5,4},{6,7},{7,6},{8,9},{9,8},{10,11... | collective-permute-start | bytes 1572872 | tf_op jit(solution)/shard_map/ppermute | solution.py:644
  730.3 31.6 %collective-permute-start.102 = (bf16[4,512,128]{2,1,0:T(8,128)(2,1)S(1)}, bf16[4,512,128]{2,1,0:T(8,128)(2,1)S(1)}, u32[]{:S(2)}, u32[]{:S(2)}) collective-permute-start(bf16[4,512,128]{2,1,0:T(8,128)(2,1)S(1)} %fusion.17), channel_id=1, source_target_pairs={{0,2},{1,3},{2,0},{3,1},{4,6},{5,7},{6,4},{7,5},{8,10},{9,11},{10,... | collective-permute-start | bytes 1572872 | tf_op jit(solution)/shard_map/ppermute | solution.py:644
  731.9 30.0 %collective-permute-start.103 = (bf16[2048,128]{1,0:T(8,128)(2,1)S(1)}, bf16[2048,128]{1,0:T(8,128)(2,1)S(1)}, u32[]{:S(2)}, u32[]{:S(2)}) collective-permute-start(bf16[2048,128]{1,0:T(8,128)(2,1)S(1)} %pad_maximum_fusion.11), channel_id=1, source_target_pairs={{0,4},{1,5},{2,6},{3,7},{4,8},{5,9},{6,10},{7,11},{8,12},{9,13},{1... | collective-permute-start | bytes 1572872 | tf_op jit(solution)/shard_map/ppermute | solution.py:644
  (296 other events, 4572.2 us)

commit v3 on v2

--- a/solution.py
+++ b/solution.py
@@ -146,7 +146,7 @@
 
 
 def conv_forward_kernel(
-    scalar_ref, tile_ref, pos_ref, g_ref, w_ref, len_ref, kept_ref, pooled_ref, x_ref, pre_ref
+    scalar_ref, tile_ref, pos_ref, g_ref, w_ref, len_ref, pooled_ref, x_ref, pre_ref
 ):
     filters = w_ref.shape[1]
     part = pre_ref.shape[1]
@@ -170,29 +170,18 @@
     pooled_ref[...] = pooled_ref[...] / len_ref[...].astype(F32)
 
 
-def conv_forward(prep, char_groups, half_matrix, pooled, first, part):
+def conv_forward(prep, char_groups, half_matrix):
     _, ids, lengths, scalars, tile, position = prep
-    words = ids.shape[0]
     return pl.pallas_call(
         conv_forward_kernel,
-        grid=(1,),
-        out_shape=jax.ShapeDtypeStruct((words, half_matrix.shape[1]), F32),
-        in_specs=[
-            SMEM,
-            SMEM,
-            SMEM,
-            VMEM,
-            pl.BlockSpec((LANES, part), lambda i: (0, first // part)),
-            VMEM,
-            pl.BlockSpec(memory_space=pl.ANY),
-        ],
-        out_specs=pl.BlockSpec((words, part), lambda i: (0, first // part)),
+        out_shape=jax.ShapeDtypeStruct((ids.shape[0], half_matrix.shape[1]), F32),
+        in_specs=[SMEM, SMEM, SMEM, VMEM, VMEM, VMEM],
+        out_specs=VMEM,
         scratch_shapes=[pltpu.VMEM((CHUNK, LANES), BF16), pltpu.VMEM((CHUNK, 512), F32)],
-        input_output_aliases={6: 0},
         compiler_params=pltpu.CompilerParams(vmem_limit_bytes=32 * MIB),
-        cost_estimate=cost(8),
+        cost_estimate=cost(16),
         name="conv_forward",
-    )(scalars, tile, position, char_groups, half_matrix, lengths[:, None], pooled)
+    )(scalars, tile, position, char_groups, half_matrix, lengths[:, None])
 
 
 def conv_backward_kernel(
@@ -632,6 +621,7 @@
     "x": [(w, w ^ 1) for w in range(16)],
     "y": [(w, w ^ 2) for w in range(16)],
     "z": [(w, (w + 4) % 16) for w in range(16)],
+    "back": [(w, (w - 4) % 16) for w in range(16)],
     "z1": [(w, w ^ 4) for w in range(16)],
     "z2": [(w, w ^ 8) for w in range(16)],
 }
@@ -732,6 +722,11 @@
 
     def ring_step(self, name, step):
         self.move(f"{name}r{step}", f"{name}r{step - 1}" if step > 1 else name, "z")
+
+    def ring_both(self, name):
+        self.put(name + "r1", send(self.state[name], "z"))
+        self.put(name + "r3", send(self.state[name], "back"))
+        self.put(name + "r2", send(self.state[name + "r1"], "z"))
 
     def ring_done(self, name):
         self.state[name + "o"] = jnp.stack(
@@ -848,8 +843,9 @@
 
 
 class Ring:
-    def __init__(self, net, sums):
-        self.net, self.sums, self.done, self.running = net, sums, 0, None
+    def __init__(self, net, sums, both):
+        self.net, self.sums, self.both, self.done = net, sums, both, 0
+        self.arrived = []
         net.count += 1
         self.name = f"ring{net.count}"
 
@@ -857,23 +853,26 @@
         index = (self.net.z + distance) % 4
         parts = [total_of(item.pick(item.all_terms(), index, 0)) for item in self.sums]
         value = parts[0] if len(parts) == 1 else jnp.concatenate(parts, axis=0)
-        if self.running is not None:
-            value = value + self.net.state[self.running].astype(F32)
+        for key in self.arrived:
+            value = value + self.net.state[key].astype(F32)
         return value
 
-    def step(self, put=None):
-        value = self.part(3 - self.done).astype(BF16)
+    def step(self, put):
         self.done += 1
         self.key = key = f"{self.name}_{self.done}"
-        if put:
-            put(key, value, "z")
+        if self.both and self.done == 1:
+            self.last_key = f"{self.name}_back"
+            put(self.last_key, self.part(3).astype(BF16), "back")
+            put(key, self.part(2).astype(BF16), "z")
         else:
-            self.net.put(key, send(value, "z"))
-        self.running = key
+            put(key, self.part((3 if self.both else 4) - self.done).astype(BF16), "z")
+        self.arrived = [key]
         return self
 
     def result(self):
-        assert self.done == 3
+        assert self.done == (2 if self.both else 3)
+        if self.both:
+            self.arrived = self.arrived + [self.last_key]
         return self.part(0)
 
 
@@ -932,53 +931,43 @@
     return grad, jnp.sum(grad_rows * normal, axis=0), jnp.sum(grad_rows, axis=0)
 
 
-def row_copies(slots, own, arrays, array, up_refs, down_refs, up_ref, down_ref, sems, buffer):
-    rows = up_refs[0].shape[1]
-    copies = []
-    for refs, whole_ref in ((up_refs, up_ref), (down_refs, down_ref)):
-        for half in range(2):
-            ref = refs[half * arrays + array]
-            for number, slot in enumerate(slots):
-                start = pl.multiple_of((own if half == 0 else 1 - own) * rows, rows)
-                copies.append(
-                    pltpu.make_async_copy(
-                        ref.at[slot],
-                        whole_ref.at[buffer, pl.ds(number * 2 * rows + start, rows), :],
-                        sems.at[buffer, len(copies)],
-                    )
-                )
-    return copies
-
-
-def fetch_rows(slot_ref, own, up_refs, down_refs, up_ref, down_ref, sems):
-    arrays = len(up_refs) // 2
+def array_copies(array, refs, held_ref, sems):
+    count = len(refs)
+    return [
+        pltpu.make_async_copy(
+            refs[index], held_ref.at[index], sems.at[index]
+        )
+        for index in range(array, count, count // 4)
+    ]
+
+
+def join_rows(slot_ref, own, refs, held_ref, up_ref, down_ref, sems):
+    count = len(refs)
+    arrays = count // 4
     step = pl.program_id(0)
-
-    def start(index):
-        for array in range(arrays):
-
-            @pl.when(index // 2 == array)
-            def _(array=array):
-                slots = [slot_ref[index, number] for number in range(2)]
-                for copy in row_copies(
-                    slots, own, arrays, array, up_refs, down_refs, up_ref, down_ref, sems, index % 2
-                ):
-                    copy.start()
 
     @pl.when(step == 0)
     def _():
-        start(0)
-
-    @pl.when(step + 1 < pl.num_programs(0))
-    def _():
-        start(step + 1)
-
-    buffer = step % 2
-    for copy in row_copies(
-        (0, 0), own, arrays, 0, up_refs, down_refs, up_ref, down_ref, sems, buffer
-    ):
-        copy.wait()
-    return buffer
+        for array in range(arrays):
+            for copy in array_copies(array, refs, held_ref, sems):
+                copy.start()
+
+    for array in range(arrays):
+
+        @pl.when(step == 2 * array)
+        def _(array=array):
+            for copy in array_copies(array, refs, held_ref, sems):
+                copy.wait()
+
+    rows = held_ref.shape[2]
+    near = step // 2
+    for number in range(2):
+        slot = slot_ref[step, number]
+        for half in range(2):
+            start = (own if half == 0 else 1 - own) * rows + number * 2 * rows
+            where = pl.ds(pl.multiple_of(start, rows), rows)
+            up_ref[where, :] = held_ref[half * arrays + near, slot]
+            down_ref[where, :] = held_ref[(2 + half) * arrays + near, slot]
 
 
 def normal_share(value, bell):
@@ -993,10 +982,19 @@
 def feed_forward_kernel(
     count, slot_ref, block_ref, core_ref, first_ref, bias_ref, vectors_ref, cotangent_ref, *refs
 ):
-    up_refs, down_refs = refs[:count], refs[count : 2 * count]
-    act_ref, slope_ref, hidden_ref, grad_ref, sums_ref, up_ref, down_ref, low_ref, total_ref, sems = refs[
-        2 * count :
-    ]
+    (
+        act_ref,
+        slope_ref,
+        hidden_ref,
+        grad_ref,
+        sums_ref,
+        held_ref,
+        up_ref,
+        down_ref,
+        low_ref,
+        total_ref,
+        sems,
+    ) = refs[2 * count :]
     step = pl.program_id(0)
 
     @pl.when(step == 0)
@@ -1004,8 +1002,8 @@
         low_ref[...] = first_ref[...].astype(BF16)
         total_ref[...] = first_ref[...] + vectors_ref[0:1, :]
 
-    buffer = fetch_rows(slot_ref, core_ref[0], up_refs, down_refs, up_ref, down_ref, sems)
-    inner = dot_nt(low_ref[...], up_ref[buffer]) + bias_ref[block_ref[step]]
+    join_rows(slot_ref, core_ref[0], refs[: 2 * count], held_ref, up_ref, down_ref, sems)
+    inner = dot_nt(low_ref[...], up_ref[...]) + bias_ref[block_ref[step]]
     bell = jnp.exp(-0.5 * inner * inner)
     share = normal_share(inner, bell)
     act = (inner * share).astype(BF16)
@@ -1013,7 +1011,7 @@
     slope_ref[0] = (
         share + inner * (bell * (2.0 * jnp.pi) ** -0.5)
     ).astype(BF16)
-    total_ref[...] += dot(act, down_ref[buffer])
+    total_ref[...] += dot(act, down_ref[...])
 
     @pl.when(step == pl.num_programs(0) - 1)
     def _():
@@ -1057,11 +1055,12 @@
             + [ANY] * (len(up) + len(down)),
             out_specs=[tile, tile, whole(first.shape), whole(first.shape), whole((8, columns))],
             scratch_shapes=[
-                pltpu.VMEM((2, width, columns), BF16),
-                pltpu.VMEM((2, width, columns), BF16),
+                pltpu.VMEM((len(up) + len(down),) + up[0].shape, BF16),
+                pltpu.VMEM((width, columns), BF16),
+                pltpu.VMEM((width, columns), BF16),
                 pltpu.VMEM((words, columns), BF16),
                 pltpu.VMEM((words, columns), F32),
-                pltpu.SemaphoreType.DMA((2, 8)),
+                pltpu.SemaphoreType.DMA((len(up) + len(down),)),
             ],
         ),
         out_shape=(
@@ -1071,7 +1070,7 @@
             jax.ShapeDtypeStruct((words, columns), F32),
             jax.ShapeDtypeStruct((8, columns), F32),
         ),
-        compiler_params=pltpu.CompilerParams(vmem_limit_bytes=48 * MIB),
+        compiler_params=pltpu.CompilerParams(vmem_limit_bytes=56 * MIB),
         cost_estimate=cost(20),
         name="feed_forward",
     )(slots, block, core, first, bias_blocks, vectors, cotangent, *up, *down)
@@ -1090,7 +1089,6 @@
     gain_ref,
     *refs,
 ):
-    up_refs, down_refs = refs[:count], refs[count : 2 * count]
     (
         up_keep_ref,
         up_sent_ref,
@@ -1099,6 +1097,7 @@
         bias_ref,
         out_ref,
         sums_ref,
+        held_ref,
         up_ref,
         down_ref,
         low_ref,
@@ -1114,13 +1113,13 @@
         low_ref[...] = grad_ref[...].astype(BF16)
         low_first_ref[...] = first_ref[...].astype(BF16)
 
-    buffer = fetch_rows(slot_ref, core_ref[0], up_refs, down_refs, up_ref, down_ref, sems)
+    join_rows(slot_ref, core_ref[0], refs[: 2 * count], held_ref, up_ref, down_ref, sems)
     low = low_ref[...]
-    inner = (dot_nt(low, down_ref[buffer]) * slope_ref[0].astype(F32)).astype(BF16)
+    inner = (dot_nt(low, down_ref[...]) * slope_ref[0].astype(F32)).astype(BF16)
     bias_ref[0] = jnp.sum(inner.astype(F32), axis=0, keepdims=True)
     grad_down = dot_tn(act_ref[0], low).astype(BF16)
     grad_up = dot_tn(inner, low_first_ref[...]).astype(BF16)
-    total_ref[...] += dot(inner, up_ref[buffer])
+    total_ref[...] += dot(inner, up_ref[...])
     rows = up_keep_ref.shape[3]
 
     def store(value, ref):
@@ -1192,12 +1191,13 @@
                 whole((8, columns)),
             ],
             scratch_shapes=[
-                pltpu.VMEM((2, width, columns), BF16),
-                pltpu.VMEM((2, width, columns), BF16),
+                pltpu.VMEM((len(up) + len(down),) + up[0].shape, BF16),
+                pltpu.VMEM((width, columns), BF16),
+                pltpu.VMEM((width, columns), BF16),
                 pltpu.VMEM((words, columns), BF16),
                 pltpu.VMEM((words, columns), BF16),
                 pltpu.VMEM((words, columns), F32),
-                pltpu.SemaphoreType.DMA((2, 8)),
+                pltpu.SemaphoreType.DMA((len(up) + len(down),)),
             ],
         ),
         out_shape=(
@@ -1209,7 +1209,7 @@
             jax.ShapeDtypeStruct((words, columns), F32),
             jax.ShapeDtypeStruct((8, columns), F32),
         ),
-        compiler_params=pltpu.CompilerParams(vmem_limit_bytes=48 * MIB),
+        compiler_params=pltpu.CompilerParams(vmem_limit_bytes=56 * MIB),
         cost_estimate=cost(25),
         name="feed_forward_back",
     )(slots, block, core, grad, first, act, slope, value, gain, *up, *down)
@@ -1459,48 +1459,62 @@
         window(())
         net.ring_done("L00")
         net.plan_move("L00o", "x", "y")
-        net.plan_ring("L01", 1)
         net.plan("smallo2", net.state["smallo1"], "z")
         launch(())
+        net.ring_both("L01")
         net.state["eo0"] = jnp.stack([net.state["e" + part] for part in ("", "x", "y", "xy")])
-        net.ring_step("L01", 2)
-        net.turn_ring("small", 3)
-        net.ring_step("L01", 3)
+        prep, table_blocks = window((prep, table_blocks))
+        net.ring_done("L01")
+        net.plan_move("L01o", "x", "y")
+        net.plan("smallo3", net.state["smallo2"], "z")
+        prep, table_blocks = launch((prep, table_blocks))
+        net.ring_both("L10")
+        net.swap_chain("L00o", "L00ox", "L00oy")
+    char_groups = embed_characters(prep, table_blocks)
+    char_groups = window(char_groups)
+
+    if permutes:
+        net.ring_done("L10")
         conv_all, whole_vectors, pos_all = place_small(
             [net.state[f"smallo{step}"] for step in range(4)],
             net.place(True),
             LANES,
             [vector_block.shape[0], pos_table.size // LANES],
         )
-        conv_all, whole_vectors, pos_all = window((conv_all, whole_vectors, pos_all))
-        net.ring_done("L01")
-        net.plan_move("L01o", "x", "y")
-        net.plan_ring("L10", 1)
-        prep, table_blocks, conv_all, whole_vectors, pos_all = launch(
-            (prep, table_blocks, conv_all, whole_vectors, pos_all)
-        )
-        net.ring_step("L10", 2)
-        net.ring_step("L10", 3)
-        net.swap_chain("L00o", "L00ox", "L00oy")
     else:
         conv_all = gather_plain(conv_block, 1)
         whole_vectors = lax.all_gather(vector_block, "wide", axis=0, tiled=False)
         pos_all = gather_plain(pos_table.T, 0)
-    pos_rows = pos_all.reshape(model_width, words).T.astype(F32)
+    filters = conv_all.shape[1]
+    row = jnp.arange(LANES)[:, None]
+    usable = row // CHAR_DIM < filter_widths(filters)[None, :]
+    half_matrix = jnp.where(usable | (row >= conv_rows), conv_all * BF16(0.5), BF16(0.0))
+    if permutes:
+        net.plan("L00oxy", net.state["L00ox"], "y")
+        net.plan("L01oxy", net.state["L01oy"], "x")
+        net.plan("eo1", net.state["eo0"], "z")
+        half_matrix = launch(half_matrix)
+        net.swap_chain("L01o", "L01ox", "L01oy")
+    pooled = conv_forward(prep, char_groups, half_matrix)
+    pooled, whole_vectors, pos_all = window((pooled, whole_vectors, pos_all))
     whole = [
         whole_vectors[:, start : start + count].reshape(wide, -1)[:, :size].reshape(-1)
         for start, count, size in places
     ]
-    filters = conv_all.shape[1]
-    row = jnp.arange(LANES)[:, None]
-    usable = row // CHAR_DIM < filter_widths(filters)[None, :]
-    half_matrix = jnp.where(usable | (row >= conv_rows), conv_all * BF16(0.5), BF16(0.0))
-    char_groups = embed_characters(prep, table_blocks)
-    pooled = jnp.zeros((words, filters), F32)
-    pooled = conv_forward(prep, char_groups, half_matrix, pooled, 0, filters // 2)
-    pooled, char_groups, half_matrix, whole, pos_rows = window(
-        (pooled, char_groups, half_matrix, whole, pos_rows)
-    )
+    if permutes:
+        net.plan_move("L10o", "x", "y")
+        launch(())
+        net.ring_both("L11")
+        net.swap_chain("L00oxy", "L01oxy", "eo0")
+        pooled, whole, pos_all = window((pooled, whole, pos_all))
+        net.ring_done("L11")
+        net.plan_move("L11o", "x", "y")
+        net.plan("eo2", net.state["eo1"], "z")
+        pooled = launch(pooled)
+        net.swap_chain("L10o", "L10ox", "L10oy")
+        pieces = [net.layer("L0", 2)]
+    else:
+        pieces = [plain_pieces(high_weight[layer], 2) for layer in range(layers)]
     high_bias_all, attn_bias_all = whole[:layers], whole[layers]
     (
         type_zero,
@@ -1516,32 +1530,6 @@
         gain_two,
         shift_two,
     ) = (value.astype(F32) for value in whole[layers + 1 :])
-
-    if permutes:
-        net.ring_done("L10")
-        net.plan("L00oxy", net.state["L00ox"], "y")
-        net.plan("L01oxy", net.state["L01oy"], "x")
-        net.plan("eo1", net.state["eo0"], "z")
-        pooled = launch(pooled)
-        net.swap_chain("L01o", "L01ox", "L01oy")
-    pooled = conv_forward(prep, char_groups, half_matrix, pooled, filters // 2, filters // 2)
-    if permutes:
-        pooled = window(pooled)
-        net.plan_move("L10o", "x", "y")
-        net.plan_ring("L11", 1)
-        launch(())
-        net.ring_step("L11", 2)
-        net.ring_step("L11", 3)
-        net.swap_chain("L00oxy", "L01oxy", "eo0")
-        pooled = window(pooled)
-        net.ring_done("L11")
-        net.plan_move("L11o", "x", "y")
-        net.plan("eo2", net.state["eo1"], "z")
-        pooled = launch(pooled)
-        net.swap_chain("L10o", "L10ox", "L10oy")
-        pieces = [net.layer("L0", 2)]
-    else:
-        pieces = [plain_pieces(high_weight[layer], 2) for layer in range(layers)]
     width = 2 * features // 16
     order = jnp.arange(8)
     near, low_slot = order // 2, order % 2
@@ -1557,18 +1545,19 @@
         net.plan("L10oxy", net.state["L10ox"], "y")
         net.plan("L11oxy", net.state["L11oy"], "x")
         net.plan("eo3", net.state["eo2"], "z")
-        first_layer = launch(first_layer)
+        first_layer, pos_all = launch((first_layer, pos_all))
         net.swap_chain("L11o", "L11ox", "L11oy", "eo1", "eo2")
     turned = [turn(first_layer[3])]
-    turned = window(turned)
+    pos_rows = pos_all.reshape(model_width, words).T.astype(F32)
+    turned, pos_rows = window((turned, pos_rows))
     if permutes:
         net.plan_swap("L10oxy", "L11oxy", "eo3")
         net.plan_ring("up", 1)
         net.plan_ring("down", 1)
+        first_layer = net.stage(first_layer)
+        net.plan_ring("up", 2)
+        net.plan_ring("down", 2)
         first_layer = launch(first_layer)
-        for step in (2, 3):
-            net.ring_step("up", step)
-            net.ring_step("down", step)
         pieces.append(net.layer("L1", 2))
         qkv_all, out_all, proj_all = net.rows(
             [net.state[f"eo{step}"] for step in range(4)],
@@ -1581,6 +1570,11 @@
             gather_plain(value, 0) for value in (qkv_weight.T, out_weight, proj_weight)
         )
     second_layer = highway_forward(first_layer[0], pieces[1], bias_blocks[1], place, select, core)
+    second_layer = window(second_layer)
+    if permutes:
+        net.plan_ring("up", 3)
+        net.plan_ring("down", 3)
+        second_layer = launch(second_layer)
     states = [pooled, first_layer[0], second_layer[0]]
     transforms = [first_layer[1], second_layer[1]]
     gatings = [first_layer[2], second_layer[2]]
@@ -1681,8 +1675,8 @@
             return Reduction(net, keep, sent, order)
         return sum_rows([jnp.concatenate([keep, sent], axis=0).reshape(-1, model_width)], "")
 
-    def ring_of(*sums):
-        return Ring(net, sums) if permutes else sums
+    def ring_of(*sums, both=False):
+        return Ring(net, sums, both) if permutes else sums
 
     def advance(*sums):
         if permutes:
@@ -1726,14 +1720,15 @@
     ready(sum_down, sum_up)
     grad_resid = launch(grad_resid)
     grad_branch = grad_resid.astype(BF16)
-    grad_out = dot_tn(context, grad_branch).astype(BF16)
     grad_context = dot_nt(grad_branch, out_all).astype(BF16)
+    grad_resid, grad_context = window((grad_resid, grad_context))
+    ready(sum_down, sum_up)
+    grad_context = launch(grad_context)
     grad_qkv = attend_back(qkv, grad_context)
-    grad_resid, grad_out, grad_qkv = window((grad_resid, grad_out, grad_qkv))
+    grad_resid, grad_qkv = window((grad_resid, grad_qkv))
 
     ready(sum_down, sum_up)
     grad_qkv, grad_resid = launch((grad_qkv, grad_resid))
-    grad_qkv_weight = dot_tn(grad_qkv, low_embedded)
     qkv_sums = column_sum(grad_qkv)
     grad_attn_bias = jnp.concatenate([qkv_sums[:model_width], qkv_sums[2 * model_width :]])
     grad_summed, grad_embed_gain, grad_embed_shift = norm_back(
@@ -1743,16 +1738,15 @@
     grad_proj_bias = column_sum(grad_word)
     running = dot_nt(dot(perm, grad_word).astype(BF16), proj_all)
     running = window(running)
-    ready(sum_down, sum_up)
+    ring_feed = ring_of(sum_up, sum_down)
+    ready(ring_feed)
     running = launch(running)
     mixed_one, sums_one, running = highway_backward(
         running, states[1], transforms[1], gatings[1], pieces[1], place, select, core
     )
-    grad_pos = turn(grad_summed)
-    if permutes:
-        grad_pos = grad_pos.reshape(-1, model_width)
-    grad_proj = dot_tn(last, grad_word)
-    encoder_grads = [grad_qkv_weight, grad_out, grad_proj]
+    mixed_one, running, grad_qkv, grad_branch, grad_word, grad_summed = window(
+        (mixed_one, running, grad_qkv, grad_branch, grad_word, grad_summed)
+    )
     type_hot = (type_ids[0] == 1).astype(F32)[:, None]
     vector_grads = [
         grad_proj_bias,
@@ -1769,8 +1763,29 @@
         grad_ffn_gain,
         grad_ffn_shift,
     ]
+
+    half_rows, quarter = features // 2, features // 4
+
+    def quarters(jobs, layer, mixed):
+        return [
+            (layer, mixed, start * quarter, quarter, (jobs[start // 2][-1][0], start % 2))
+            for start in range(4)
+        ]
+
+    jobs = [send_layer(1, mixed_one, start, half_rows) for start in (0, half_rows)]
+    ready(ring_feed)
+    mixed_one, grad_qkv, grad_branch, grad_word, grad_summed = launch(
+        (mixed_one, grad_qkv, grad_branch, grad_word, grad_summed)
+    )
+    grad_pos = turn(grad_summed)
+    encoder_grads = [
+        dot_tn(grad_qkv, low_embedded),
+        dot_tn(context, grad_branch),
+        dot_tn(last, grad_word),
+    ]
     if permutes:
-        sum_encoder = sum_rows(encoder_grads + [grad_pos], "c321xy")
+        encoder_grads.append(grad_pos.reshape(-1, model_width))
+        sum_encoder = sum_rows(encoder_grads, "c321xy")
         mixed_one, running, sum_encoder.terms, sum_encoder.sent = window(
             (mixed_one, running, sum_encoder.terms, sum_encoder.sent)
         )
@@ -1778,57 +1793,63 @@
         sum_encoder = sum_rows(encoder_grads, "")
         sum_pos = sum_rows([grad_pos], "")
 
-    half_rows, quarter = features // 2, features // 4
-    jobs = [send_layer(1, mixed_one, start, half_rows) for start in (0, half_rows)]
-    ring_feed = ring_of(sum_up, sum_down)
-    ready(sum_encoder, ring_feed)
+    jobs = quarters(jobs, 1, mixed_one)
+    one = [None] * 4
+    one[0], one[2] = keep_layer(jobs[0], "yx"), keep_layer(jobs[2], "xy")
+    ready(one[0], one[2], sum_encoder, ring_feed)
     running = launch(running)
     mixed_zero, sums_zero, running = highway_backward(
         running, states[0], transforms[0], gatings[0], pieces[0], place, select, core
     )
-    mixed_one, mixed_zero, running = window((mixed_one, mixed_zero, running))
-
-    one = [keep_layer(job, order_) for job, order_ in zip(jobs, ("yx", "xy"))]
+    mixed_zero, running = window((mixed_zero, running))
+
+    one[1], one[3] = keep_layer(jobs[1], "yx"), keep_layer(jobs[3], "xy")
     jobs = [send_layer(0, mixed_zero, start, half_rows) for start in (0, half_rows)]
     grad_scaled = running * (0.5 / sorted_lengths.astype(F32))[:, None]
-    ready(*one, sum_encoder, ring_feed)
+    ready(one[1], one[3], sum_encoder)
     grad_scaled = launch(grad_scaled)
     matrix_turned, grad_groups = conv_backward(prep, char_groups, half_matrix, grad_scaled)
     mixed_zero, matrix_turned, grad_groups = window((mixed_zero, matrix_turned, grad_groups))
 
-    ready(*one, sum_encoder, ring_feed)
+    ready(*one, sum_encoder)
     mixed_zero, grad_groups = launch((mixed_zero, grad_groups))
-    jobs = [
-        (0, mixed_zero, start * quarter, quarter, (jobs[start // 2][-1][0], start % 2))
-        for start in range(4)
-    ]
+    jobs = quarters(jobs, 0, mixed_zero)
     zero = [keep_layer(job, order_) for job, order_ in zip(jobs, ("yx", "yx", "xy", "xy"))]
     first_two = (zero[0], zero[2])
     terms = [item.terms for item in zero] if permutes else ()
-    terms, grad_groups = window((terms, grad_groups))
+    grad_table = table_gradient(prep, grad_groups, character_embedding_table.shape[0])
+    first_sum, vector_places = vector_rows(vector_grads)
+    last_sum, high_places = vector_rows(
+        [sums_zero.reshape(-1), sums_one.reshape(-1), grad_table.reshape(-1)]
+    )
+    high_places = [(first_sum.shape[0] + start, *rest) for start, *rest in high_places]
+    last_sum = jnp.concatenate([first_sum, last_sum], axis=0)
+    terms, last_sum = window((terms, last_sum))
+    last_sum = Small(net, last_sum) if permutes else lax.psum(last_sum, ("narrow", "wide"))
     for item, value in zip(zero, terms):
         item.terms = value
 
-    ready(*first_two, sum_encoder)
-    grad_groups = launch(grad_groups)
-    grad_table = table_gradient(prep, grad_groups, character_embedding_table.shape[0])
-    last_sum, vector_places = vector_rows(
-        vector_grads + [sums_zero.reshape(-1), sums_one.reshape(-1), grad_table.reshape(-1)]
-    )
-    last_sum = window(last_sum)
-    last_sum = Small(net, last_sum) if permutes else lax.psum(last_sum, ("narrow", "wide"))
+    if permutes:
+        conv_keep, conv_sent = net.split([matrix_turned])
+        net.plan("conv", conv_sent, "c")
+    else:
+        sum_conv = sum_rows([matrix_turned], "")
+    ready(*first_two, sum_encoder, last_sum)
+    launch(())
+    window(())
+    if permutes:
+        conv_total = total_of([conv_keep, net.state["conv"]]).astype(BF16)
+        conv_total = conv_total.reshape((4, 2, 2) + conv_total.shape[1:])
+        zero[3].terms = [jnp.concatenate([zero[3].terms[0], conv_total], axis=3)]
 
     ring_one = ring_of(*one)
     together(zero[1], zero[3], *first_two, ring_one)
-    sum_conv = sum_rows([matrix_turned], "cxy321")
-    ring_first = ring_of(*first_two)
-    together(zero[1], zero[3], ring_first, ring_one, sum_conv)
-    together(ring_first, ring_one, sum_encoder, last_sum, sum_conv)
-    together(ring_first, sum_encoder, last_sum, sum_conv)
-    ring_last = ring_of(zero[1], zero[3])
-    together(ring_last, last_sum, sum_conv)
-    together(ring_last, last_sum, sum_conv)
-    together(ring_last, last_sum, sum_conv)
+    together(zero[1], zero[3], ring_one, last_sum)
+    ring_first = ring_of(*first_two, both=True)
+    together(ring_first, ring_one, sum_encoder, last_sum)
+    ring_last = ring_of(zero[1], zero[3], both=True)
+    together(ring_first, ring_last, sum_encoder, last_sum)
+    together(ring_last, last_sum)
     total = last_sum.result() if permutes else last_sum
 
     device = lax.axis_index("narrow") * wide + lax.axis_index("wide")
@@ -1841,8 +1862,7 @@
         piece = where[2] // devices
         return lax.dynamic_slice_in_dim(whole_vector(total, where), device * piece, piece, 0)
 
-    results = [own_part(total, where) for where in vector_places[: len(vector_grads)]]
-    high_places = vector_places[len(vector_grads) :]
+    results = [own_part(total, where) for where in vector_places]
     (
         sum_proj_bias,
         sum_type_zero,
@@ -1890,7 +1910,11 @@
         up_rows, down_rows = jnp.split(ring_feed.result(), 2)
     else:
         (up_rows,), (down_rows,) = sum_up.result(), sum_down.result()
-    (conv_turned,) = rows_of(sum_conv, [filters // devices])
+    if permutes:
+        first_rows, last_rows = ring_first.result(), ring_last.result()
+        conv_turned = last_rows[2 * quarter :]
+    else:
+        (conv_turned,) = sum_conv.result()
     own_filters = lax.dynamic_slice_in_dim(
         filter_widths(filters), device * (filters // devices), filters // devices
     )
@@ -1898,8 +1922,7 @@
     sum_conv_weight = jnp.where(taps < own_filters[None, :], conv_turned[:, :conv_rows].T, 0.0)
 
     if permutes:
-        first_rows, last_rows = ring_first.result(), ring_last.result()
-        parts = [first_rows[:quarter], last_rows[:quarter], first_rows[quarter:], last_rows[quarter:]]
+        parts = [first_rows[:quarter], last_rows[:quarter], first_rows[quarter:], last_rows[quarter : 2 * quarter]]
         high_rows = [jnp.concatenate(parts, axis=0), ring_one.result()]
     else:
         high_rows = [

time: 886 us -> 831 us (0.938)
  waiting for transfers between devices: 308 us -> 262 us
  local copies, waits for them, and re-layouts: 97.3 us -> 76.5 us
    ppermute x90 -> x89, waiting for transfers between devices: 292 us -> 249 us  [send(): return lax.ppermute(value, 'wide', LINKS[link])]
    unnamed x422 -> x416, local copies, waits for them, and re-layouts: 46.8 us -> 36.3 us
    ppermute x90 -> x89, starting transfers between devices: 69.8 us -> 77.9 us  [send(): return lax.ppermute(value, 'wide', LINKS[link])]
    pallas_call x10 -> x12, Pallas kernels: 36.4 us -> 40.9 us  [highway_weight_gradient(): pl.pallas_call(weight_kernel, grid_spec=pltpu.PrefetchScalarGridSpec(num_...]
    add x10 -> x11, other arithmetic: 20.5 us -> 21.5 us  [total_of(): return sum((term.astype(F32) for term in terms[1:]), terms[0].astype(F32))]
  transfers between devices with their start and end apart: 127 -> 126, of which waited for: 53 -> 48; matrix products, arithmetic and copies ran while one was open for 10% -> 13% of each run, Pallas kernels for 22% -> 24%
where the time goes in v3:
time: 831 us; the launch traced here: 817 us
  Pallas kernels  267 us (32%)
  waiting for transfers between devices  262 us (32%)
  other arithmetic  101 us (12%)
  starting transfers between devices  84.3 us (10%)
  local copies, waits for them, and re-layouts  76.5 us (9%)
  matrix products  22.2 us (3%)
    ppermute x89, waiting for transfers between devices, send(): return lax.ppermute(value, 'wide', LINKS[link])  249 us
    ppermute x89, starting transfers between devices, send(): return lax.ppermute(value, 'wide', LINKS[link])  77.9 us
    pallas_call x2, Pallas kernels, highway_backward(): pl.pallas_call(partial(highway_backward_kernel, layout), grid_spec=pltpu....  42.8 us
    pallas_call x12, Pallas kernels, highway_weight_gradient(): pl.pallas_call(weight_kernel, grid_spec=pltpu.PrefetchScalarGridSpec(num_...  40.9 us
    pallas_call x2, Pallas kernels, highway_forward(): pl.pallas_call(partial(highway_forward_kernel, layout), grid_spec=pltpu.P...  39 us
    unnamed x416, local copies, waits for them, and re-layouts  36.3 us
    pallas_call x1, Pallas kernels, conv_backward(): pl.pallas_call(conv_backward_kernel, out_shape=(jax.ShapeDtypeStruct((fil...  34.5 us
    pallas_call x1, Pallas kernels, feed_forward_back(): pl.pallas_call(partial(feed_forward_back_kernel, len(up)), grid_spec=pltp...  24.6 us
  transfers between devices with their start and end apart: 126, of which 48 were waited for; matrix products, arithmetic and copies ran while one was open for 13% of the time, Pallas kernels for 24%

profile of v3, /device:TPU:0, one launch (start us, length us, event | category | flops | bytes accessed | tf_op | source)
XLA Modules:
  0.0 817.4 jit_solution(2945560616649275319)
XLA Ops:
  34.2 7.0 collective-permute-done.7
  47.5 7.2 collective-permute-done.13
  57.5 15.1 %collective-permute-done.15 = bf16[512,256]{1,0:T(8,128)(2,1)S(1)} collective-permute-done((bf16[512,256]{1,0:T(8,128)(2,1)S(1)}, bf16[512,256]{1,0:T(8,128)(2,1)S(1)}, u32[]{:S(2)}, u32[]{:S(2)}) %collective-permute-start.15) | collective-permute-done | bytes 262176 | tf_op jit(solution)/shard_map/ppermute | solution.py:634
  76.5 7.6 collective-permute-done.19
  84.2 7.6 collective-permute-done.20
  92.7 8.8 %collective-permute-done.21 = bf16[512,256]{1,0:T(8,128)(2,1)} collective-permute-done((bf16[512,256]{1,0:T(8,128)(2,1)}, bf16[512,256]{1,0:T(8,128)(2,1)}, u32[]{:S(2)}, u32[]{:S(2)}) %collective-permute-start.21) | collective-permute-done | bytes 262176 | tf_op jit(solution)/shard_map/ppermute | solution.py:634
  120.1 12.7 %conv_forward.1.h_ref = f32[512,2048]{1,0:T(8,128)S(1)} custom-call(s32[8]{0:T(128)S(1)} %pad_add_fusion.scalar_ref, s32[816]{0:T(1024)S(1)} %fusion.76.tile_ref, s32[816]{0:T(1024)S(1)} %subtract_select_fusion.pos_ref, bf16[8,512,128]{2,1,0:T(8,128)(2,1)S(1)} %copy-done.57, bf16[128,2048]{1,0:T(8,128)(2,1)S(1)} %or_select_fusion.w_ref, ...), custom_call_target="tpu_custom_call" | custom-call | flops 17600000000 | bytes 48000000 | tf_op jit(solution)/shard_map/conv_forward/pallas_call | solution.py:175
  134.8 10.6 %collective-permute-done.32.refs_1_ = bf16[4,160,768]{2,1,0:T(8,128)(2,1)S(1)} collective-permute-done((bf16[4,160,768]{2,1,0:T(8,128)(2,1)S(1)}, bf16[4,160,768]{2,1,0:T(8,128)(2,1)S(1)}, u32[]{:S(2)}, u32[]{:S(2)}) %collective-permute-start.32) | collective-permute-done | bytes 983072 | tf_op jit(solution)/shard_map/ppermute | solution.py:634
  153.3 10.5 %collective-permute-done.27 = bf16[512,256]{1,0:T(8,128)(2,1)} collective-permute-done((bf16[512,256]{1,0:T(8,128)(2,1)S(1)}, bf16[512,256]{1,0:T(8,128)(2,1)}, u32[]{:S(2)}, u32[]{:S(2)}) %collective-permute-start.27) | collective-permute-done | bytes 262176 | tf_op jit(solution)/shard_map/ppermute | solution.py:634
  163.8 7.1 collective-permute-done.28
  185.3 19.5 %highway_forward.2 = (f32[512,2048]{1,0:T(8,128)}, f32[512,2048]{1,0:T(8,128)}, f32[512,2048]{1,0:T(8,128)}, bf16[512,2048]{1,0:T(8,128)(2,1)}) custom-call(s32[8]{0:T(128)} %get-tuple-element.1008.place_ref, s32[8]{0:T(128)} %get-tuple-element.1007.select_ref, s32[1]{0:T(128)} %bitcast.core_ref.which_ref, f32[512,2048]{1,0:T(8,128)} %copy-done.59, ...), custom_call_target="tpu_custom_call" | custom-call | flops 20899999744 | bytes 57000000 | tf_op jit(solution)/shard_map/highway_forward/pallas_call | solution.py:385
  228.1 15.1 %collective-permute-done.47.refs_3_ = bf16[4,160,768]{2,1,0:T(8,128)(2,1)} collective-permute-done((bf16[4,160,768]{2,1,0:T(8,128)(2,1)}, bf16[4,160,768]{2,1,0:T(8,128)(2,1)}, u32[]{:S(2)}, u32[]{:S(2)}) %collective-permute-start.47) | collective-permute-done | bytes 983072 | tf_op jit(solution)/shard_map/ppermute | solution.py:634
  245.2 7.6 collective-permute-done.56
  256.9 19.5 %highway_forward.3 = (f32[512,2048]{1,0:T(8,128)}, f32[512,2048]{1,0:T(8,128)}, f32[512,2048]{1,0:T(8,128)}, bf16[512,2048]{1,0:T(8,128)(2,1)}) custom-call(s32[8]{0:T(128)} %get-tuple-element.1008.place_ref, s32[8]{0:T(128)} %get-tuple-element.1007.select_ref, s32[1]{0:T(128)} %bitcast.core_ref.which_ref, f32[512,2048]{1,0:T(8,128)} %get-tuple-element.585.h_ref, ...), custom_call_target="tpu_custom_call" | custom-call | flops 20899999744 | bytes 57000000 | tf_op jit(solution)/shard_map/highway_forward/pallas_call | solution.py:385
  276.4 8.6 %place_rows.1 = (bf16[2304,768]{1,0:T(8,128)(2,1)S(1)}, bf16[768,768]{1,0:T(8,128)(2,1)S(1)}, bf16[2048,768]{1,0:T(8,128)(2,1)S(1)}) custom-call(s32[16]{0:T(128)S(1)} %fusion.80.place_ref, s32[1]{0:T(128)} %bitcast.core_ref.which_ref, bf16[4,160,768]{2,1,0:T(8,128)(2,1)S(1)} %pad_maximum_fusion.8.refs_0_, bf16[4,160,768]{2,1,0:T(8,128)(2,1)S(1)} %copy-done.37, ...), custom_call_target="tpu_custom_call" | custom-call | flops 7699999744 | bytes 21000000 | tf_op jit(solution)/shard_map/place_rows/pallas_call | solution.py:560
  306.9 11.1 %attend.1 = bf16[512,768]{1,0:T(8,128)(2,1)S(1)} custom-call(bf16[512,2304]{1,0:T(8,128)(2,1)S(1)} %fusion.query_ref.key_ref.value_ref, bf16[512,2304]{1,0:T(8,128)(2,1)S(1)} %fusion.query_ref.key_ref.value_ref, bf16[512,2304]{1,0:T(8,128)(2,1)S(1)} %fusion.query_ref.key_ref.value_ref), custom_call_target="tpu_custom_call" | custom-call | flops 13200000000 | bytes 36000000 | tf_op jit(solution)/shard_map/attend/pallas_call | solution.py:1240
  318.1 10.0 %collective-permute-done.64.refs_9_ = bf16[4,96,768]{2,1,0:T(8,128)(2,1)S(1)} collective-permute-done((bf16[4,96,768]{2,1,0:T(8,128)(2,1)S(1)}, bf16[4,96,768]{2,1,0:T(8,128)(2,1)S(1)}, u32[]{:S(2)}, u32[]{:S(2)}) %collective-permute-start.64) | collective-permute-done | bytes 589856 | tf_op jit(solution)/shard_map/ppermute | solution.py:634
  338.6 9.8 %collective-permute-done.68.refs_3_ = bf16[4,96,768]{2,1,0:T(8,128)(2,1)} collective-permute-done((bf16[4,96,768]{2,1,0:T(8,128)(2,1)S(1)}, bf16[4,96,768]{2,1,0:T(8,128)(2,1)}, u32[]{:S(2)}, u32[]{:S(2)}) %collective-permute-start.68) | collective-permute-done | bytes 589856 | tf_op jit(solution)/shard_map/ppermute | solution.py:634
  353.4 21.2 %feed_forward.1 = (bf16[8,512,384]{2,1,0:T(8,128)(2,1)}, bf16[8,512,384]{2,1,0:T(8,128)(2,1)}, bf16[512,768]{1,0:T(8,128)(2,1)}, f32[512,768]{1,0:T(8,128)}, f32[8,768]{1,0:T(8,128)}) custom-call(s32[8,2]{1,0:T(8,128)} %add_select_fusion.slot_ref, s32[8]{0:T(128)} %add_add_fusion.2.block_ref, s32[1]{0:T(128)} %bitcast.core_ref.which_ref, ...), custom_call_target="tpu_custom_call" | custom-call | flops 22000001024 | bytes 60000000 | tf_op jit(solution)/shard_map/feed_forward/pallas_call | solution.py:1044
  374.6 24.6 %feed_forward_back.1 = (bf16[2,4,2,96,768]{4,3,2,1,0:T(8,128)(2,1)}, bf16[2,4,2,96,768]{4,3,2,1,0:T(8,128)(2,1)}, bf16[2,4,2,96,768]{4,3,2,1,0:T(8,128)(2,1)}, b...) custom-call(s32[8,2]{1,0:T(8,128)} %add_select_fusion.slot_ref, ...), custom_call_target="tpu_custom_call" | custom-call | flops 27499999232 | bytes 75000000 | tf_op jit(solution)/shard_map/feed_forward_back/pallas_call | solution.py:1170
  412.9 16.6 %attend_back.1 = (bf16[512,768]{1,0:T(8,128)(2,1)S(1)}, bf16[512,768]{1,0:T(8,128)(2,1)S(1)}, bf16[512,768]{1,0:T(8,128)(2,1)S(1)}) custom-call(bf16[512,2304]{1,0:T(8,128)(2,1)S(1)} %copy-done.55, bf16[512,2304]{1,0:T(8,128)(2,1)S(1)} %copy-done.55, bf16[512,2304]{1,0:T(8,128)(2,1)S(1)} %copy-done.55, bf16[512,768]{1,0:T(8,128)(2,1)S(1)} %convolution_convert_fusion.4.grad_ref), custom_call_target="tpu_custom_call" | custom-call | flops 18699999232 | bytes 51000000 | tf_op jit(solution)/shard_map/attend_back/pallas_call | solution.py:1275
  429.7 9.3 %collective-permute-done.78 = bf16[4,2,96,768]{3,2,1,0:T(8,128)(2,1)S(1)} collective-permute-done((bf16[4,2,96,768]{3,2,1,0:T(8,128)(2,1)S(1)}, bf16[4,2,96,768]{3,2,1,0:T(8,128)(2,1)S(1)}, u32[]{:S(2)}, u32[]{:S(2)}) %collective-permute-start.78) | collective-permute-done | bytes 1179680 | tf_op jit(solution)/shard_map/ppermute | solution.py:634
  450.9 6.5 fusion.26.grad_ref
  465.1 21.4 %highway_backward.2 = (bf16[2,512,2048]{2,1,0:T(8,128)(2,1)}, f32[2,1,2048]{2,1,0:T(1,128)}, f32[512,2048]{1,0:T(8,128)}) custom-call(s32[8]{0:T(128)} %get-tuple-element.1008.place_ref, s32[8]{0:T(128)} %get-tuple-element.1007.select_ref, s32[1]{0:T(128)} %bitcast.core_ref.which_ref, f32[512,2048]{1,0:T(8,128)} %fusion.26.grad_ref, ...), custom_call_target="tpu_custom_call" | custom-call | flops 23100000256 | bytes 63000000 | tf_op jit(solution)/shard_map/highway_backward/pallas_call | solution.py:449
  537.1 21.5 %highway_backward.3 = (bf16[2,512,2048]{2,1,0:T(8,128)(2,1)}, f32[2,1,2048]{2,1,0:T(1,128)}, f32[512,2048]{1,0:T(8,128)}) custom-call(s32[8]{0:T(128)} %get-tuple-element.1008.place_ref, s32[8]{0:T(128)} %get-tuple-element.1007.select_ref, s32[1]{0:T(128)} %bitcast.core_ref.which_ref, f32[512,2048]{1,0:T(8,128)} %get-tuple-element.737.grad_ref, ...), custom_call_target="tpu_custom_call" | custom-call | flops 23100000256 | bytes 63000000 | tf_op jit(solution)/shard_map/highway_backward/pallas_call | solution.py:449
  592.0 34.5 %conv_backward.1 = (bf16[2048,128]{1,0:T(8,128)(2,1)S(1)}, f32[8,512,128]{2,1,0:T(8,128)S(1)}) custom-call(s32[8]{0:T(128)S(1)} %copy-done.47, s32[816]{0:T(1024)S(1)} %copy-done.32, s32[816]{0:T(1024)S(1)} %copy-done.34, bf16[8,512,128]{2,1,0:T(8,128)(2,1)S(1)} %copy-done.58, bf16[128,2048]{1,0:T(8,128)(2,1)S(1)} %copy-done.26, s32[512,1]{1,0:T(8,128)S(1)} %copy-done.30, ...), custom_call_target="tpu_custom_call" | custom-call | flops 38499999744 | bytes 105000000 | tf_op jit(solution)/shard_map/conv_backward/pallas_call | solution.py:232
  682.3 6.5 collective-permute-done.101
  702.1 26.9 %collective-permute-done.107 = bf16[4,512,128]{2,1,0:T(8,128)(2,1)} collective-permute-done((bf16[4,512,128]{2,1,0:T(8,128)(2,1)}, bf16[4,512,128]{2,1,0:T(8,128)(2,1)}, u32[]{:S(2)}, u32[]{:S(2)}) %collective-permute-start.107) | collective-permute-done | bytes 524320 | tf_op jit(solution)/shard_map/ppermute | solution.py:634
  744.1 5.8 collective-permute-done.112
  763.7 8.1 collective-permute-done.116
  777.3 16.2 %collective-permute-done.123 = f32[224,128]{1,0:T(8,128)S(1)} collective-permute-done((f32[224,128]{1,0:T(8,128)S(1)}, f32[224,128]{1,0:T(8,128)S(1)}, u32[]{:S(2)}, u32[]{:S(2)}) %collective-permute-start.123) | collective-permute-done | bytes 114720 | tf_op jit(solution)/shard_map/ppermute | solution.py:634
  798.4 5.9 collective-permute-done.125
  (924 shorter events, 392.0 us)
Async XLA Ops:
  41.3 31.3 %collective-permute-start.22 = (bf16[4,512,256]{2,1,0:T(8,128)(2,1)S(1)}, bf16[4,512,256]{2,1,0:T(8,128)(2,1)S(1)}, u32[]{:S(2)}, u32[]{:S(2)}) collective-permute-start(bf16[4,512,256]{2,1,0:T(8,128)(2,1)S(1)} %pad_maximum_fusion.4), channel_id=1, source_target_pairs={{0,16},{16,0},{1,17},{17,1},{2,18},{18,2},{3,19},{19,3},{4,20},{20... | collective-permute-start | bytes 3145736 | tf_op jit(solution)/shard_map/ppermute | solution.py:633
  41.4 31.2 %collective-permute-start.10 = (bf16[4,512,256]{2,1,0:T(8,128)(2,1)S(1)}, bf16[4,512,256]{2,1,0:T(8,128)(2,1)S(1)}, u32[]{:S(2)}, u32[]{:S(2)}) collective-permute-start(bf16[4,512,256]{2,1,0:T(8,128)(2,1)S(1)} %pad_maximum_fusion.4), channel_id=1, source_target_pairs={{0,1},{1,0},{2,3},{3,2},{4,5},{5,4},{6,7},{7,6},{8,9},{9,8},{10,11... | collective-permute-start | bytes 3145736 | tf_op jit(solution)/shard_map/ppermute | solution.py:634
  43.0 29.7 %collective-permute-start.11 = (bf16[4,512,256]{2,1,0:T(8,128)(2,1)S(1)}, bf16[4,512,256]{2,1,0:T(8,128)(2,1)}, u32[]{:S(2)}, u32[]{:S(2)}) collective-permute-start(bf16[4,512,256]{2,1,0:T(8,128)(2,1)S(1)} %pad_maximum_fusion.4), channel_id=1, source_target_pairs={{0,2},{1,3},{2,0},{3,1},{4,6},{5,7},{6,4},{7,5},{8,10},{9,11},{10,... | collective-permute-start | bytes 3145736 | tf_op jit(solution)/shard_map/ppermute | solution.py:634
  73.9 37.4 %collective-permute-start.16 = (bf16[4,512,256]{2,1,0:T(8,128)(2,1)S(1)}, bf16[4,512,256]{2,1,0:T(8,128)(2,1)}, u32[]{:S(2)}, u32[]{:S(2)}) collective-permute-start(bf16[4,512,256]{2,1,0:T(8,128)(2,1)S(1)} %pad_maximum_fusion.5), channel_id=1, source_target_pairs={{0,1},{1,0},{2,3},{3,2},{4,5},{5,4},{6,7},{7,6},{8,9},{9,8},{10,11... | collective-permute-start | bytes 3145736 | tf_op jit(solution)/shard_map/ppermute | solution.py:634
  74.5 36.8 %collective-permute-start.17 = (bf16[4,512,256]{2,1,0:T(8,128)(2,1)S(1)}, bf16[4,512,256]{2,1,0:T(8,128)(2,1)}, u32[]{:S(2)}, u32[]{:S(2)}) collective-permute-start(bf16[4,512,256]{2,1,0:T(8,128)(2,1)S(1)} %pad_maximum_fusion.5), channel_id=1, source_target_pairs={{0,2},{1,3},{2,0},{3,1},{4,6},{5,7},{6,4},{7,5},{8,10},{9,11},{10,... | collective-permute-start | bytes 3145736 | tf_op jit(solution)/shard_map/ppermute | solution.py:634
  76.0 35.2 %collective-permute-start.24 = (bf16[4,512,256]{2,1,0:T(8,128)(2,1)}, bf16[4,512,256]{2,1,0:T(8,128)(2,1)}, u32[]{:S(2)}, u32[]{:S(2)}) collective-permute-start(bf16[4,512,256]{2,1,0:T(8,128)(2,1)} %collective-permute-done.11), channel_id=1, source_target_pairs={{0,16},{16,0},{1,17},{17,1},{2,18},{18,2},{3,19},{19,3},{4,20},{20... | collective-permute-start | bytes 3145736 | tf_op jit(solution)/shard_map/ppermute | solution.py:633
  76.0 35.2 %collective-permute-start.33 = (bf16[4,512,256]{2,1,0:T(8,128)(2,1)S(1)}, bf16[4,512,256]{2,1,0:T(8,128)(2,1)}, u32[]{:S(2)}, u32[]{:S(2)}) collective-permute-start(bf16[4,512,256]{2,1,0:T(8,128)(2,1)S(1)} %pad_maximum_fusion.5), channel_id=1, source_target_pairs={{0,16},{16,0},{1,17},{17,1},{2,18},{18,2},{3,19},{19,3},{4,20},{20... | collective-permute-start | bytes 3145736 | tf_op jit(solution)/shard_map/ppermute | solution.py:633
  117.9 27.5 %collective-permute-start.30 = (bf16[4,512,256]{2,1,0:T(8,128)(2,1)S(1)}, bf16[4,512,256]{2,1,0:T(8,128)(2,1)S(1)}, u32[]{:S(2)}, u32[]{:S(2)}) collective-permute-start(bf16[4,512,256]{2,1,0:T(8,128)(2,1)S(1)} %copy-done.169), channel_id=1, source_target_pairs={{0,2},{1,3},{2,0},{3,1},{4,6},{5,7},{6,4},{7,5},{8,10},{9,11},{10,... | collective-permute-start | bytes 3145736 | tf_op jit(solution)/shard_map/ppermute | solution.py:634
  150.7 29.4 %collective-permute-start.25 = (bf16[4,512,256]{2,1,0:T(8,128)(2,1)}, bf16[4,512,256]{2,1,0:T(8,128)(2,1)}, u32[]{:S(2)}, u32[]{:S(2)}) collective-permute-start(bf16[4,512,256]{2,1,0:T(8,128)(2,1)} %pad_maximum_fusion.6), channel_id=1, source_target_pairs={{0,1},{1,0},{2,3},{3,2},{4,5},{5,4},{6,7},{7,6},{8,9},{9,8},{10,11... | collective-permute-start | bytes 3145736 | tf_op jit(solution)/shard_map/ppermute | solution.py:634
  152.2 27.9 %collective-permute-start.26 = (bf16[4,512,256]{2,1,0:T(8,128)(2,1)}, bf16[4,512,256]{2,1,0:T(8,128)(2,1)}, u32[]{:S(2)}, u32[]{:S(2)}) collective-permute-start(bf16[4,512,256]{2,1,0:T(8,128)(2,1)} %pad_maximum_fusion.6), channel_id=1, source_target_pairs={{0,2},{1,3},{2,0},{3,1},{4,6},{5,7},{6,4},{7,5},{8,10},{9,11},{10,... | collective-permute-start | bytes 3145736 | tf_op jit(solution)/shard_map/ppermute | solution.py:634
  152.7 27.4 %collective-permute-start.42 = (bf16[4,512,256]{2,1,0:T(8,128)(2,1)}, bf16[4,512,256]{2,1,0:T(8,128)(2,1)}, u32[]{:S(2)}, u32[]{:S(2)}) collective-permute-start(bf16[4,512,256]{2,1,0:T(8,128)(2,1)} %pad_maximum_fusion.6), channel_id=1, source_target_pairs={{0,16},{16,0},{1,17},{17,1},{2,18},{18,2},{3,19},{19,3},{4,20},{20... | collective-permute-start | bytes 3145736 | tf_op jit(solution)/shard_map/ppermute | solution.py:633
  152.7 27.4 %collective-permute-start.38 = (bf16[4,160,768]{2,1,0:T(8,128)(2,1)S(1)}, bf16[4,160,768]{2,1,0:T(8,128)(2,1)}, u32[]{:S(2)}, u32[]{:S(2)}) collective-permute-start(bf16[4,160,768]{2,1,0:T(8,128)(2,1)S(1)} %pad_maximum_fusion.8.refs_0_), channel_id=1, source_target_pairs={{0,16},{16,0},{1,17},{17,1},{2,18},{18,2},{3,19},{19,3},{4,20},{20... | collective-permute-start | bytes 2949128 | tf_op jit(solution)/shard_map/ppermute | solution.py:633
  182.1 27.7 %collective-permute-start.48 = (bf16[4,512,256]{2,1,0:T(8,128)(2,1)S(1)}, bf16[4,512,256]{2,1,0:T(8,128)(2,1)S(1)}, u32[]{:S(2)}, u32[]{:S(2)}) collective-permute-start(bf16[4,512,256]{2,1,0:T(8,128)(2,1)S(1)} %pad_maximum_fusion.7), channel_id=1, source_target_pairs={{0,16},{16,0},{1,17},{17,1},{2,18},{18,2},{3,19},{19,3},{4,20},{20... | collective-permute-start | bytes 3145736 | tf_op jit(solution)/shard_map/ppermute | solution.py:633
  215.5 27.6 %collective-permute-start.45 = (bf16[4,512,256]{2,1,0:T(8,128)(2,1)}, bf16[4,512,256]{2,1,0:T(8,128)(2,1)}, u32[]{:S(2)}, u32[]{:S(2)}) collective-permute-start(bf16[4,512,256]{2,1,0:T(8,128)(2,1)} %collective-permute-done.25), channel_id=1, source_target_pairs={{0,2},{1,3},{2,0},{3,1},{4,6},{5,7},{6,4},{7,5},{8,10},{9,11},{10,... | collective-permute-start | bytes 3145736 | tf_op jit(solution)/shard_map/ppermute | solution.py:634
  255.6 29.5 %collective-permute-start.58 = (bf16[96,768]{1,0:T(8,128)(2,1)S(1)}, bf16[96,768]{1,0:T(8,128)(2,1)}, u32[]{:S(2)}, u32[]{:S(2)}) collective-permute-start(bf16[96,768]{1,0:T(8,128)(2,1)S(1)} %collective-permute-done.56), channel_id=1, source_target_pairs={{0,4},{1,5},{2,6},{3,7},{4,8},{5,9},{6,10},{7,11},{8,12},{9,13},{1... | collective-permute-start | bytes 442376 | tf_op jit(solution)/shard_map/ppermute | solution.py:634
  255.7 29.4 %collective-permute-start.59 = (bf16[96,768]{1,0:T(8,128)(2,1)S(1)}, bf16[96,768]{1,0:T(8,128)(2,1)}, u32[]{:S(2)}, u32[]{:S(2)}) collective-permute-start(bf16[96,768]{1,0:T(8,128)(2,1)S(1)} %collective-permute-done.57), channel_id=1, source_target_pairs={{0,4},{1,5},{2,6},{3,7},{4,8},{5,9},{6,10},{7,11},{8,12},{9,13},{1... | collective-permute-start | bytes 442376 | tf_op jit(solution)/shard_map/ppermute | solution.py:634
  410.9 28.1 %collective-permute-start.78 = (bf16[4,2,96,768]{3,2,1,0:T(8,128)(2,1)S(1)}, bf16[4,2,96,768]{3,2,1,0:T(8,128)(2,1)S(1)}, u32[]{:S(2)}, u32[]{:S(2)}) collective-permute-start(bf16[4,2,96,768]{3,2,1,0:T(8,128)(2,1)S(1)} %fusion.6), channel_id=1, source_target_pairs={{0,2},{1,3},{2,0},{3,1},{4,6},{5,7},{6,4},{7,5},{8,10},{9,11},{10,... | collective-permute-start | bytes 3538952 | tf_op jit(solution)/shard_map/ppermute | solution.py:634
  411.4 27.7 %collective-permute-start.79 = (bf16[4,2,96,768]{3,2,1,0:T(8,128)(2,1)S(1)}, bf16[4,2,96,768]{3,2,1,0:T(8,128)(2,1)S(1)}, u32[]{:S(2)}, u32[]{:S(2)}) collective-permute-start(bf16[4,2,96,768]{3,2,1,0:T(8,128)(2,1)S(1)} %fusion.7), channel_id=1, source_target_pairs={{0,1},{1,0},{2,3},{3,2},{4,5},{5,4},{6,7},{7,6},{8,9},{9,8},{10,11... | collective-permute-start | bytes 3538952 | tf_op jit(solution)/shard_map/ppermute | solution.py:634
  530.7 37.9 %collective-permute-start.88 = (bf16[16,176,768]{2,1,0:T(8,128)(2,1)}, bf16[16,176,768]{2,1,0:T(8,128)(2,1)}, u32[]{:S(2)}, u32[]{:S(2)}) collective-permute-start(bf16[16,176,768]{2,1,0:T(8,128)(2,1)} %pad_maximum_fusion.1), channel_id=1, source_target_pairs={{0,16},{16,0},{1,17},{17,1},{2,18},{18,2},{3,19},{19,3},{4,20},{20... | collective-permute-start | bytes 12976136 | tf_op jit(solution)/shard_map/ppermute | solution.py:633
  534.9 33.8 %collective-permute-start.86 = (bf16[4,2,512,128]{3,2,1,0:T(8,128)(2,1)}, bf16[4,2,512,128]{3,2,1,0:T(8,128)(2,1)}, u32[]{:S(2)}, u32[]{:S(2)}) collective-permute-start(bf16[4,2,512,128]{3,2,1,0:T(8,128)(2,1)} %dynamic-slice_bitcast_fusion.8), channel_id=1, source_target_pairs={{0,2},{1,3},{2,0},{3,1},{4,6},{5,7},{6,4},{7,5},{8,10},{9,11},{10,... | collective-permute-start | bytes 3145736 | tf_op jit(solution)/shard_map/ppermute | solution.py:634
  536.3 32.3 %collective-permute-start.87 = (bf16[4,2,512,128]{3,2,1,0:T(8,128)(2,1)S(1)}, bf16[4,2,512,128]{3,2,1,0:T(8,128)(2,1)}, u32[]{:S(2)}, u32[]{:S(2)}) collective-permute-start(bf16[4,2,512,128]{3,2,1,0:T(8,128)(2,1)S(1)} %copy-done.83), channel_id=1, source_target_pairs={{0,1},{1,0},{2,3},{3,2},{4,5},{5,4},{6,7},{7,6},{8,9},{9,8},{10,11... | collective-permute-start | bytes 3145736 | tf_op jit(solution)/shard_map/ppermute | solution.py:634
  536.9 31.7 %collective-permute-start.89 = (bf16[192,768]{1,0:T(8,128)(2,1)}, bf16[192,768]{1,0:T(8,128)(2,1)S(1)}, u32[]{:S(2)}, u32[]{:S(2)}) collective-permute-start(bf16[192,768]{1,0:T(8,128)(2,1)} %fusion.30), channel_id=1, source_target_pairs={{0,4},{1,5},{2,6},{3,7},{4,8},{5,9},{6,10},{7,11},{8,12},{9,13},{1... | collective-permute-start | bytes 884744 | tf_op jit(solution)/shard_map/ppermute | solution.py:634
  583.5 46.5 %collective-permute-start.90 = (bf16[16,1024,128]{2,1,0:T(8,128)(2,1)}, bf16[16,1024,128]{2,1,0:T(8,128)(2,1)}, u32[]{:S(2)}, u32[]{:S(2)}) collective-permute-start(bf16[16,1024,128]{2,1,0:T(8,128)(2,1)} %highway_weight.17), channel_id=1, source_target_pairs={{0,16},{16,0},{1,17},{17,1},{2,18},{18,2},{3,19},{19,3},{4,20},{20... | collective-permute-start | bytes 12582920 | tf_op jit(solution)/shard_map/ppermute | solution.py:633
  583.5 46.5 %collective-permute-start.91 = (bf16[16,1024,128]{2,1,0:T(8,128)(2,1)}, bf16[16,1024,128]{2,1,0:T(8,128)(2,1)}, u32[]{:S(2)}, u32[]{:S(2)}) collective-permute-start(bf16[16,1024,128]{2,1,0:T(8,128)(2,1)} %highway_weight.18), channel_id=1, source_target_pairs={{0,16},{16,0},{1,17},{17,1},{2,18},{18,2},{3,19},{19,3},{4,20},{20... | collective-permute-start | bytes 12582920 | tf_op jit(solution)/shard_map/ppermute | solution.py:633
  585.1 44.9 %collective-permute-start.92 = (bf16[4,2,512,128]{3,2,1,0:T(8,128)(2,1)}, bf16[4,2,512,128]{3,2,1,0:T(8,128)(2,1)S(1)}, u32[]{:S(2)}, u32[]{:S(2)}) collective-permute-start(bf16[4,2,512,128]{3,2,1,0:T(8,128)(2,1)} %dynamic-slice_bitcast_fusion.6), channel_id=1, source_target_pairs={{0,2},{1,3},{2,0},{3,1},{4,6},{5,7},{6,4},{7,5},{8,10},{9,11},{10,... | collective-permute-start | bytes 3145736 | tf_op jit(solution)/shard_map/ppermute | solution.py:634
  585.8 44.2 %collective-permute-start.93 = (bf16[4,2,512,128]{3,2,1,0:T(8,128)(2,1)}, bf16[4,2,512,128]{3,2,1,0:T(8,128)(2,1)S(1)}, u32[]{:S(2)}, u32[]{:S(2)}) collective-permute-start(bf16[4,2,512,128]{3,2,1,0:T(8,128)(2,1)} %dynamic-slice_bitcast_fusion.5), channel_id=1, source_target_pairs={{0,1},{1,0},{2,3},{3,2},{4,5},{5,4},{6,7},{7,6},{8,9},{9,8},{10,11... | collective-permute-start | bytes 3145736 | tf_op jit(solution)/shard_map/ppermute | solution.py:634
  587.2 42.8 %collective-permute-start.94 = (bf16[2,2,176,768]{3,2,1,0:T(8,128)(2,1)}, bf16[2,2,176,768]{3,2,1,0:T(8,128)(2,1)S(1)}, u32[]{:S(2)}, u32[]{:S(2)}) collective-permute-start(bf16[2,2,176,768]{3,2,1,0:T(8,128)(2,1)} %fusion.11), channel_id=1, source_target_pairs={{0,4},{1,5},{2,6},{3,7},{4,8},{5,9},{6,10},{7,11},{8,12},{9,13},{1... | collective-permute-start | bytes 3244040 | tf_op jit(solution)/shard_map/ppermute | solution.py:634
  693.8 35.2 %collective-permute-start.106 = (bf16[4,2,576,128]{3,2,1,0:T(8,128)(2,1)}, bf16[4,2,576,128]{3,2,1,0:T(8,128)(2,1)}, u32[]{:S(2)}, u32[]{:S(2)}) collective-permute-start(bf16[4,2,576,128]{3,2,1,0:T(8,128)(2,1)} %fusion.5), channel_id=1, source_target_pairs={{0,1},{1,0},{2,3},{3,2},{4,5},{5,4},{6,7},{7,6},{8,9},{9,8},{10,11... | collective-permute-start | bytes 3538952 | tf_op jit(solution)/shard_map/ppermute | solution.py:634
  695.5 33.4 %collective-permute-start.105 = (bf16[4,2,512,128]{3,2,1,0:T(8,128)(2,1)}, bf16[4,2,512,128]{3,2,1,0:T(8,128)(2,1)}, u32[]{:S(2)}, u32[]{:S(2)}) collective-permute-start(bf16[4,2,512,128]{3,2,1,0:T(8,128)(2,1)} %dynamic-slice_bitcast_fusion.2), channel_id=1, source_target_pairs={{0,2},{1,3},{2,0},{3,1},{4,6},{5,7},{6,4},{7,5},{8,10},{9,11},{10,... | collective-permute-start | bytes 3145736 | tf_op jit(solution)/shard_map/ppermute | solution.py:634
  696.4 32.5 %collective-permute-start.107 = (bf16[4,512,128]{2,1,0:T(8,128)(2,1)}, bf16[4,512,128]{2,1,0:T(8,128)(2,1)}, u32[]{:S(2)}, u32[]{:S(2)}) collective-permute-start(bf16[4,512,128]{2,1,0:T(8,128)(2,1)} %fusion.18), channel_id=1, source_target_pairs={{0,1},{1,0},{2,3},{3,2},{4,5},{5,4},{6,7},{7,6},{8,9},{9,8},{10,11... | collective-permute-start | bytes 1572872 | tf_op jit(solution)/shard_map/ppermute | solution.py:634
  696.9 32.1 %collective-permute-start.108 = (bf16[4,512,128]{2,1,0:T(8,128)(2,1)}, bf16[4,512,128]{2,1,0:T(8,128)(2,1)}, u32[]{:S(2)}, u32[]{:S(2)}) collective-permute-start(bf16[4,512,128]{2,1,0:T(8,128)(2,1)} %fusion.17), channel_id=1, source_target_pairs={{0,2},{1,3},{2,0},{3,1},{4,6},{5,7},{6,4},{7,5},{8,10},{9,11},{10,... | collective-permute-start | bytes 1572872 | tf_op jit(solution)/shard_map/ppermute | solution.py:634
  697.9 31.1 %collective-permute-start.109 = (bf16[2048,128]{1,0:T(8,128)(2,1)}, bf16[2048,128]{1,0:T(8,128)(2,1)}, u32[]{:S(2)}, u32[]{:S(2)}) collective-permute-start(bf16[2048,128]{1,0:T(8,128)(2,1)} %pad_maximum_fusion.11), channel_id=1, source_target_pairs={{0,4},{1,5},{2,6},{3,7},{4,8},{5,9},{6,10},{7,11},{8,12},{9,13},{1... | collective-permute-start | bytes 1572872 | tf_op jit(solution)/shard_map/ppermute | solution.py:634
  (292 other events, 3951.1 us)
